TPU v7x, 32 devices: a whole 2x2x4 slice. The times are simulated.
32 devices in a mesh: lat: 8 (over z, x), deg: 4 (over y, core).
Axes of the slice: x: 2, y: 2, z: 4, core: 2. Of those that a mesh axis runs over, the one named last changes fastest.
Arguments:
- eta_tl: float32 [64, 10752], P('lat'), may hold values from -6 to 6
- vel_tl: float32 [2, 64, 10752], P(None, 'lat'), may hold values from -6 to 6
- eta_adj: float32 [64, 10752], P('lat'), may hold values from -6 to 6
- vel_adj: float32 [2, 64, 10752], P(None, 'lat'), may hold values from -6 to 6
- depth: float32 [64, 10752], P('lat'), may hold values from 0.2 to 1
- drag: float32 [64, 10752], P('lat'), may hold values from 0.01 to 0.3
- ocean: int32 [64, 10752], P('lat'), may hold values 0 or 1
- basis: bfloat16 [1024, 64, 1024], P('lat', None, 'deg'), may hold values from -5 to 5
- love: float32 [1024], P('deg'), may hold values from 0.05 to 0.5
Outputs:
- eta_tl_out: float32 [64, 10752], P('lat')
- vel_tl_out: float32 [2, 64, 10752], P(None, 'lat')
- eta_adj_out: float32 [64, 10752], P('lat')
- vel_adj_out: float32 [2, 64, 10752], P(None, 'lat')
All inputs are finite; a program needn't handle non-finite values. No bound on the sum of `ocean` on one device may be relied on, other than what follows from the above.
Results may differ from a plain program's by a relative error of at most 0.02.
Values may be sent and summed in bfloat16 or wider, within the bound.
A program may use at most 320 MiB of HBM per device.

v0:
```python
import jax
import jax.numpy as jnp
from jax import lax
from jax.sharding import PartitionSpec as P

STEPS = 2


kappa_x = 0.3
kappa_y = 0.4


def as_sent(value):
    return jax.tree.map(lambda a: a.astype(jnp.bfloat16) if a.dtype == jnp.float32 else a, value)


def passed_along(value, axis, by):
    length = lax.axis_size(axis)
    pairs = [(i, i + by) for i in range(length) if 0 <= i + by < length]
    return lax.ppermute(value, axis, pairs)


def trig_table(orders, lon_count):
    lon_cells = jnp.arange(lon_count, dtype=jnp.int32)
    phase_index = lon_cells[:, None] * orders[None, :] % lon_count
    angles = phase_index.astype(jnp.float32) * (2.0 * jnp.pi / lon_count)
    return jnp.concatenate([jnp.cos(angles), jnp.sin(angles)], axis=1).astype(jnp.bfloat16)


def order_factor(orders):
    return jnp.where(orders == 0, 1.0, 2.0).astype(jnp.bfloat16)


def analyse(stacked, analysis_weight, table_now, order_count):
    row_count = stacked.shape[1]
    lon_count = stacked.shape[2]
    flat_rows = stacked.astype(jnp.bfloat16).reshape(2 * row_count, lon_count)
    spectra = lax.dot_general(
        table_now, flat_rows, (((0,), (1,)), ((), ())), preferred_element_type=jnp.float32
    )
    spectra = spectra.reshape(2, order_count, 2, row_count) * (1.0 / lon_count)
    return (spectra * analysis_weight[None, None, :, :]).astype(jnp.bfloat16)


def legendre(spectra, basis, love):
    coeffs = jnp.einsum("cmfi,mil->cmfl", spectra, basis, preferred_element_type=jnp.float32)
    scaled = (coeffs * love[None, None, None, :]).astype(jnp.bfloat16)
    return jnp.einsum("cmfl,mil->cmfi", scaled, basis, preferred_element_type=jnp.float32)


def synthesise(coeffs, factors, table_now, output_weight):
    order_count = coeffs.shape[1]
    row_count = coeffs.shape[3]
    scaled = (coeffs * factors[None, :, None, None]).reshape(2 * order_count, 2 * row_count)
    grid_out = lax.dot_general(
        scaled, table_now, (((0,), (1,)), ((), ())), preferred_element_type=jnp.float32
    )
    return grid_out.reshape(2, row_count, -1) * output_weight[:, :, None]


def from_north(edge_row):
    return passed_along(as_sent(edge_row), "lat", -1).astype(edge_row.dtype)


def from_south(edge_row):
    return passed_along(as_sent(edge_row), "lat", 1).astype(edge_row.dtype)


def on_device(eta_tl, vel_tl, eta_adj, vel_adj, depth, drag, ocean, basis, love):
    row_count = eta_tl.shape[0]
    lon_count = eta_tl.shape[1]
    lat_count = lax.axis_size("lat")
    total_rows = row_count * lat_count
    first_row = lax.axis_index("lat") * row_count
    indices = first_row + jnp.arange(row_count, dtype=jnp.int32)
    latitude = (indices.astype(jnp.float32) + 0.5) * (jnp.pi / total_rows) - 0.5 * jnp.pi
    cosine = jnp.cos(latitude)
    quad_weight = jnp.pi / total_rows * cosine
    east_factor = (kappa_x / (0.5 + 0.5 * cosine))[:, None]
    wet_mask = ocean.astype(jnp.float32)
    north_depth, north_wet = (
        passed_along(depth[:1].astype(jnp.bfloat16), "lat", -1).astype(jnp.float32),
        passed_along(wet_mask[:1].astype(jnp.bfloat16), "lat", -1).astype(jnp.float32),
    )
    depth_up = jnp.concatenate([depth[1:], north_depth], 0)
    wet_up = jnp.concatenate([wet_mask[1:], north_wet], 0)
    mask_u = wet_mask * jnp.roll(wet_mask, -1, 1)
    mask_v = wet_mask * wet_up
    depth_u = 0.5 * (depth + jnp.roll(depth, -1, 1))
    depth_v = 0.5 * (depth + depth_up)
    retain = 1.0 - drag
    ones_weight = jnp.ones_like(quad_weight)
    analysis_weight = jnp.stack([quad_weight, ones_weight])
    output_weight = jnp.stack([ones_weight, quad_weight])
    owned_count = basis.shape[0]
    order_total = owned_count * lat_count
    full_orders = jnp.arange(order_total, dtype=jnp.int32)
    full_table = trig_table(full_orders, lon_count)
    full_factor = order_factor(full_orders)
    state_eta, state_vel = (eta_tl, vel_tl)
    back_eta, back_vel = (eta_adj, vel_adj)
    for step_index in range(STEPS):
        flux_east = east_factor * wet_mask * back_eta
        flux_north = kappa_y * wet_mask * back_eta
        north_up = jnp.concatenate([flux_north[1:], from_north(flux_north[:1])], 0)
        p_term = mask_u * (back_vel[0] + depth_u * (jnp.roll(flux_east, -1, 1) - flux_east))
        q_term = mask_v * (back_vel[1] + depth_v * (north_up - flux_north))
        q_down = jnp.concatenate([from_south(q_term[-1:]), q_term[:-1]], 0)
        flux_p = east_factor * p_term
        psi_bar = flux_p - jnp.roll(flux_p, 1, 1) + kappa_y * (q_term - q_down)
        spectra = analyse(jnp.stack([state_eta, psi_bar]), analysis_weight, full_table, order_total)
        owned_rows = lax.all_to_all(spectra, "lat", split_axis=1, concat_axis=3, tiled=True)
        partial_value = legendre(owned_rows, basis, love)
        total_sum = lax.psum(partial_value.astype(jnp.bfloat16), "deg")
        banded = lax.all_to_all(total_sum, "lat", split_axis=3, concat_axis=1, tiled=True)
        loads = synthesise(banded, full_factor, full_table, output_weight)
        psi_now = state_eta - loads[0]
        psi_up = jnp.concatenate([psi_now[1:], from_north(psi_now[:1])], 0)
        new_u = mask_u * (
            retain * state_vel[0] - east_factor * (jnp.roll(psi_now, -1, 1) - psi_now)
        )
        new_v = mask_v * (retain * state_vel[1] - kappa_y * (psi_up - psi_now))
        flux_x = depth_u * new_u
        flux_y = depth_v * new_v
        flux_down = jnp.concatenate([from_south(flux_y[-1:]), flux_y[:-1]], 0)
        state_eta = state_eta - wet_mask * (
            east_factor * (flux_x - jnp.roll(flux_x, 1, 1)) + kappa_y * (flux_y - flux_down)
        )
        state_vel = jnp.stack([new_u, new_v])
        back_eta = back_eta + psi_bar - loads[1]
        back_vel = jnp.stack([retain * p_term, retain * q_term])
    return (state_eta, state_vel, back_eta, back_vel)


def solution(mesh):
    in_specs = (
        P("lat", None),
        P(None, "lat", None),
        P("lat", None),
        P(None, "lat", None),
        P("lat", None),
        P("lat", None),
        P("lat", None),
        P("lat", None, "deg"),
        P("deg"),
    )
    out_specs = (P("lat", None), P(None, "lat", None), P("lat", None), P(None, "lat", None))
    return jax.shard_map(
        on_device, mesh=mesh, in_specs=in_specs, out_specs=out_specs, check_vma=False
    )
```

profile of v0, /device:TPU:0, one launch (start us, length us, event | category | flops | bytes accessed | tf_op | source)
XLA Modules:
  0.0 552.0 jit_solution(11705418563088993422)
XLA Ops:
  14.5 187.3 %sine_convert_fusion = (bf16[10752,1024]{1,0:T(8,128)(2,1)}, bf16[10752,1024]{1,0:T(8,128)(2,1)}) fusion(), kind=kLoop, calls=%fused_computation.8 | loop fusion | flops 121110528 | bytes 44040192 | tf_op jit(solution)/shard_map/convert.19
  202.5 29.5 %fusion.9 = bf16[2048,10752]{0,1:T(8,128)(2,1)} fusion(bf16[10752,1024]{1,0:T(8,128)(2,1)} %get-tuple-element.48, bf16[10752,1024]{1,0:T(8,128)(2,1)} %get-tuple-element.49), kind=kLoop, calls=%fused_computation.14 | loop fusion | flops 88080384 | bytes 88080384 | tf_op jit(solution)/shard_map/dot_general | solution.py:38
  232.9 2.4 broadcast_multiply_fusion.1
  235.3 6.7 %collective-permute-start.3 = (bf16[1,10752]{1,0:T(2,128)(2,1)S(1)}, bf16[1,10752]{1,0:T(2,128)(2,1)S(1)}, u32[]{:S(2)}, u32[]{:S(2)}) collective-permute-start(bf16[1,10752]{1,0:T(2,128)(2,1)S(1)} %slice.279), channel_id=1, source_target_pairs={{0,4},{4,8},{8,12},{12,16},{16,20},{20,24},{24,28},{1,5},{5,9},{9,... | collective-permute-start | bytes 64520 | tf_op jit(solution)/shard_map/ppermute | solution.py:20
  242.1 56.8 %copy.41 = bf16[2048,10752]{1,0:T(8,128)(2,1)} copy(bf16[2048,10752]{0,1:T(8,128)(2,1)} %fusion.9) | data formatting | bytes 88080384 | tf_op jit(solution)/shard_map/dot_general | solution.py:38
  299.9 19.5 %fusion.66 = bf16[2,1024,2,8]{1,3,2,0:T(8,128)(2,1)S(1)} fusion(bf16[2,1024,10752,1]{2,1,3,0:T(8,128)(2,1)} %bitcast.190, bf16[1,8,10752]{2,1,0:T(8,128)(2,1)S(1)} %get-tuple-element.22, bf16[1,8,10752]{2,1,0:T(8,128)(2,1)S(1)} %copy-done.10, f32[2,8]{1,0:T(2,128)S(1)} %get-tuple-element.46), kind=kOutput, calls=%fused_computation.37 | convolution fusion | flops 705396736 | bytes 44449856 | tf_op jit(solution)/shard_map/dot_general | solution.py:38
  321.2 14.8 %all_to_all.72 = bf16[8,2,2048]{2,1,0:T(2,128)(2,1)S(1)} all-to-all(bf16[8,2,2048]{2,1,0:T(2,128)(2,1)S(1)} %reshape.79), channel_id=1, replica_groups=mesh['lat'=8,'deg'=4] {'lat'}, dimensions={0} | all-to-all | bytes 131072 | tf_op jit(solution)/shard_map/all_to_all | solution.py:112
  337.2 1.3 copy.59
  338.6 6.0 %fusion.61 = bf16[2,128,2,64]{3,2,0,1:T(2,128)(2,1)} fusion(bf16[128,64,256]{2,1,0:T(8,128)(2,1)} %param.16, bf16[2,128,2,64]{3,2,0,1:T(2,128)(2,1)S(1)} %copy.45, f32[256]{0:T(256)S(1)} %copy-done.11), kind=kOutput, calls=%fused_computation.34 | convolution fusion | flops 33849344 | bytes 4326400 | tf_op jit(solution)/shard_map/cmfl,mil->cmfi/dot_general | solution.py:48
  344.7 29.1 %all-reduce.5.cloned.1.call-done = bf16[2,128,2,64]{3,2,0,1:T(2,128)(2,1)} async-done(((bf16[2,128,2,64]{3,2,0,1:T(2,128)(2,1)}), bf16[2,128,2,64]{3,2,0,1:T(2,128)(2,1)}) %all-reduce.5.cloned.1.call-update) | async-done | bytes 65552 | tf_op jit(solution)/shard_map/psum | solution.py:114
  373.8 1.7 copy.46
  375.5 5.5 all-to-all-start.1
  381.1 6.8 %all-to-all-done.1 = bf16[2,128,2,64]{1,2,0,3:T(2,128)(2,1)S(1)} async-done(((bf16[2,128,2,64]{1,2,0,3:T(2,128)(2,1)}), bf16[2,128,2,64]{1,2,0,3:T(2,128)(2,1)S(1)}, u32[]{:S(2)}, u32[]{:S(2)}) %all-to-all-start.1) | async-done | bytes 65568 | tf_op jit(solution)/shard_map/all_to_all | solution.py:115
  388.0 18.4 %fusion.10 = f32[2,8,10752]{2,1,0:T(8,128)} fusion(bf16[10752,1024]{1,0:T(8,128)(2,1)} %get-tuple-element.48, bf16[10752,1024]{1,0:T(8,128)(2,1)} %get-tuple-element.49, f32[2,8]{1,0:T(2,128)S(1)} %get-tuple-element.47, bf16[2048,16]{0,1:T(8,128)(2,1)S(1)} %all_to_all.59, bf16[2048]{0:T(1024)(128)(2,1)S(1)} %bitcast.210), kind=kOutput, calls=%fused_computation.15 | convolution fusion | flops 792928256 | bytes 44798016 | tf_op jit(solution)/shard_map/dot_general | solution.py:55
  406.4 1.4 multiply_multiply_fusion
  410.7 3.0 collective-permute-done.4
  413.8 1.9 collective-permute-done.6
  415.8 2.4 fusion.139
  418.2 4.8 collective-permute-start.5
  423.2 2.3 collective-permute-start.7
  425.9 1.8 multiply_bitcast_fusion.1
  428.2 19.5 %fusion.67 = bf16[2,1024,2,8]{1,3,2,0:T(8,128)(2,1)S(1)} fusion(bf16[2,1024,10752,1]{2,1,3,0:T(8,128)(2,1)} %bitcast.191, bf16[1,8,10752]{2,1,0:T(8,128)(2,1)S(1)} %get-tuple-element.14, bf16[1,8,10752]{2,1,0:T(8,128)(2,1)S(1)} %get-tuple-element.12, f32[2,8]{1,0:T(2,128)S(1)} %get-tuple-element.46), kind=kOutput, calls=%fused_computation.38 | convolution fusion | flops 705396736 | bytes 44449856 | tf_op jit(solution)/shard_map/dot_general | solution.py:38
  449.5 10.5 %all_to_all.73 = bf16[8,2,2048]{2,1,0:T(2,128)(2,1)S(1)} all-to-all(bf16[8,2,2048]{2,1,0:T(2,128)(2,1)S(1)} %reshape.81), channel_id=1, replica_groups=mesh['lat'=8,'deg'=4] {'lat'}, dimensions={0} | all-to-all | bytes 131072 | tf_op jit(solution)/shard_map/all_to_all | solution.py:112
  463.3 6.1 %fusion.56 = bf16[2,128,2,64]{3,2,0,1:T(2,128)(2,1)} fusion(bf16[128,64,256]{2,1,0:T(8,128)(2,1)} %param.16, bf16[2,128,2,64]{3,2,0,1:T(2,128)(2,1)} %copy.52, f32[256]{0:T(256)S(1)} %copy-done.11), kind=kOutput, calls=%fused_computation.33 | convolution fusion | flops 33849344 | bytes 4326400 | tf_op jit(solution)/shard_map/cmfl,mil->cmfi/dot_general | solution.py:48
  469.4 28.1 %all-reduce.7.cloned.1.call-done = bf16[2,128,2,64]{3,2,0,1:T(2,128)(2,1)} async-done(((bf16[2,128,2,64]{3,2,0,1:T(2,128)(2,1)}), bf16[2,128,2,64]{3,2,0,1:T(2,128)(2,1)}) %all-reduce.7.cloned.1.call-update) | async-done | bytes 65552 | tf_op jit(solution)/shard_map/psum | solution.py:114
  498.6 12.2 %all_to_all.74 = bf16[2,128,2,64]{1,2,0,3:T(2,128)(2,1)S(1)} all-to-all(bf16[2,128,2,64]{1,2,0,3:T(2,128)(2,1)S(1)} %copy.53), channel_id=1, replica_groups=mesh['lat'=8,'deg'=4] {'lat'}, dimensions={3} | all-to-all | bytes 131072 | tf_op jit(solution)/shard_map/all_to_all | solution.py:115
  511.5 18.4 %fusion.13 = f32[2,8,10752]{2,1,0:T(8,128)} fusion(bf16[10752,1024]{1,0:T(8,128)(2,1)} %get-tuple-element.48, bf16[10752,1024]{1,0:T(8,128)(2,1)} %get-tuple-element.49, f32[2,8]{1,0:T(2,128)S(1)} %get-tuple-element.47, bf16[2048,16]{0,1:T(8,128)(2,1)} %all_to_all.67, bf16[2048]{0:T(1024)(128)(2,1)S(1)} %bitcast.211), kind=kOutput, calls=%fused_computation.16 | convolution fusion | flops 792928256 | bytes 44798016 | tf_op jit(solution)/shard_map/dot_general | solution.py:55
  529.9 1.9 fusion.68
  533.2 1.9 pad_maximum_fusion.4
  535.2 2.5 collective-permute-done.8
  537.8 1.4 fusion.130
  539.3 3.2 collective-permute-start.9
  (115 shorter events, 28.0 us)
Async XLA Ops:
  7.2 194.6 %copy-start.2 = (f32[8,10752]{1,0:T(8,128)S(1)}, f32[8,10752]{1,0:T(8,128)}, u32[]{:S(2)}) copy-start(f32[8,10752]{1,0:T(8,128)} %param.9) | copy-start | bytes 1032196
  7.2 366.7 %all-reduce.5.cloned.1.call-start = ((), (), s32[]{:S(2)}) async-start(), calls=%async_computation.4 | async-start | bytes 262144 | tf_op jit(solution)/shard_map/psum | solution.py:114
  8.5 224.2 %collective-permute-start.2 = (bf16[1,10752]{1,0:T(2,128)(2,1)S(1)}, bf16[1,10752]{1,0:T(2,128)(2,1)S(1)}, u32[]{:S(2)}, u32[]{:S(2)}) collective-permute-start(bf16[1,10752]{1,0:T(2,128)(2,1)S(1)} %slice.280), channel_id=1, source_target_pairs={{4,0},{8,4},{12,8},{16,12},{20,16},{24,20},{28,24},{5,1},{9,5},{13... | collective-permute-start | bytes 64520 | tf_op jit(solution)/shard_map/ppermute | solution.py:20
  10.8 221.9 %collective-permute-start.1 = (bf16[1,10752]{1,0:T(2,128)(2,1)S(1)}, bf16[1,10752]{1,0:T(2,128)(2,1)S(1)}, u32[]{:S(2)}, u32[]{:S(2)}) collective-permute-start(bf16[1,10752]{1,0:T(2,128)(2,1)S(1)} %slice.281), channel_id=1, source_target_pairs={{4,0},{8,4},{12,8},{16,12},{20,16},{24,20},{28,24},{5,1},{9,5},{13... | collective-permute-start | bytes 64520 | tf_op jit(solution)/shard_map/ppermute | solution.py:20
  13.2 219.7 %collective-permute-start = (bf16[1,10752]{1,0:T(2,128)(2,1)S(1)}, bf16[1,10752]{1,0:T(2,128)(2,1)S(1)}, u32[]{:S(2)}, u32[]{:S(2)}) collective-permute-start(bf16[1,10752]{1,0:T(2,128)(2,1)S(1)} %slice.282), channel_id=1, source_target_pairs={{4,0},{8,4},{12,8},{16,12},{20,16},{24,20},{28,24},{5,1},{9,5},{13... | collective-permute-start | bytes 64520 | tf_op jit(solution)/shard_map/ppermute | solution.py:20
  202.5 29.9 %copy-start.1 = (f32[8,10752]{1,0:T(8,128)S(1)}, f32[8,10752]{1,0:T(8,128)}, u32[]{:S(2)}) copy-start(f32[8,10752]{1,0:T(8,128)} %param.13) | copy-start | bytes 1032196
  202.5 30.4 %copy-start = (s32[8,10752]{1,0:T(8,128)S(1)}, s32[8,10752]{1,0:T(8,128)}, u32[]{:S(2)}) copy-start(s32[8,10752]{1,0:T(8,128)} %param.15) | copy-start | bytes 1032196
  202.5 30.4 %slice-start = ((f32[8,10752]{1,0:T(8,128)}), f32[8,1]{1,0:T(8,128)S(1)}, s32[]{:S(2)}) async-start(f32[8,10752]{1,0:T(8,128)} %param.13), calls=%async_computation.6 | async-start | bytes 8192 | tf_op jit(solution)/shard_map/jit(_roll_static)/slice | solution.py:89
  235.2 180.5 %copy-start.5 = (f32[8,10752]{1,0:T(8,128)}, f32[8,10752]{1,0:T(8,128)S(1)}, u32[]{:S(2)}) copy-start(f32[8,10752]{1,0:T(8,128)S(1)} %get-tuple-element.34) | copy-start | bytes 1032196
  235.3 63.6 %collective-permute-start.3 = (bf16[1,10752]{1,0:T(2,128)(2,1)S(1)}, bf16[1,10752]{1,0:T(2,128)(2,1)S(1)}, u32[]{:S(2)}, u32[]{:S(2)}) collective-permute-start(bf16[1,10752]{1,0:T(2,128)(2,1)S(1)} %slice.279), channel_id=1, source_target_pairs={{0,4},{4,8},{8,12},{12,16},{16,20},{20,24},{24,28},{1,5},{5,9},{9,... | collective-permute-start | bytes 64520 | tf_op jit(solution)/shard_map/ppermute | solution.py:20
  242.0 57.8 %copy-start.10 = (bf16[1,8,10752]{2,1,0:T(8,128)(2,1)S(1)}, bf16[1,8,10752]{2,1,0:T(8,128)(2,1)}, u32[]{:S(2)}) copy-start(bf16[1,8,10752]{2,1,0:T(8,128)(2,1)} %convert_bitcast_fusion.3) | copy-start | bytes 516100
  298.8 39.8 %copy-start.11 = (f32[256]{0:T(256)S(1)}, f32[256]{0:T(256)}, u32[]{:S(2)}) copy-start(f32[256]{0:T(256)} %param.17) | copy-start | bytes 3076
  338.6 77.2 %copy-start.3 = (f32[8,10752]{1,0:T(8,128)S(1)}, f32[8,10752]{1,0:T(8,128)}, u32[]{:S(2)}) copy-start(f32[8,10752]{1,0:T(8,128)} %param.14) | copy-start | bytes 1032196
  338.6 77.2 %copy-start.7 = (f32[8,10752]{1,0:T(8,128)S(1)}, f32[8,10752]{1,0:T(8,128)}, u32[]{:S(2)}) copy-start(f32[8,10752]{1,0:T(8,128)} %get-tuple-element.35) | copy-start | bytes 1032196
  375.5 12.4 %all-to-all-start.1 = ((bf16[2,128,2,64]{1,2,0,3:T(2,128)(2,1)}), bf16[2,128,2,64]{1,2,0,3:T(2,128)(2,1)S(1)}, u32[]{:S(2)}, u32[]{:S(2)}) async-start(bf16[2,128,2,64]{1,2,0,3:T(2,128)(2,1)} %copy.46), calls=%async_computation.1 | async-start | bytes 131072 | tf_op jit(solution)/shard_map/all_to_all | solution.py:115
  381.0 116.6 %all-reduce.7.cloned.1.call-start = ((), (), s32[]{:S(2)}) async-start(), calls=%async_computation.5 | async-start | bytes 262144 | tf_op jit(solution)/shard_map/psum | solution.py:114
  407.8 5.9 %collective-permute-start.4 = (bf16[1,10752]{1,0:T(2,128)(2,1)S(1)}, bf16[1,10752]{1,0:T(2,128)(2,1)S(1)}, u32[]{:S(2)}, u32[]{:S(2)}) collective-permute-start(bf16[1,10752]{1,0:T(2,128)(2,1)S(1)} %slice.278), channel_id=1, source_target_pairs={{4,0},{8,4},{12,8},{16,12},{20,16},{24,20},{28,24},{5,1},{9,5},{13... | collective-permute-start | bytes 64520 | tf_op jit(solution)/shard_map/ppermute | solution.py:20
  409.2 6.5 %collective-permute-start.6 = (bf16[1,10752]{1,0:T(2,128)(2,1)S(1)}, bf16[1,10752]{1,0:T(2,128)(2,1)S(1)}, u32[]{:S(2)}, u32[]{:S(2)}) collective-permute-start(bf16[1,10752]{1,0:T(2,128)(2,1)S(1)} %slice.276), channel_id=1, source_target_pairs={{4,0},{8,4},{12,8},{16,12},{20,16},{24,20},{28,24},{5,1},{9,5},{13... | collective-permute-start | bytes 64520 | tf_op jit(solution)/shard_map/ppermute | solution.py:20
  418.2 7.3 %collective-permute-start.5 = (bf16[1,10752]{1,0:T(2,128)(2,1)S(1)}, bf16[1,10752]{1,0:T(2,128)(2,1)S(1)}, u32[]{:S(2)}, u32[]{:S(2)}) collective-permute-start(bf16[1,10752]{1,0:T(2,128)(2,1)S(1)} %slice.277), channel_id=1, source_target_pairs={{0,4},{4,8},{8,12},{12,16},{16,20},{20,24},{24,28},{1,5},{5,9},{9,... | collective-permute-start | bytes 64520 | tf_op jit(solution)/shard_map/ppermute | solution.py:20
  423.2 4.8 collective-permute-start.7
  460.0 73.2 %copy-start.9 = (f32[1,8,10752]{2,1,0:T(8,128)S(1)}, f32[1,8,10752]{2,1,0:T(8,128)}, u32[]{:S(2)}) copy-start(f32[1,8,10752]{2,1,0:T(8,128)} %get-tuple-element.4) | copy-start | bytes 1032196
  463.3 74.5 %copy-start.4 = (f32[8,10752]{1,0:T(8,128)S(1)}, f32[8,10752]{1,0:T(8,128)}, u32[]{:S(2)}) copy-start(f32[8,10752]{1,0:T(8,128)} %param.14) | copy-start | bytes 1032196
  463.3 74.5 %copy-start.6 = (f32[8,10752]{1,0:T(8,128)S(1)}, f32[8,10752]{1,0:T(8,128)}, u32[]{:S(2)}) copy-start(f32[8,10752]{1,0:T(8,128)} %copy-done.5) | copy-start | bytes 1032196
  463.3 74.5 %copy-start.8 = (f32[8,10752]{1,0:T(8,128)S(1)}, f32[8,10752]{1,0:T(8,128)}, u32[]{:S(2)}) copy-start(f32[8,10752]{1,0:T(8,128)} %get-tuple-element.35) | copy-start | bytes 1032196
  531.9 5.9 %collective-permute-start.8 = (bf16[1,10752]{1,0:T(2,128)(2,1)S(1)}, bf16[1,10752]{1,0:T(2,128)(2,1)S(1)}, u32[]{:S(2)}, u32[]{:S(2)}) collective-permute-start(bf16[1,10752]{1,0:T(2,128)(2,1)S(1)} %slice.274), channel_id=1, source_target_pairs={{4,0},{8,4},{12,8},{16,12},{20,16},{24,20},{28,24},{5,1},{9,5},{13... | collective-permute-start | bytes 64520 | tf_op jit(solution)/shard_map/ppermute | solution.py:20
  539.3 4.9 collective-permute-start.9
Sparse Core Ops, SparseCore 0:
  344.8 28.9 all-reduce.4
  469.6 27.9 all-reduce.6
where the time goes:
time: 554 us; the launch traced here: 552 us
  other arithmetic  237 us (43%)
  matrix products  88 us (16%)
  local copies, waits for them, and re-layouts  72.5 us (13%)
  waiting for transfers between devices  72.3 us (13%)
  blocking collectives  37.5 us (7%)
  starting transfers between devices  30.4 us (5%)
  between operations  14.7 us (3%)
    another operation x1, other arithmetic  187 us
    psum x2, waiting for transfers between devices, on_device(): total_sum = lax.psum(partial_value.astype(jnp.bfloat16), 'deg')  57.2 us
    dot_general x1, local copies, waits for them, and re-layouts, analyse(): lax.dot_general(table_now, flat_rows, (((0,), (1,)), ((), ())), preferred...  56.8 us
    dot_general x2, matrix products, analyse(): lax.dot_general(table_now, flat_rows, (((0,), (1,)), ((), ())), preferred...  39 us
    dot_general x2, matrix products, synthesise(): lax.dot_general(scaled, table_now, (((0,), (1,)), ((), ())), preferred_el...  36.8 us
    dot_general x1, other arithmetic, analyse(): lax.dot_general(table_now, flat_rows, (((0,), (1,)), ((), ())), preferred...  29.5 us
    all_to_all x2, blocking collectives, on_device(): lax.all_to_all(spectra, 'lat', split_axis=1, concat_axis=3, tiled=True)  25.3 us
    ppermute x10, starting transfers between devices, passed_along(): return lax.ppermute(value, axis, pairs)  24.8 us
  transfers between devices with their start and end apart: 13, of which 7 were waited for; matrix products, arithmetic and copies ran while one was open for 51% of the time, Pallas kernels for 0%

commit v1 on v0

v1 whole, which is shorter than its diff:
```python
import jax
import jax.numpy as jnp
import numpy as np
from jax import lax
from jax.sharding import PartitionSpec as P

STEPS = 2
LANES = 128


kappa_x = 0.3
kappa_y = 0.4


def passed_along(value, axis, by):
    length = lax.axis_size(axis)
    pairs = [(i, i + by) for i in range(length) if 0 <= i + by < length]
    return lax.ppermute(value, axis, pairs)


def circle(numerator, period):
    angles = 2.0 * np.pi * (numerator % period) / period
    return np.cos(angles), np.sin(angles)


def fourier_tables(lon_count, order_total):
    major = lon_count // LANES
    blocks = -(-order_total // major)
    residues, lanes = np.arange(major), np.arange(LANES)
    outer = np.stack(circle(residues[:, None] * residues[None, :], major))
    turn = np.stack(circle(residues[:, None] * lanes[None, :], lon_count))
    inner = np.stack(circle(np.arange(blocks)[:, None] * lanes[None, :], LANES))
    return (
        jnp.asarray(outer, jnp.bfloat16),
        jnp.asarray(turn, jnp.float32),
        jnp.asarray(inner, jnp.bfloat16),
    )


def order_factor(orders):
    return jnp.where(orders == 0, 1.0, 2.0).astype(jnp.bfloat16)


def analyse(stacked, analysis_weight, tables, order_count):
    outer, turn, inner = tables
    row_count = stacked.shape[1]
    lon_count = stacked.shape[2]
    split_rows = stacked.astype(jnp.bfloat16).reshape(2 * row_count, lon_count // LANES, LANES)
    first = jnp.einsum("cka,rab->crkb", outer, split_rows, preferred_element_type=jnp.float32)
    turned = jnp.stack(
        [first[0] * turn[0] - first[1] * turn[1], first[1] * turn[0] + first[0] * turn[1]]
    ).astype(jnp.bfloat16)
    second = jnp.stack([jnp.stack([inner[0], -inner[1]]), jnp.stack([inner[1], inner[0]])])
    spectra = jnp.einsum("crkb,dcnb->dnkr", turned, second, preferred_element_type=jnp.float32)
    spectra = spectra.reshape(2, -1, 2, row_count)[:, :order_count] * (1.0 / lon_count)
    return (spectra * analysis_weight[None, None, :, :]).astype(jnp.bfloat16)


def legendre(spectra, basis, love):
    coeffs = jnp.einsum("cmfi,mil->cmfl", spectra, basis, preferred_element_type=jnp.float32)
    scaled = (coeffs * love[None, None, None, :]).astype(jnp.bfloat16)
    return jnp.einsum("cmfl,mil->cmfi", scaled, basis, preferred_element_type=jnp.float32)


def synthesise(coeffs, factors, tables, output_weight):
    outer, turn, inner = tables
    major, blocks = turn.shape[1], inner.shape[1]
    order_count = coeffs.shape[1]
    row_count = coeffs.shape[3]
    scaled = coeffs * factors[None, :, None, None]
    padded = jnp.pad(scaled, ((0, 0), (0, major * blocks - order_count), (0, 0), (0, 0)))
    padded = padded.reshape(2, blocks, major, 2 * row_count)
    second = jnp.stack([jnp.stack([inner[0], inner[1]]), jnp.stack([-inner[1], inner[0]])])
    first = jnp.einsum("cnkr,dcnb->drkb", padded, second, preferred_element_type=jnp.float32)
    turned = jnp.stack(
        [first[0] * turn[0] + first[1] * turn[1], first[1] * turn[0] - first[0] * turn[1]]
    ).astype(jnp.bfloat16)
    grid_out = jnp.einsum("cka,crkb->rab", outer, turned, preferred_element_type=jnp.float32)
    return grid_out.reshape(2, row_count, -1) * output_weight[:, :, None]


def edges_from(rows, by):
    sent = jnp.concatenate(rows, 0).astype(jnp.bfloat16)
    got = passed_along(sent, "lat", by).astype(jnp.float32)
    return [got[i : i + 1] for i in range(len(rows))]


def northward(values, edge):
    return jnp.concatenate([values[1:], edge], 0)


def southward(values, edge):
    return jnp.concatenate([edge, values[:-1]], 0)


def on_device(eta_tl, vel_tl, eta_adj, vel_adj, depth, drag, ocean, basis, love):
    row_count = eta_tl.shape[0]
    lon_count = eta_tl.shape[1]
    lat_count = lax.axis_size("lat")
    total_rows = row_count * lat_count
    first_row = lax.axis_index("lat") * row_count
    indices = first_row + jnp.arange(row_count, dtype=jnp.int32)
    latitude = (indices.astype(jnp.float32) + 0.5) * (jnp.pi / total_rows) - 0.5 * jnp.pi
    cosine = jnp.cos(latitude)
    quad_weight = jnp.pi / total_rows * cosine
    east_factor = (kappa_x / (0.5 + 0.5 * cosine))[:, None]
    wet_mask = ocean.astype(jnp.float32)
    flux_north = kappa_y * wet_mask * eta_adj
    north_depth, north_wet, north_flux = edges_from(
        [depth[:1], wet_mask[:1], flux_north[:1]], -1
    )
    depth_up = northward(depth, north_depth)
    wet_up = northward(wet_mask, north_wet)
    mask_u = wet_mask * jnp.roll(wet_mask, -1, 1)
    mask_v = wet_mask * wet_up
    depth_u = 0.5 * (depth + jnp.roll(depth, -1, 1))
    depth_v = 0.5 * (depth + depth_up)
    retain = 1.0 - drag
    ones_weight = jnp.ones_like(quad_weight)
    analysis_weight = jnp.stack([quad_weight, ones_weight])
    output_weight = jnp.stack([ones_weight, quad_weight])
    owned_count = basis.shape[0]
    order_total = owned_count * lat_count
    full_orders = jnp.arange(order_total, dtype=jnp.int32)
    tables = fourier_tables(lon_count, order_total)
    full_factor = order_factor(full_orders)
    state_eta, state_vel = (eta_tl, vel_tl)
    back_eta, back_vel = (eta_adj, vel_adj)

    def adjoint_terms(eta, vel, flux_edge):
        flux_east = east_factor * wet_mask * eta
        flux_up = kappa_y * wet_mask * eta
        north_up = northward(flux_up, flux_edge)
        p_term = mask_u * (vel[0] + depth_u * (jnp.roll(flux_east, -1, 1) - flux_east))
        q_term = mask_v * (vel[1] + depth_v * (north_up - flux_up))
        return p_term, q_term

    p_term, q_term = adjoint_terms(back_eta, back_vel, north_flux)
    (q_edge,) = edges_from([q_term[-1:]], 1)
    for step_index in range(STEPS):
        flux_p = east_factor * p_term
        q_down = southward(q_term, q_edge)
        psi_bar = flux_p - jnp.roll(flux_p, 1, 1) + kappa_y * (q_term - q_down)
        spectra = analyse(jnp.stack([state_eta, psi_bar]), analysis_weight, tables, order_total)
        owned_rows = lax.all_to_all(spectra, "lat", split_axis=1, concat_axis=3, tiled=True)
        partial_value = legendre(owned_rows, basis, love)
        total_sum = lax.psum(partial_value.astype(jnp.bfloat16), "deg")
        banded = lax.all_to_all(total_sum, "lat", split_axis=3, concat_axis=1, tiled=True)
        loads = synthesise(banded, full_factor, tables, output_weight)
        last = step_index == STEPS - 1
        psi_now = state_eta - loads[0]
        back_eta = back_eta + psi_bar - loads[1]
        back_vel = (retain * p_term, retain * q_term)
        north_rows = [psi_now[:1]]
        if not last:
            north_rows.append(kappa_y * wet_mask[:1] * back_eta[:1])
        north_edges = edges_from(north_rows, -1)
        psi_up = northward(psi_now, north_edges[0])
        new_u = mask_u * (
            retain * state_vel[0] - east_factor * (jnp.roll(psi_now, -1, 1) - psi_now)
        )
        new_v = mask_v * (retain * state_vel[1] - kappa_y * (psi_up - psi_now))
        flux_x = depth_u * new_u
        flux_y = depth_v * new_v
        south_rows = [flux_y[-1:]]
        if not last:
            p_term, q_term = adjoint_terms(back_eta, back_vel, north_edges[1])
            south_rows.append(q_term[-1:])
        south_edges = edges_from(south_rows, 1)
        flux_down = southward(flux_y, south_edges[0])
        if not last:
            q_edge = south_edges[1]
        state_eta = state_eta - wet_mask * (
            east_factor * (flux_x - jnp.roll(flux_x, 1, 1)) + kappa_y * (flux_y - flux_down)
        )
        state_vel = (new_u, new_v)
    state_vel, back_vel = jnp.stack(state_vel), jnp.stack(back_vel)
    return (state_eta, state_vel, back_eta, back_vel)


def solution(mesh):
    in_specs = (
        P("lat", None),
        P(None, "lat", None),
        P("lat", None),
        P(None, "lat", None),
        P("lat", None),
        P("lat", None),
        P("lat", None),
        P("lat", None, "deg"),
        P("deg"),
    )
    out_specs = (P("lat", None), P(None, "lat", None), P("lat", None), P(None, "lat", None))
    return jax.shard_map(
        on_device, mesh=mesh, in_specs=in_specs, out_specs=out_specs, check_vma=False
    )
```

time: 554 us -> 201 us (0.36)
  other arithmetic: 237 us -> 14.2 us
  matrix products: 88 us -> 14.8 us
  local copies, waits for them, and re-layouts: 72.5 us -> 20.4 us
  starting transfers between devices: 30.4 us -> 20.9 us
  waiting for transfers between devices: 72.3 us -> 79.5 us
    another operation x4 -> x9, other arithmetic: 192 us -> 3.5 us  [the longest x3 2.66 us: on_device(): state_vel, back_vel = (jnp.stack(state_vel), jnp.stack(back_vel))]
    dot_general x4 -> x8, matrix products: 75.8 us -> 2.78 us  [the longest x2 0.81 us: synthesise(): jnp.einsum('cnkr,dcnb->drkb', padded, second, preferred_element_type=jnp....]
    dot_general x1 -> x0, local copies, waits for them, and re-layouts: 56.8 us -> none  [analyse(): lax.dot_general(table_now, flat_rows, (((0,), (1,)), ((), ())), preferred...]
    dot_general x1 -> x0, other arithmetic: 29.5 us -> none  [analyse(): lax.dot_general(table_now, flat_rows, (((0,), (1,)), ((), ())), preferred...]
    ppermute x10 -> x6, starting transfers between devices: 24.8 us -> 15.3 us  [passed_along(): return lax.ppermute(value, axis, pairs)]
    ppermute x10 -> x6, waiting for transfers between devices: 8.21 us -> 15.4 us  [passed_along(): return lax.ppermute(value, axis, pairs)]
  transfers between devices with their start and end apart: 13 -> 9, of which waited for: 7 -> 9; matrix products, arithmetic and copies ran while one was open for 51% -> 2% of each run, Pallas kernels for 0% -> 0%
where the time goes in v1:
time: 201 us; the launch traced here: 200 us
  waiting for transfers between devices  79.5 us (40%)
  blocking collectives  35.2 us (18%)
  starting transfers between devices  20.9 us (10%)
  local copies, waits for them, and re-layouts  20.4 us (10%)
  between operations  15 us (7%)
  matrix products  14.8 us (7%)
  other arithmetic  14.2 us (7%)
    psum x2, waiting for transfers between devices, on_device(): total_sum = lax.psum(partial_value.astype(jnp.bfloat16), 'deg')  57.2 us
    all_to_all x2, blocking collectives, on_device(): lax.all_to_all(spectra, 'lat', split_axis=1, concat_axis=3, tiled=True)  23 us
    ppermute x6, waiting for transfers between devices, passed_along(): return lax.ppermute(value, axis, pairs)  15.4 us
    ppermute x6, starting transfers between devices, passed_along(): return lax.ppermute(value, axis, pairs)  15.3 us
    all_to_all x1, blocking collectives, on_device(): lax.all_to_all(total_sum, 'lat', split_axis=3, concat_axis=1, tiled=True)  12.2 us
    dot_general x2, matrix products, legendre(): jnp.einsum('cmfl,mil->cmfi', scaled, basis, preferred_element_type=jnp.fl...  12 us
    unnamed x74, local copies, waits for them, and re-layouts  8.38 us
    all_to_all x1, waiting for transfers between devices, on_device(): lax.all_to_all(total_sum, 'lat', split_axis=3, concat_axis=1, tiled=True)  6.85 us
  transfers between devices with their start and end apart: 9, of which 9 were waited for; matrix products, arithmetic and copies ran while one was open for 2% of the time, Pallas kernels for 0%

profile of v1, /device:TPU:0, one launch (start us, length us, event | category | flops | bytes accessed | tf_op | source)
XLA Modules:
  0.0 200.0 jit_solution(16623130963314955521)
XLA Ops:
  9.3 1.3 multiply_multiply_fusion.3
  10.8 1.3 collective-permute-start
  13.4 4.8 %collective-permute-done = bf16[3,10752]{1,0:T(4,128)(2,1)S(1)} collective-permute-done((bf16[3,10752]{1,0:T(4,128)(2,1)S(1)}, bf16[3,10752]{1,0:T(4,128)(2,1)S(1)}, u32[]{:S(2)}, u32[]{:S(2)}) %collective-permute-start) | collective-permute-done | bytes 64544 | tf_op jit(solution)/shard_map/ppermute | solution.py:18
  18.3 1.3 broadcast_multiply_fusion.3
  19.7 4.8 %collective-permute-start.1 = (bf16[1,10752]{1,0:T(2,128)(2,1)S(1)}, bf16[1,10752]{1,0:T(2,128)(2,1)S(1)}, u32[]{:S(2)}, u32[]{:S(2)}) collective-permute-start(bf16[1,10752]{1,0:T(2,128)(2,1)S(1)} %slice.440), channel_id=1, source_target_pairs={{0,4},{4,8},{8,12},{12,16},{16,20},{20,24},{24,28},{1,5},{5,9},{9,... | collective-permute-start | bytes 64520 | tf_op jit(solution)/shard_map/ppermute | solution.py:18
  24.6 1.6 collective-permute-done.1
  30.0 1.1 reshape.104
  31.1 12.4 %all_to_all.72 = bf16[8,2,2048]{2,1,0:T(2,128)(2,1)S(1)} all-to-all(bf16[8,2,2048]{2,1,0:T(2,128)(2,1)S(1)} %reshape.104), channel_id=1, replica_groups=mesh['lat'=8,'deg'=4] {'lat'}, dimensions={0} | all-to-all | bytes 131072 | tf_op jit(solution)/shard_map/all_to_all | solution.py:145
  43.5 1.2 reshape.105
  44.7 1.3 copy.90
  46.2 6.0 %fusion.45 = bf16[2,128,2,64]{3,2,0,1:T(2,128)(2,1)} fusion(bf16[128,64,256]{2,1,0:T(8,128)(2,1)} %param.19, bf16[2,128,2,64]{3,2,0,1:T(2,128)(2,1)S(1)} %copy.60, f32[256]{0:T(256)S(1)} %copy-done.31), kind=kOutput, calls=%fused_computation.25 | convolution fusion | flops 33849344 | bytes 4326400 | tf_op jit(solution)/shard_map/cmfl,mil->cmfi/dot_general | solution.py:62
  52.2 29.1 %all-reduce.7.cloned.1.call-done = bf16[2,128,2,64]{3,2,0,1:T(2,128)(2,1)} async-done(((bf16[2,128,2,64]{3,2,0,1:T(2,128)(2,1)}), bf16[2,128,2,64]{3,2,0,1:T(2,128)(2,1)}) %all-reduce.7.cloned.1.call-update) | async-done | bytes 65552 | tf_op jit(solution)/shard_map/psum | solution.py:147
  81.3 1.7 copy.61
  83.0 5.5 %all-to-all-start.1 = ((bf16[2,128,2,64]{1,2,0,3:T(2,128)(2,1)}), bf16[2,128,2,64]{1,2,0,3:T(2,128)(2,1)S(1)}, u32[]{:S(2)}, u32[]{:S(2)}) async-start(bf16[2,128,2,64]{1,2,0,3:T(2,128)(2,1)} %copy.61), calls=%async_computation.1 | async-start | bytes 131072 | tf_op jit(solution)/shard_map/all_to_all | solution.py:148
  88.5 6.8 %all-to-all-done.1 = bf16[2,128,2,64]{1,2,0,3:T(2,128)(2,1)S(1)} async-done(((bf16[2,128,2,64]{1,2,0,3:T(2,128)(2,1)}), bf16[2,128,2,64]{1,2,0,3:T(2,128)(2,1)S(1)}, u32[]{:S(2)}, u32[]{:S(2)}) %all-to-all-start.1) | async-done | bytes 65568 | tf_op jit(solution)/shard_map/all_to_all | solution.py:148
  98.9 1.3 collective-permute-start.2
  101.4 3.5 %collective-permute-done.2 = bf16[2,10752]{1,0:T(2,128)(2,1)S(1)} collective-permute-done((bf16[2,10752]{1,0:T(2,128)(2,1)S(1)}, bf16[2,10752]{1,0:T(2,128)(2,1)S(1)}, u32[]{:S(2)}, u32[]{:S(2)}) %collective-permute-start.2) | collective-permute-done | bytes 43040 | tf_op jit(solution)/shard_map/ppermute | solution.py:18
  104.9 1.3 fusion.128
  106.5 3.4 %collective-permute-start.3 = (bf16[2,10752]{1,0:T(2,128)(2,1)S(1)}, bf16[2,10752]{1,0:T(2,128)(2,1)S(1)}, u32[]{:S(2)}, u32[]{:S(2)}) collective-permute-start(bf16[2,10752]{1,0:T(2,128)(2,1)S(1)} %pad_maximum_fusion.6), channel_id=1, source_target_pairs={{0,4},{4,8},{8,12},{12,16},{16,20},{20,24},{24,28},{1,5},{5,9},{9,... | collective-permute-start | bytes 129032 | tf_op jit(solution)/shard_map/ppermute | solution.py:18
  110.0 1.3 collective-permute-done.3
  114.7 1.1 reshape.106
  115.8 10.6 %all_to_all.73 = bf16[8,2,2048]{2,1,0:T(2,128)(2,1)S(1)} all-to-all(bf16[8,2,2048]{2,1,0:T(2,128)(2,1)S(1)} %reshape.106), channel_id=1, replica_groups=mesh['lat'=8,'deg'=4] {'lat'}, dimensions={0} | all-to-all | bytes 131072 | tf_op jit(solution)/shard_map/all_to_all | solution.py:145
  126.4 1.2 reshape.107
  127.6 1.3 copy.96
  129.1 6.0 %fusion.40 = bf16[2,128,2,64]{3,2,0,1:T(2,128)(2,1)} fusion(bf16[128,64,256]{2,1,0:T(8,128)(2,1)} %param.19, bf16[2,128,2,64]{3,2,0,1:T(2,128)(2,1)S(1)} %copy.69, f32[256]{0:T(256)S(1)} %copy-done.32), kind=kOutput, calls=%fused_computation.24 | convolution fusion | flops 33849344 | bytes 4326400 | tf_op jit(solution)/shard_map/cmfl,mil->cmfi/dot_general | solution.py:62
  135.1 28.1 %all-reduce.9.cloned.1.call-done = bf16[2,128,2,64]{3,2,0,1:T(2,128)(2,1)} async-done(((bf16[2,128,2,64]{3,2,0,1:T(2,128)(2,1)}), bf16[2,128,2,64]{3,2,0,1:T(2,128)(2,1)}) %all-reduce.9.cloned.1.call-update) | async-done | bytes 65552 | tf_op jit(solution)/shard_map/psum | solution.py:147
  163.2 1.0 copy.70
  164.3 12.2 %all_to_all.74 = bf16[2,128,2,64]{1,2,0,3:T(2,128)(2,1)S(1)} all-to-all(bf16[2,128,2,64]{1,2,0,3:T(2,128)(2,1)S(1)} %copy.70), channel_id=1, replica_groups=mesh['lat'=8,'deg'=4] {'lat'}, dimensions={3} | all-to-all | bytes 131072 | tf_op jit(solution)/shard_map/all_to_all | solution.py:148
  178.6 1.2 broadcast_multiply_fusion
  180.8 1.4 collective-permute-start.4
  183.3 3.5 %collective-permute-done.4 = bf16[1,10752]{1,0:T(2,128)(2,1)S(1)} collective-permute-done((bf16[1,10752]{1,0:T(2,128)(2,1)S(1)}, bf16[1,10752]{1,0:T(2,128)(2,1)S(1)}, u32[]{:S(2)}, u32[]{:S(2)}) %collective-permute-start.4) | collective-permute-done | bytes 21536 | tf_op jit(solution)/shard_map/ppermute | solution.py:18
  187.3 3.2 %collective-permute-start.5 = (bf16[1,10752]{1,0:T(2,128)(2,1)S(1)}, bf16[1,10752]{1,0:T(2,128)(2,1)S(1)}, u32[]{:S(2)}, u32[]{:S(2)}) collective-permute-start(bf16[1,10752]{1,0:T(2,128)(2,1)S(1)} %slice.435), channel_id=1, source_target_pairs={{0,4},{4,8},{8,12},{12,16},{16,20},{20,24},{24,28},{1,5},{5,9},{9,... | collective-permute-start | bytes 64520 | tf_op jit(solution)/shard_map/ppermute | solution.py:18
  (167 shorter events, 23.2 us)
Async XLA Ops:
  7.2 74.1 %all-reduce.7.cloned.1.call-start = ((), (), s32[]{:S(2)}) async-start(), calls=%async_computation.4 | async-start | bytes 262144 | tf_op jit(solution)/shard_map/psum | solution.py:147
  9.3 3.1 %copy-start.1 = (f32[8,10752]{1,0:T(8,128)}, f32[8,10752]{1,0:T(8,128)S(1)}, u32[]{:S(2)}) copy-start(f32[8,10752]{1,0:T(8,128)S(1)} %convert_element_type.99) | copy-start | bytes 1032196
  9.3 3.0 %copy-start.3 = (f32[8,10752]{1,0:T(8,128)S(1)}, f32[8,10752]{1,0:T(8,128)}, u32[]{:S(2)}) copy-start(f32[8,10752]{1,0:T(8,128)} %param.16) | copy-start | bytes 1032196
  10.8 7.4 %collective-permute-start = (bf16[3,10752]{1,0:T(4,128)(2,1)S(1)}, bf16[3,10752]{1,0:T(4,128)(2,1)S(1)}, u32[]{:S(2)}, u32[]{:S(2)}) collective-permute-start(bf16[3,10752]{1,0:T(4,128)(2,1)S(1)} %pad_maximum_fusion.4), channel_id=1, source_target_pairs={{4,0},{8,4},{12,8},{16,12},{20,16},{24,20},{28,24},{5,1},{9,5},{13... | collective-permute-start | bytes 193544 | tf_op jit(solution)/shard_map/ppermute | solution.py:18
  12.5 5.8 %copy-start = (s32[8,10752]{1,0:T(8,128)S(1)}, s32[8,10752]{1,0:T(8,128)}, u32[]{:S(2)}) copy-start(s32[8,10752]{1,0:T(8,128)} %param.18) | copy-start | bytes 1032196
  12.5 5.8 %slice-start = ((f32[8,10752]{1,0:T(8,128)}), f32[8,1]{1,0:T(8,128)S(1)}, s32[]{:S(2)}) async-start(f32[8,10752]{1,0:T(8,128)} %copy-done.1), calls=%async_computation.6 | async-start | bytes 8192 | tf_op jit(solution)/shard_map/jit(_roll_static)/slice | solution.py:114
  12.5 5.8 %slice-start.1 = ((f32[8,10752]{1,0:T(8,128)}), f32[8,1]{1,0:T(8,128)S(1)}, s32[]{:S(2)}) async-start(f32[8,10752]{1,0:T(8,128)} %param.16), calls=%async_computation.7 | async-start | bytes 8192 | tf_op jit(solution)/shard_map/jit(_roll_static)/slice | solution.py:116
  12.6 5.8 %copy-start.23 = (f32[2,8,10752]{2,1,0:T(8,128)S(1)}, f32[2,8,10752]{2,1,0:T(8,128)}, u32[]{:S(2)}) copy-start(f32[2,8,10752]{2,1,0:T(8,128)} %param.15) | copy-start | bytes 2064388
  19.7 6.4 %collective-permute-start.1 = (bf16[1,10752]{1,0:T(2,128)(2,1)S(1)}, bf16[1,10752]{1,0:T(2,128)(2,1)S(1)}, u32[]{:S(2)}, u32[]{:S(2)}) collective-permute-start(bf16[1,10752]{1,0:T(2,128)(2,1)S(1)} %slice.440), channel_id=1, source_target_pairs={{0,4},{4,8},{8,12},{12,16},{16,20},{20,24},{24,28},{1,5},{5,9},{9,... | collective-permute-start | bytes 64520 | tf_op jit(solution)/shard_map/ppermute | solution.py:18
  24.5 4.7 %copy-start.29 = (f32[2,8]{1,0:T(2,128)}, f32[2,8]{1,0:T(2,128)S(1)}, u32[]{:S(2)}) copy-start(f32[2,8]{1,0:T(2,128)S(1)} %get-tuple-element.62) | copy-start | bytes 196
  24.5 72.2 %copy-start.27 = (f32[2,8]{1,0:T(2,128)}, f32[2,8]{1,0:T(2,128)S(1)}, u32[]{:S(2)}) copy-start(f32[2,8]{1,0:T(2,128)S(1)} %get-tuple-element.61) | copy-start | bytes 196
  31.1 15.1 %copy-start.31 = (f32[256]{0:T(256)S(1)}, f32[256]{0:T(256)}, u32[]{:S(2)}) copy-start(f32[256]{0:T(256)} %param.20) | copy-start | bytes 3076
  46.1 49.5 %copy-start.25 = (bf16[2,2,13,128,1]{3,2,1,0,4:T(8,128)(2,1)S(1)}, bf16[2,2,13,128,1]{3,2,1,0,4:T(8,128)(2,1)}, u32[]{:S(2)}) copy-start(bf16[2,2,13,128,1]{3,2,1,0,4:T(8,128)(2,1)} %constant.67) | copy-start | bytes 39940
  83.0 12.4 %all-to-all-start.1 = ((bf16[2,128,2,64]{1,2,0,3:T(2,128)(2,1)}), bf16[2,128,2,64]{1,2,0,3:T(2,128)(2,1)S(1)}, u32[]{:S(2)}, u32[]{:S(2)}) async-start(bf16[2,128,2,64]{1,2,0,3:T(2,128)(2,1)} %copy.61), calls=%async_computation.1 | async-start | bytes 131072 | tf_op jit(solution)/shard_map/all_to_all | solution.py:148
  88.5 74.7 %all-reduce.9.cloned.1.call-start = ((), (), s32[]{:S(2)}) async-start(), calls=%async_computation.5 | async-start | bytes 262144 | tf_op jit(solution)/shard_map/psum | solution.py:147
  97.8 2.5 %copy-start.5 = (f32[8,10752]{1,0:T(8,128)S(1)}, f32[8,10752]{1,0:T(8,128)}, u32[]{:S(2)}) copy-start(f32[8,10752]{1,0:T(8,128)} %param.17) | copy-start | bytes 1032196
  97.8 2.5 %copy-start.17 = (f32[8,10752]{1,0:T(8,128)S(1)}, f32[8,10752]{1,0:T(8,128)}, u32[]{:S(2)}) copy-start(f32[8,10752]{1,0:T(8,128)} %get-tuple-element.28) | copy-start | bytes 1032196
  98.9 5.9 %collective-permute-start.2 = (bf16[2,10752]{1,0:T(2,128)(2,1)S(1)}, bf16[2,10752]{1,0:T(2,128)(2,1)S(1)}, u32[]{:S(2)}, u32[]{:S(2)}) collective-permute-start(bf16[2,10752]{1,0:T(2,128)(2,1)S(1)} %pad_maximum_fusion.5), channel_id=1, source_target_pairs={{4,0},{8,4},{12,8},{16,12},{20,16},{24,20},{28,24},{5,1},{9,5},{13... | collective-permute-start | bytes 129032 | tf_op jit(solution)/shard_map/ppermute | solution.py:18
  101.1 3.8 %copy-start.7 = (f32[8,10752]{1,0:T(8,128)S(1)}, f32[8,10752]{1,0:T(8,128)}, u32[]{:S(2)}) copy-start(f32[8,10752]{1,0:T(8,128)} %get-tuple-element.42) | copy-start | bytes 1032196
  101.1 3.8 %copy-start.9 = (f32[8,10752]{1,0:T(8,128)S(1)}, f32[8,10752]{1,0:T(8,128)}, u32[]{:S(2)}) copy-start(f32[8,10752]{1,0:T(8,128)} %get-tuple-element.43) | copy-start | bytes 1032196
  101.1 3.8 %copy-start.24 = (f32[2,8,10752]{2,1,0:T(8,128)S(1)}, f32[2,8,10752]{2,1,0:T(8,128)}, u32[]{:S(2)}) copy-start(f32[2,8,10752]{2,1,0:T(8,128)} %param.13) | copy-start | bytes 2064388
  106.5 4.9 %collective-permute-start.3 = (bf16[2,10752]{1,0:T(2,128)(2,1)S(1)}, bf16[2,10752]{1,0:T(2,128)(2,1)S(1)}, u32[]{:S(2)}, u32[]{:S(2)}) collective-permute-start(bf16[2,10752]{1,0:T(2,128)(2,1)S(1)} %pad_maximum_fusion.6), channel_id=1, source_target_pairs={{0,4},{4,8},{8,12},{12,16},{16,20},{20,24},{24,28},{1,5},{5,9},{9,... | collective-permute-start | bytes 129032 | tf_op jit(solution)/shard_map/ppermute | solution.py:18
  115.8 13.2 %copy-start.32 = (f32[256]{0:T(256)S(1)}, f32[256]{0:T(256)}, u32[]{:S(2)}) copy-start(f32[256]{0:T(256)} %param.20) | copy-start | bytes 3076
  129.0 47.7 %copy-start.26 = (bf16[2,2,13,128,1]{3,2,1,0,4:T(8,128)(2,1)S(1)}, bf16[2,2,13,128,1]{3,2,1,0,4:T(8,128)(2,1)}, u32[]{:S(2)}) copy-start(bf16[2,2,13,128,1]{3,2,1,0,4:T(8,128)(2,1)} %constant.67) | copy-start | bytes 39940
  135.1 42.1 %copy-start.22 = (f32[84,128]{1,0:T(8,128)S(1)}, f32[84,128]{1,0:T(8,128)}, u32[]{:S(2)}) copy-start(f32[84,128]{1,0:T(8,128)} %constant.64) | copy-start | bytes 129028
  180.7 6.2 %copy-start.6 = (f32[8,10752]{1,0:T(8,128)S(1)}, f32[8,10752]{1,0:T(8,128)}, u32[]{:S(2)}) copy-start(f32[8,10752]{1,0:T(8,128)} %param.17) | copy-start | bytes 1032196
  180.7 6.2 %copy-start.8 = (f32[8,10752]{1,0:T(8,128)S(1)}, f32[8,10752]{1,0:T(8,128)}, u32[]{:S(2)}) copy-start(f32[8,10752]{1,0:T(8,128)} %get-tuple-element.42) | copy-start | bytes 1032196
  180.7 6.2 %copy-start.10 = (f32[8,10752]{1,0:T(8,128)S(1)}, f32[8,10752]{1,0:T(8,128)}, u32[]{:S(2)}) copy-start(f32[8,10752]{1,0:T(8,128)} %get-tuple-element.43) | copy-start | bytes 1032196
  180.7 6.2 %copy-start.15 = (f32[8,10752]{1,0:T(8,128)S(1)}, f32[8,10752]{1,0:T(8,128)}, u32[]{:S(2)}) copy-start(f32[8,10752]{1,0:T(8,128)} %get-tuple-element.21) | copy-start | bytes 1032196
  180.7 6.2 %copy-start.16 = (f32[8,10752]{1,0:T(8,128)S(1)}, f32[8,10752]{1,0:T(8,128)}, u32[]{:S(2)}) copy-start(f32[8,10752]{1,0:T(8,128)} %get-tuple-element.40) | copy-start | bytes 1032196
  180.8 6.0 %collective-permute-start.4 = (bf16[1,10752]{1,0:T(2,128)(2,1)S(1)}, bf16[1,10752]{1,0:T(2,128)(2,1)S(1)}, u32[]{:S(2)}, u32[]{:S(2)}) collective-permute-start(bf16[1,10752]{1,0:T(2,128)(2,1)S(1)} %slice.436), channel_id=1, source_target_pairs={{4,0},{8,4},{12,8},{16,12},{20,16},{24,20},{28,24},{5,1},{9,5},{13... | collective-permute-start | bytes 64520 | tf_op jit(solution)/shard_map/ppermute | solution.py:18
  187.3 4.9 %collective-permute-start.5 = (bf16[1,10752]{1,0:T(2,128)(2,1)S(1)}, bf16[1,10752]{1,0:T(2,128)(2,1)S(1)}, u32[]{:S(2)}, u32[]{:S(2)}) collective-permute-start(bf16[1,10752]{1,0:T(2,128)(2,1)S(1)} %slice.435), channel_id=1, source_target_pairs={{0,4},{4,8},{8,12},{12,16},{16,20},{20,24},{24,28},{1,5},{5,9},{9,... | collective-permute-start | bytes 64520 | tf_op jit(solution)/shard_map/ppermute | solution.py:18
  (14 other events, 16.2 us)
Sparse Core Ops, SparseCore 0:
  52.3 28.9 all-reduce.6
  135.2 27.9 all-reduce.8

commit v2 on v1

--- a/solution.py
+++ b/solution.py
@@ -1,7 +1,10 @@
+import functools
 import jax
 import jax.numpy as jnp
 import numpy as np
 from jax import lax
+from jax.experimental import pallas as pl
+from jax.experimental.pallas import tpu as pltpu
 from jax.sharding import PartitionSpec as P
 
 STEPS = 2
@@ -51,9 +54,9 @@
         [first[0] * turn[0] - first[1] * turn[1], first[1] * turn[0] + first[0] * turn[1]]
     ).astype(jnp.bfloat16)
     second = jnp.stack([jnp.stack([inner[0], -inner[1]]), jnp.stack([inner[1], inner[0]])])
-    spectra = jnp.einsum("crkb,dcnb->dnkr", turned, second, preferred_element_type=jnp.float32)
-    spectra = spectra.reshape(2, -1, 2, row_count)[:, :order_count] * (1.0 / lon_count)
-    return (spectra * analysis_weight[None, None, :, :]).astype(jnp.bfloat16)
+    spectra = jnp.einsum("crkb,dcnb->drnk", turned, second, preferred_element_type=jnp.float32)
+    spectra = spectra.reshape(2, 2, row_count, -1)[..., :order_count] * (1.0 / lon_count)
+    return (spectra * analysis_weight[None, :, :, None]).astype(jnp.bfloat16)
 
 
 def legendre(spectra, basis, love):
@@ -65,18 +68,134 @@
 def synthesise(coeffs, factors, tables, output_weight):
     outer, turn, inner = tables
     major, blocks = turn.shape[1], inner.shape[1]
-    order_count = coeffs.shape[1]
-    row_count = coeffs.shape[3]
-    scaled = coeffs * factors[None, :, None, None]
-    padded = jnp.pad(scaled, ((0, 0), (0, major * blocks - order_count), (0, 0), (0, 0)))
-    padded = padded.reshape(2, blocks, major, 2 * row_count)
+    row_count, order_count = coeffs.shape[2:]
+    scaled = (coeffs * factors).reshape(2, 2 * row_count, order_count)
+    padded = jnp.pad(scaled, ((0, 0), (0, 0), (0, major * blocks - order_count)))
+    padded = padded.reshape(2, 2 * row_count, blocks, major)
     second = jnp.stack([jnp.stack([inner[0], inner[1]]), jnp.stack([-inner[1], inner[0]])])
-    first = jnp.einsum("cnkr,dcnb->drkb", padded, second, preferred_element_type=jnp.float32)
+    first = jnp.einsum("crnk,dcnb->drkb", padded, second, preferred_element_type=jnp.float32)
     turned = jnp.stack(
         [first[0] * turn[0] + first[1] * turn[1], first[1] * turn[0] - first[0] * turn[1]]
     ).astype(jnp.bfloat16)
     grid_out = jnp.einsum("cka,crkb->rab", outer, turned, preferred_element_type=jnp.float32)
     return grid_out.reshape(2, row_count, -1) * output_weight[:, :, None]
+
+
+def greet(count, device_of):
+    barrier = pltpu.get_barrier_semaphore()
+
+    def one(step, carry):
+        pl.semaphore_signal(
+            barrier, inc=1, device_id=device_of(step), device_id_type=pl.DeviceIdType.MESH
+        )
+        return carry
+
+    lax.fori_loop(1, count, one, 0)
+    pl.semaphore_wait(barrier, count - 1)
+
+
+def swap(count, copy_of):
+    def begin(step, carry):
+        copy_of(step).start()
+        return carry
+
+    def finish(step, carry):
+        copy_of(step).wait()
+        return carry
+
+    lax.fori_loop(1, count, begin, 0)
+    return lambda: lax.fori_loop(1, count, finish, 0)
+
+
+def spread_kernel(lat_count, send_ref, out_ref, held, send_sem, recv_sem):
+    me_lat, me_deg = lax.axis_index("lat"), lax.axis_index("deg")
+
+    def device_of(step):
+        return (lax.rem(me_lat + step, lat_count), me_deg)
+
+    def copy_of(step):
+        peer = device_of(step)
+        return pltpu.make_async_remote_copy(
+            src_ref=send_ref.at[peer[0]],
+            dst_ref=held.at[me_lat],
+            send_sem=send_sem.at[step - 1],
+            recv_sem=recv_sem.at[step - 1],
+            device_id=peer,
+            device_id_type=pl.DeviceIdType.MESH,
+        )
+
+    greet(lat_count, device_of)
+    finish = swap(lat_count, copy_of)
+    held[me_lat] = send_ref[me_lat]
+    finish()
+    out_ref[...] = held[...]
+
+
+def gather_kernel(lat_count, deg_count, send_ref, out_ref, held, send_sem, recv_sem):
+    count = lat_count * deg_count
+    me_lat, me_deg = lax.axis_index("lat"), lax.axis_index("deg")
+    me = me_lat * deg_count + me_deg
+
+    def device_of(step):
+        peer = lax.rem(me + step, count)
+        return (lax.div(peer, deg_count), lax.rem(peer, deg_count))
+
+    def copy_of(step):
+        peer = device_of(step)
+        return pltpu.make_async_remote_copy(
+            src_ref=send_ref.at[peer[0]],
+            dst_ref=held.at[me],
+            send_sem=send_sem.at[step - 1],
+            recv_sem=recv_sem.at[step - 1],
+            device_id=peer,
+            device_id_type=pl.DeviceIdType.MESH,
+        )
+
+    greet(count, device_of)
+    finish = swap(count, copy_of)
+    held[me] = send_ref[me_lat]
+    finish()
+    for source in range(lat_count):
+        total = held[source * deg_count].astype(jnp.float32)
+        for part in range(1, deg_count):
+            total = total + held[source * deg_count + part].astype(jnp.float32)
+        out_ref[source] = total.astype(out_ref.dtype)
+
+
+def exchange(kernel, count, peers, blocks, collective_id):
+    return pl.pallas_call(
+        kernel,
+        out_shape=jax.ShapeDtypeStruct(blocks.shape, blocks.dtype),
+        in_specs=[pl.BlockSpec(memory_space=pltpu.VMEM)],
+        out_specs=pl.BlockSpec(memory_space=pltpu.VMEM),
+        scratch_shapes=[
+            pltpu.VMEM((count,) + blocks.shape[1:], blocks.dtype),
+            pltpu.SemaphoreType.DMA((peers - 1,)),
+            pltpu.SemaphoreType.DMA((peers - 1,)),
+        ],
+        compiler_params=pltpu.CompilerParams(collective_id=collective_id, has_side_effects=True),
+    )(blocks)
+
+
+def spread_orders(spectra, lat_count):
+    row_count, order_total = spectra.shape[2:]
+    owned = order_total // lat_count
+    blocks = spectra.reshape(4 * row_count, lat_count, owned).transpose(1, 0, 2)
+    kernel = functools.partial(spread_kernel, lat_count)
+    got = exchange(kernel, lat_count, lat_count, blocks, 0)
+    got = got.reshape(lat_count, 2, 2, row_count, owned).transpose(1, 4, 2, 0, 3)
+    return got.reshape(2, owned, 2, lat_count * row_count)
+
+
+def gather_rows(partial_value, lat_count, deg_count):
+    owned, total_rows = partial_value.shape[1], partial_value.shape[3]
+    row_count = total_rows // lat_count
+    blocks = partial_value.reshape(2, owned, 2, lat_count, row_count).transpose(3, 0, 2, 4, 1)
+    blocks = blocks.reshape(lat_count, 4 * row_count, owned)
+    kernel = functools.partial(gather_kernel, lat_count, deg_count)
+    count = lat_count * deg_count
+    got = exchange(kernel, count, count, blocks, 1)
+    return got.transpose(1, 0, 2).reshape(2, 2, row_count, lat_count * owned)
 
 
 def edges_from(rows, by):
@@ -142,10 +261,9 @@
         q_down = southward(q_term, q_edge)
         psi_bar = flux_p - jnp.roll(flux_p, 1, 1) + kappa_y * (q_term - q_down)
         spectra = analyse(jnp.stack([state_eta, psi_bar]), analysis_weight, tables, order_total)
-        owned_rows = lax.all_to_all(spectra, "lat", split_axis=1, concat_axis=3, tiled=True)
-        partial_value = legendre(owned_rows, basis, love)
-        total_sum = lax.psum(partial_value.astype(jnp.bfloat16), "deg")
-        banded = lax.all_to_all(total_sum, "lat", split_axis=3, concat_axis=1, tiled=True)
+        owned_rows = spread_orders(spectra, lat_count)
+        partial_value = legendre(owned_rows, basis, love).astype(jnp.bfloat16)
+        banded = gather_rows(partial_value, lat_count, lax.axis_size("deg"))
         loads = synthesise(banded, full_factor, tables, output_weight)
         last = step_index == STEPS - 1
         psi_now = state_eta - loads[0]

time: 201 us -> 129 us (0.64)
  waiting for transfers between devices: 79.5 us -> 14.8 us
  Pallas kernels: 0 us -> 42.7 us
  blocking collectives: 35.2 us -> 0 us
  between operations: 15 us -> 1.49 us
  starting transfers between devices: 20.9 us -> 18.3 us
  matrix products: 14.8 us -> 16.9 us
    psum x2 -> x0, waiting for transfers between devices: 57.2 us -> none  [on_device(): total_sum = lax.psum(partial_value.astype(jnp.bfloat16), 'deg')]
    pallas_call x0 -> x4, Pallas kernels: none -> 42.7 us  [exchange(): pl.pallas_call(kernel, out_shape=jax.ShapeDtypeStruct(blocks.shape, block...]
    all_to_all x3 -> x0, blocking collectives: 35.2 us -> none  [the longest x2 23 us: on_device(): lax.all_to_all(spectra, 'lat', split_axis=1, concat_axis=3, tiled=True)]
    all_to_all x1 -> x0, waiting for transfers between devices: 6.85 us -> none  [on_device(): lax.all_to_all(total_sum, 'lat', split_axis=3, concat_axis=1, tiled=True)]
    all_to_all x1 -> x0, starting transfers between devices: 5.51 us -> none  [on_device(): lax.all_to_all(total_sum, 'lat', split_axis=3, concat_axis=1, tiled=True)]
    unnamed x74 -> x58, local copies, waits for them, and re-layouts: 8.38 us -> 3.51 us
    reshape x4 -> x12, local copies, waits for them, and re-layouts: 0.7 us -> 4.93 us  [the longest x2 1.7 us: spread_orders(): got.reshape(lat_count, 2, 2, row_count, owned).transpose(1, 4, 2, 0, 3)]
    transpose x0 -> x4, local copies, waits for them, and re-layouts: none -> 3.03 us  [the longest x2 1.74 us: gather_rows(): return got.transpose(1, 0, 2).reshape(2, 2, row_count, lat_count * owned)]
  transfers between devices with their start and end apart: 9 -> 6, of which waited for: 9 -> 6; matrix products, arithmetic and copies ran while one was open for 2% -> 4% of each run, Pallas kernels for 0% -> 0%
where the time goes in v2:
time: 129 us; the launch traced here: 128 us
  Pallas kernels  42.7 us (33%)
  local copies, waits for them, and re-layouts  18.9 us (15%)
  starting transfers between devices  18.3 us (14%)
  matrix products  16.9 us (13%)
  waiting for transfers between devices  14.8 us (11%)
  other arithmetic  14.7 us (11%)
  between operations  1.49 us (1%)
    pallas_call x4, Pallas kernels, exchange(): pl.pallas_call(kernel, out_shape=jax.ShapeDtypeStruct(blocks.shape, block...  42.7 us
    ppermute x6, starting transfers between devices, passed_along(): return lax.ppermute(value, axis, pairs)  18.3 us
    ppermute x6, waiting for transfers between devices, passed_along(): return lax.ppermute(value, axis, pairs)  14.8 us
    dot_general x2, matrix products, legendre(): jnp.einsum('cmfl,mil->cmfi', scaled, basis, preferred_element_type=jnp.fl...  10.7 us
    unnamed x58, local copies, waits for them, and re-layouts  3.51 us
    reshape x2, local copies, waits for them, and re-layouts, synthesise(): return grid_out.reshape(2, row_count, -1) * output_weight[:, :, None]  3.27 us
    another operation x3, other arithmetic, on_device(): state_vel, back_vel = (jnp.stack(state_vel), jnp.stack(back_vel))  2.74 us
  transfers between devices with their start and end apart: 6, of which 6 were waited for; matrix products, arithmetic and copies ran while one was open for 4% of the time, Pallas kernels for 0%

profile of v2, /device:TPU:0, one launch (start us, length us, event | category | flops | bytes accessed | tf_op | source)
XLA Modules:
  0.0 127.8 jit_solution(3103316773328808224)
XLA Ops:
  0.7 1.0 slice.442
  1.7 1.0 convert_element_type.99
  2.8 1.3 %multiply_multiply_fusion.3 = (f32[8,10752]{1,0:T(8,128)S(1)}, f32[8,10752]{1,0:T(8,128)S(1)}) fusion(f32[8,10752]{1,0:T(8,128)} %param.14, f32[8]{0:T(128)S(1)} %add_divide_fusion, s32[8,10752]{1,0:T(8,128)} %param.18), kind=kLoop, calls=%fused_computation.129 | loop fusion | flops 430080 | bytes 1376288 | tf_op jit(solution)/shard_map/mul | solution.py:250
  4.3 1.3 %collective-permute-start = (bf16[3,10752]{1,0:T(4,128)(2,1)S(1)}, bf16[3,10752]{1,0:T(4,128)(2,1)S(1)}, u32[]{:S(2)}, u32[]{:S(2)}) collective-permute-start(bf16[3,10752]{1,0:T(4,128)(2,1)S(1)} %pad_maximum_fusion.4), channel_id=1, source_target_pairs={{4,0},{8,4},{12,8},{16,12},{20,16},{24,20},{28,24},{5,1},{9,5},{13... | collective-permute-start | bytes 193544 | tf_op jit(solution)/shard_map/ppermute | solution.py:21
  6.8 4.8 %collective-permute-done = bf16[3,10752]{1,0:T(4,128)(2,1)S(1)} collective-permute-done((bf16[3,10752]{1,0:T(4,128)(2,1)S(1)}, bf16[3,10752]{1,0:T(4,128)(2,1)S(1)}, u32[]{:S(2)}, u32[]{:S(2)}) %collective-permute-start) | collective-permute-done | bytes 64544 | tf_op jit(solution)/shard_map/ppermute | solution.py:21
  11.8 1.2 broadcast_multiply_fusion.3
  13.0 4.8 %collective-permute-start.1 = (bf16[1,10752]{1,0:T(2,128)(2,1)S(1)}, bf16[1,10752]{1,0:T(2,128)(2,1)S(1)}, u32[]{:S(2)}, u32[]{:S(2)}) collective-permute-start(bf16[1,10752]{1,0:T(2,128)(2,1)S(1)} %slice.440), channel_id=1, source_target_pairs={{0,4},{4,8},{8,12},{12,16},{16,20},{20,24},{24,28},{1,5},{5,9},{9,... | collective-permute-start | bytes 64520 | tf_op jit(solution)/shard_map/ppermute | solution.py:21
  18.4 1.0 collective-permute-done.1
  23.2 9.5 %shard_map.147 = bf16[8,32,128]{2,1,0:T(8,128)(2,1)} custom-call(bf16[8,32,128]{2,1,0:T(8,128)(2,1)} %bitcast.239), custom_call_target="tpu_custom_call" | custom-call | tf_op jit(solution)/shard_map/pallas_call | solution.py:166
  33.7 5.3 %fusion.45 = bf16[2,128,2,64]{3,2,0,1:T(2,128)(2,1)S(1)} fusion(bf16[128,64,256]{2,1,0:T(8,128)(2,1)} %param.19, bf16[2,128,2,64]{3,2,0,1:T(2,128)(2,1)S(1)} %copy.41, f32[256]{0:T(256)S(1)} %copy-done.24), kind=kOutput, calls=%fused_computation.25 | convolution fusion | flops 33849344 | bytes 4326400 | tf_op jit(solution)/shard_map/cmfl,mil->cmfi/dot_general | solution.py:65
  39.8 11.9 %shard_map.148 = bf16[8,32,128]{2,1,0:T(8,128)(2,1)} custom-call(bf16[8,32,128]{2,1,0:T(8,128)(2,1)} %bitcast.241), custom_call_target="tpu_custom_call" | custom-call | tf_op jit(solution)/shard_map/pallas_call | solution.py:166
  53.5 1.2 convolution_bitcast_fusion.5
  54.7 1.2 reshape.126
  58.2 1.3 %collective-permute-start.2 = (bf16[2,10752]{1,0:T(2,128)(2,1)S(1)}, bf16[2,10752]{1,0:T(2,128)(2,1)S(1)}, u32[]{:S(2)}, u32[]{:S(2)}) collective-permute-start(bf16[2,10752]{1,0:T(2,128)(2,1)S(1)} %pad_maximum_fusion.5), channel_id=1, source_target_pairs={{4,0},{8,4},{12,8},{16,12},{20,16},{24,20},{28,24},{5,1},{9,5},{13... | collective-permute-start | bytes 129032 | tf_op jit(solution)/shard_map/ppermute | solution.py:21
  59.5 1.0 multiply_bitcast_fusion.1
  60.7 3.4 %collective-permute-done.2 = bf16[2,10752]{1,0:T(2,128)(2,1)S(1)} collective-permute-done((bf16[2,10752]{1,0:T(2,128)(2,1)S(1)}, bf16[2,10752]{1,0:T(2,128)(2,1)S(1)}, u32[]{:S(2)}, u32[]{:S(2)}) %collective-permute-start.2) | collective-permute-done | bytes 43040 | tf_op jit(solution)/shard_map/ppermute | solution.py:21
  64.1 1.3 %fusion.128 = (f32[8,10752]{1,0:T(8,128)S(1)}, f32[8,10752]{1,0:T(8,128)}, f32[8,10752]{1,0:T(8,128)S(1)}, f32[8,10752]{1,0:T(8,128)}, f32[1,8,10752]{2,1,0:T(8,...) fusion(f32[8,10752]{1,0:T(8,128)S(1)} %get-tuple-element.30, f32[8,10752]{1,0:T(8,128)S(1)} %get-tuple-element.29, ...), kind=kLoop, calls=%fused_computation.176 | loop fusion | flops 1978368 | bytes 7225376 | tf_op jit(solution)/shard_map/mul | solution.py:281
  65.7 4.8 %collective-permute-start.3 = (bf16[2,10752]{1,0:T(2,128)(2,1)S(1)}, bf16[2,10752]{1,0:T(2,128)(2,1)S(1)}, u32[]{:S(2)}, u32[]{:S(2)}) collective-permute-start(bf16[2,10752]{1,0:T(2,128)(2,1)S(1)} %pad_maximum_fusion.6), channel_id=1, source_target_pairs={{0,4},{4,8},{8,12},{12,16},{16,20},{20,24},{24,28},{1,5},{5,9},{9,... | collective-permute-start | bytes 129032 | tf_op jit(solution)/shard_map/ppermute | solution.py:21
  70.6 1.3 %collective-permute-done.3 = bf16[2,10752]{1,0:T(2,128)(2,1)S(1)} collective-permute-done((bf16[2,10752]{1,0:T(2,128)(2,1)S(1)}, bf16[2,10752]{1,0:T(2,128)(2,1)S(1)}, u32[]{:S(2)}, u32[]{:S(2)}) %collective-permute-start.3) | collective-permute-done | bytes 43040 | tf_op jit(solution)/shard_map/ppermute | solution.py:21
  73.4 1.3 %convolution_bitcast_fusion.1 = f32[2,16,84,128]{3,2,0,1:T(8,128)S(1)} fusion(bf16[2,84,84,1]{2,1,0,3:T(8,128)(2,1)S(1)} %copy-done.13, bf16[16,84,128,1]{2,1,0,3:T(8,128)(2,1)} %reshape.147), kind=kOutput, calls=%fused_computation.9 | convolution fusion | flops 57802752 | bytes 1748544 | tf_op jit(solution)/shard_map/cka,rab->crkb/dot_general | solution.py:52
  75.5 1.1 convolution_bitcast_fusion.6
  76.5 1.1 reshape.127
  78.4 9.3 %shard_map.149 = bf16[8,32,128]{2,1,0:T(8,128)(2,1)} custom-call(bf16[8,32,128]{2,1,0:T(8,128)(2,1)} %bitcast.244), custom_call_target="tpu_custom_call" | custom-call | tf_op jit(solution)/shard_map/pallas_call | solution.py:166
  88.7 5.3 %fusion.40 = bf16[2,128,2,64]{3,2,0,1:T(2,128)(2,1)S(1)} fusion(bf16[128,64,256]{2,1,0:T(8,128)(2,1)} %param.19, bf16[2,128,2,64]{3,2,0,1:T(2,128)(2,1)S(1)} %copy.49, f32[256]{0:T(256)S(1)} %copy-done.25), kind=kOutput, calls=%fused_computation.24 | convolution fusion | flops 33849344 | bytes 4326400 | tf_op jit(solution)/shard_map/cmfl,mil->cmfi/dot_general | solution.py:65
  94.8 12.0 %shard_map.150 = bf16[8,32,128]{2,1,0:T(8,128)(2,1)} custom-call(bf16[8,32,128]{2,1,0:T(8,128)(2,1)} %bitcast.246), custom_call_target="tpu_custom_call" | custom-call | tf_op jit(solution)/shard_map/pallas_call | solution.py:166
  108.6 1.2 convolution_bitcast_fusion.4
  109.7 2.1 %reshape.135 = f32[2,8,10752]{2,1,0:T(8,128)} reshape(f32[16,84,128]{2,1,0:T(8,128)} %convolution_bitcast_fusion.4) | data formatting | bytes 1376256 | tf_op jit(solution)/shard_map/reshape | solution.py:81
  111.8 1.2 broadcast_multiply_fusion
  113.9 1.4 %collective-permute-start.4 = (bf16[1,10752]{1,0:T(2,128)(2,1)S(1)}, bf16[1,10752]{1,0:T(2,128)(2,1)S(1)}, u32[]{:S(2)}, u32[]{:S(2)}) collective-permute-start(bf16[1,10752]{1,0:T(2,128)(2,1)S(1)} %slice.436), channel_id=1, source_target_pairs={{4,0},{8,4},{12,8},{16,12},{20,16},{24,20},{28,24},{5,1},{9,5},{13... | collective-permute-start | bytes 64520 | tf_op jit(solution)/shard_map/ppermute | solution.py:21
  116.4 3.5 %collective-permute-done.4 = bf16[1,10752]{1,0:T(2,128)(2,1)S(1)} collective-permute-done((bf16[1,10752]{1,0:T(2,128)(2,1)S(1)}, bf16[1,10752]{1,0:T(2,128)(2,1)S(1)}, u32[]{:S(2)}, u32[]{:S(2)}) %collective-permute-start.4) | collective-permute-done | bytes 21536 | tf_op jit(solution)/shard_map/ppermute | solution.py:21
  120.4 4.7 %collective-permute-start.5 = (bf16[1,10752]{1,0:T(2,128)(2,1)S(1)}, bf16[1,10752]{1,0:T(2,128)(2,1)S(1)}, u32[]{:S(2)}, u32[]{:S(2)}) collective-permute-start(bf16[1,10752]{1,0:T(2,128)(2,1)S(1)} %slice.435), channel_id=1, source_target_pairs={{0,4},{4,8},{8,12},{12,16},{16,20},{20,24},{24,28},{1,5},{5,9},{9,... | collective-permute-start | bytes 64520 | tf_op jit(solution)/shard_map/ppermute | solution.py:21
  126.8 0.9 fusion.101
  (150 shorter events, 22.5 us)
Async XLA Ops:
  2.7 3.1 %copy-start.1 = (f32[8,10752]{1,0:T(8,128)}, f32[8,10752]{1,0:T(8,128)S(1)}, u32[]{:S(2)}) copy-start(f32[8,10752]{1,0:T(8,128)S(1)} %convert_element_type.99) | copy-start | bytes 1032196
  2.8 3.0 %copy-start.3 = (f32[8,10752]{1,0:T(8,128)S(1)}, f32[8,10752]{1,0:T(8,128)}, u32[]{:S(2)}) copy-start(f32[8,10752]{1,0:T(8,128)} %param.16) | copy-start | bytes 1032196
  4.3 7.4 %collective-permute-start = (bf16[3,10752]{1,0:T(4,128)(2,1)S(1)}, bf16[3,10752]{1,0:T(4,128)(2,1)S(1)}, u32[]{:S(2)}, u32[]{:S(2)}) collective-permute-start(bf16[3,10752]{1,0:T(4,128)(2,1)S(1)} %pad_maximum_fusion.4), channel_id=1, source_target_pairs={{4,0},{8,4},{12,8},{16,12},{20,16},{24,20},{28,24},{5,1},{9,5},{13... | collective-permute-start | bytes 193544 | tf_op jit(solution)/shard_map/ppermute | solution.py:21
  5.8 1.0 copy-start.4
  6.0 5.8 %copy-start = (s32[8,10752]{1,0:T(8,128)S(1)}, s32[8,10752]{1,0:T(8,128)}, u32[]{:S(2)}) copy-start(s32[8,10752]{1,0:T(8,128)} %param.18) | copy-start | bytes 1032196
  6.0 5.8 %slice-start = ((f32[8,10752]{1,0:T(8,128)}), f32[8,1]{1,0:T(8,128)S(1)}, s32[]{:S(2)}) async-start(f32[8,10752]{1,0:T(8,128)} %copy-done.1), calls=%async_computation | async-start | bytes 8192 | tf_op jit(solution)/shard_map/jit(_roll_static)/slice | solution.py:233
  6.0 5.8 %slice-start.1 = ((f32[8,10752]{1,0:T(8,128)}), f32[8,1]{1,0:T(8,128)S(1)}, s32[]{:S(2)}) async-start(f32[8,10752]{1,0:T(8,128)} %param.16), calls=%async_computation.1 | async-start | bytes 8192 | tf_op jit(solution)/shard_map/jit(_roll_static)/slice | solution.py:235
  6.0 5.8 %copy-start.17 = (f32[2,8,10752]{2,1,0:T(8,128)S(1)}, f32[2,8,10752]{2,1,0:T(8,128)}, u32[]{:S(2)}) copy-start(f32[2,8,10752]{2,1,0:T(8,128)} %param.15) | copy-start | bytes 2064388
  13.0 6.4 %collective-permute-start.1 = (bf16[1,10752]{1,0:T(2,128)(2,1)S(1)}, bf16[1,10752]{1,0:T(2,128)(2,1)S(1)}, u32[]{:S(2)}, u32[]{:S(2)}) collective-permute-start(bf16[1,10752]{1,0:T(2,128)(2,1)S(1)} %slice.440), channel_id=1, source_target_pairs={{0,4},{4,8},{8,12},{12,16},{16,20},{20,24},{24,28},{1,5},{5,9},{9,... | collective-permute-start | bytes 64520 | tf_op jit(solution)/shard_map/ppermute | solution.py:21
  18.3 4.2 %copy-start.22 = (f32[2,8]{1,0:T(2,128)}, f32[2,8]{1,0:T(2,128)S(1)}, u32[]{:S(2)}) copy-start(f32[2,8]{1,0:T(2,128)S(1)} %get-tuple-element.62) | copy-start | bytes 196
  19.5 1.2 copy-start.13
  21.4 12.2 %copy-start.24 = (f32[256]{0:T(256)S(1)}, f32[256]{0:T(256)}, u32[]{:S(2)}) copy-start(f32[256]{0:T(256)} %param.20) | copy-start | bytes 3076
  33.7 19.2 %copy-start.19 = (bf16[2,2,13,128,1]{3,2,1,0,4:T(8,128)(2,1)S(1)}, bf16[2,2,13,128,1]{3,2,1,0,4:T(8,128)(2,1)}, u32[]{:S(2)}) copy-start(bf16[2,2,13,128,1]{3,2,1,0,4:T(8,128)(2,1)} %constant.67) | copy-start | bytes 39940
  53.5 2.4 %copy-start.20 = (f32[2,8]{1,0:T(2,128)S(1)}, f32[2,8]{1,0:T(2,128)}, u32[]{:S(2)}) copy-start(f32[2,8]{1,0:T(2,128)} %get-tuple-element.61) | copy-start | bytes 196
  55.9 1.0 copy-start.7
  55.9 1.1 copy-start.8
  57.0 1.0 copy-start.2
  57.0 2.5 %copy-start.5 = (f32[8,10752]{1,0:T(8,128)S(1)}, f32[8,10752]{1,0:T(8,128)}, u32[]{:S(2)}) copy-start(f32[8,10752]{1,0:T(8,128)} %param.17) | copy-start | bytes 1032196
  57.0 2.5 %copy-start.12 = (f32[8,10752]{1,0:T(8,128)S(1)}, f32[8,10752]{1,0:T(8,128)}, u32[]{:S(2)}) copy-start(f32[8,10752]{1,0:T(8,128)} %get-tuple-element.28) | copy-start | bytes 1032196
  58.2 5.9 %collective-permute-start.2 = (bf16[2,10752]{1,0:T(2,128)(2,1)S(1)}, bf16[2,10752]{1,0:T(2,128)(2,1)S(1)}, u32[]{:S(2)}, u32[]{:S(2)}) collective-permute-start(bf16[2,10752]{1,0:T(2,128)(2,1)S(1)} %pad_maximum_fusion.5), channel_id=1, source_target_pairs={{4,0},{8,4},{12,8},{16,12},{20,16},{24,20},{28,24},{5,1},{9,5},{13... | collective-permute-start | bytes 129032 | tf_op jit(solution)/shard_map/ppermute | solution.py:21
  60.4 3.7 %copy-start.18 = (f32[2,8,10752]{2,1,0:T(8,128)S(1)}, f32[2,8,10752]{2,1,0:T(8,128)}, u32[]{:S(2)}) copy-start(f32[2,8,10752]{2,1,0:T(8,128)} %param.13) | copy-start | bytes 2064388
  65.7 6.3 %collective-permute-start.3 = (bf16[2,10752]{1,0:T(2,128)(2,1)S(1)}, bf16[2,10752]{1,0:T(2,128)(2,1)S(1)}, u32[]{:S(2)}, u32[]{:S(2)}) collective-permute-start(bf16[2,10752]{1,0:T(2,128)(2,1)S(1)} %pad_maximum_fusion.6), channel_id=1, source_target_pairs={{0,4},{4,8},{8,12},{12,16},{16,20},{20,24},{24,28},{1,5},{5,9},{9,... | collective-permute-start | bytes 129032 | tf_op jit(solution)/shard_map/ppermute | solution.py:21
  73.4 1.3 %copy-start.16 = (f32[84,128]{1,0:T(8,128)S(1)}, f32[84,128]{1,0:T(8,128)}, u32[]{:S(2)}) copy-start(f32[84,128]{1,0:T(8,128)} %constant.64) | copy-start | bytes 129028
  74.7 2.9 %copy-start.23 = (f32[2,8]{1,0:T(2,128)S(1)}, f32[2,8]{1,0:T(2,128)}, u32[]{:S(2)}) copy-start(f32[2,8]{1,0:T(2,128)} %copy-done.22) | copy-start | bytes 196
  75.0 13.7 %copy-start.25 = (f32[256]{0:T(256)S(1)}, f32[256]{0:T(256)}, u32[]{:S(2)}) copy-start(f32[256]{0:T(256)} %param.20) | copy-start | bytes 3076
  108.6 3.2 %copy-start.21 = (f32[2,8]{1,0:T(2,128)S(1)}, f32[2,8]{1,0:T(2,128)}, u32[]{:S(2)}) copy-start(f32[2,8]{1,0:T(2,128)} %get-tuple-element.61) | copy-start | bytes 196
  113.0 2.3 %copy-start.6 = (f32[1,8,10752]{2,1,0:T(8,128)S(1)}, f32[1,8,10752]{2,1,0:T(8,128)}, u32[]{:S(2)}) copy-start(f32[1,8,10752]{2,1,0:T(8,128)} %get-tuple-element.44) | copy-start | bytes 1032196
  113.0 2.3 %copy-start.9 = (f32[1,8,10752]{2,1,0:T(8,128)S(1)}, f32[1,8,10752]{2,1,0:T(8,128)}, u32[]{:S(2)}) copy-start(f32[1,8,10752]{2,1,0:T(8,128)} %get-tuple-element.4) | copy-start | bytes 1032196
  113.9 6.1 %copy-start.10 = (f32[8,10752]{1,0:T(8,128)S(1)}, f32[8,10752]{1,0:T(8,128)}, u32[]{:S(2)}) copy-start(f32[8,10752]{1,0:T(8,128)} %get-tuple-element.21) | copy-start | bytes 1032196
  113.9 6.1 %copy-start.11 = (f32[8,10752]{1,0:T(8,128)S(1)}, f32[8,10752]{1,0:T(8,128)}, u32[]{:S(2)}) copy-start(f32[8,10752]{1,0:T(8,128)} %get-tuple-element.40) | copy-start | bytes 1032196
  113.9 6.0 %collective-permute-start.4 = (bf16[1,10752]{1,0:T(2,128)(2,1)S(1)}, bf16[1,10752]{1,0:T(2,128)(2,1)S(1)}, u32[]{:S(2)}, u32[]{:S(2)}) collective-permute-start(bf16[1,10752]{1,0:T(2,128)(2,1)S(1)} %slice.436), channel_id=1, source_target_pairs={{4,0},{8,4},{12,8},{16,12},{20,16},{24,20},{28,24},{5,1},{9,5},{13... | collective-permute-start | bytes 64520 | tf_op jit(solution)/shard_map/ppermute | solution.py:21
  120.4 6.4 %collective-permute-start.5 = (bf16[1,10752]{1,0:T(2,128)(2,1)S(1)}, bf16[1,10752]{1,0:T(2,128)(2,1)S(1)}, u32[]{:S(2)}, u32[]{:S(2)}) collective-permute-start(bf16[1,10752]{1,0:T(2,128)(2,1)S(1)} %slice.435), channel_id=1, source_target_pairs={{0,4},{4,8},{8,12},{12,16},{16,20},{20,24},{24,28},{1,5},{5,9},{9,... | collective-permute-start | bytes 64520 | tf_op jit(solution)/shard_map/ppermute | solution.py:21
  (4 other events, 3.0 us)

commit v3 on v2

--- a/solution.py
+++ b/solution.py
@@ -228,6 +228,12 @@
     north_depth, north_wet, north_flux = edges_from(
         [depth[:1], wet_mask[:1], flux_north[:1]], -1
     )
+    south_flux, south_depth, south_wet, south_drag, south_v, south_va = edges_from(
+        [flux_north[-1:], depth[-1:], wet_mask[-1:], drag[-1:], vel_tl[1, -1:], vel_adj[1, -1:]], 1
+    )
+    south_mask = south_wet * wet_mask[:1]
+    south_height = 0.5 * (south_depth + depth[:1])
+    south_retain = 1.0 - south_drag
     depth_up = northward(depth, north_depth)
     wet_up = northward(wet_mask, north_wet)
     mask_u = wet_mask * jnp.roll(wet_mask, -1, 1)
@@ -246,16 +252,16 @@
     state_eta, state_vel = (eta_tl, vel_tl)
     back_eta, back_vel = (eta_adj, vel_adj)
 
-    def adjoint_terms(eta, vel, flux_edge):
+    def adjoint_terms(eta, vel, flux_edge, flux_below, va_below):
         flux_east = east_factor * wet_mask * eta
         flux_up = kappa_y * wet_mask * eta
         north_up = northward(flux_up, flux_edge)
         p_term = mask_u * (vel[0] + depth_u * (jnp.roll(flux_east, -1, 1) - flux_east))
         q_term = mask_v * (vel[1] + depth_v * (north_up - flux_up))
-        return p_term, q_term
-
-    p_term, q_term = adjoint_terms(back_eta, back_vel, north_flux)
-    (q_edge,) = edges_from([q_term[-1:]], 1)
+        q_below = south_mask * (va_below + south_height * (flux_up[:1] - flux_below))
+        return p_term, q_term, q_below
+
+    p_term, q_term, q_edge = adjoint_terms(back_eta, back_vel, north_flux, south_flux, south_va)
     for step_index in range(STEPS):
         flux_p = east_factor * p_term
         q_down = southward(q_term, q_edge)
@@ -269,10 +275,13 @@
         psi_now = state_eta - loads[0]
         back_eta = back_eta + psi_bar - loads[1]
         back_vel = (retain * p_term, retain * q_term)
-        north_rows = [psi_now[:1]]
+        north_rows, south_rows = [psi_now[:1]], [psi_now[-1:]]
         if not last:
-            north_rows.append(kappa_y * wet_mask[:1] * back_eta[:1])
+            flux_now = kappa_y * wet_mask * back_eta
+            north_rows.append(flux_now[:1])
+            south_rows.append(flux_now[-1:])
         north_edges = edges_from(north_rows, -1)
+        south_edges = edges_from(south_rows, 1)
         psi_up = northward(psi_now, north_edges[0])
         new_u = mask_u * (
             retain * state_vel[0] - east_factor * (jnp.roll(psi_now, -1, 1) - psi_now)
@@ -280,14 +289,13 @@
         new_v = mask_v * (retain * state_vel[1] - kappa_y * (psi_up - psi_now))
         flux_x = depth_u * new_u
         flux_y = depth_v * new_v
-        south_rows = [flux_y[-1:]]
+        south_v = south_mask * (south_retain * south_v - kappa_y * (psi_now[:1] - south_edges[0]))
+        flux_down = southward(flux_y, south_height * south_v)
         if not last:
-            p_term, q_term = adjoint_terms(back_eta, back_vel, north_edges[1])
-            south_rows.append(q_term[-1:])
-        south_edges = edges_from(south_rows, 1)
-        flux_down = southward(flux_y, south_edges[0])
-        if not last:
-            q_edge = south_edges[1]
+            south_va = south_retain * q_edge
+            p_term, q_term, q_edge = adjoint_terms(
+                back_eta, back_vel, north_edges[1], south_edges[1], south_va
+            )
         state_eta = state_eta - wet_mask * (
             east_factor * (flux_x - jnp.roll(flux_x, 1, 1)) + kappa_y * (flux_y - flux_down)
         )

time: 129 us -> 120 us (0.930)
  waiting for transfers between devices: 14.8 us -> 4.24 us
  other arithmetic: 14.7 us -> 19.7 us
  matrix products: 16.9 us -> 13.5 us
  local copies, waits for them, and re-layouts: 18.9 us -> 16.7 us
  Pallas kernels: 42.7 us -> 44 us
    ppermute x6, waiting for transfers between devices: 14.8 us -> 4.24 us  [passed_along(): return lax.ppermute(value, axis, pairs)]
    mul x0 -> x4, other arithmetic: none -> 3.93 us  [the longest x2 3.09 us: on_device(): flux_down = southward(flux_y, south_height * south_v)]
    dot_general x2, matrix products: 2.34 us -> 0.61 us  [synthesise(): jnp.einsum('cka,crkb->rab', outer, turned, preferred_element_type=jnp.flo...]
    reshape x2, local copies, waits for them, and re-layouts: 3.27 us -> 1.9 us  [synthesise(): return grid_out.reshape(2, row_count, -1) * output_weight[:, :, None]]
    pallas_call x4, Pallas kernels: 42.7 us -> 44 us  [exchange(): pl.pallas_call(kernel, out_shape=jax.ShapeDtypeStruct(blocks.shape, block...]
    unnamed x58 -> x86, local copies, waits for them, and re-layouts: 3.51 us -> 3.03 us
  transfers between devices with their start and end apart: 6 -> 6, of which waited for: 6 -> 2; matrix products, arithmetic and copies ran while one was open for 4% -> 8% of each run, Pallas kernels for 0% -> 0%
where the time goes in v3:
time: 120 us; the launch traced here: 118 us
  Pallas kernels  44 us (37%)
  other arithmetic  19.7 us (16%)
  starting transfers between devices  18.7 us (16%)
  local copies, waits for them, and re-layouts  16.7 us (14%)
  matrix products  13.5 us (11%)
  waiting for transfers between devices  4.24 us (4%)
  between operations  1.65 us (1%)
    pallas_call x4, Pallas kernels, exchange(): pl.pallas_call(kernel, out_shape=jax.ShapeDtypeStruct(blocks.shape, block...  44 us
    ppermute x6, starting transfers between devices, passed_along(): return lax.ppermute(value, axis, pairs)  18.7 us
    dot_general x2, matrix products, legendre(): jnp.einsum('cmfl,mil->cmfi', scaled, basis, preferred_element_type=jnp.fl...  10.7 us
    ppermute x6, waiting for transfers between devices, passed_along(): return lax.ppermute(value, axis, pairs)  4.24 us
    mul x2, other arithmetic, on_device(): flux_down = southward(flux_y, south_height * south_v)  3.09 us
    unnamed x86, local copies, waits for them, and re-layouts  3.03 us
    another operation x3, other arithmetic, on_device(): state_vel, back_vel = (jnp.stack(state_vel), jnp.stack(back_vel))  2.65 us
    mul x2, other arithmetic, synthesise(): return grid_out.reshape(2, row_count, -1) * output_weight[:, :, None]  2.49 us
  transfers between devices with their start and end apart: 6, of which 2 were waited for; matrix products, arithmetic and copies ran while one was open for 8% of the time, Pallas kernels for 0%

profile of v3, /device:TPU:0, one launch (start us, length us, event | category | flops | bytes accessed | tf_op | source)
XLA Modules:
  0.0 118.5 jit_solution(2273438449790415581)
XLA Ops:
  0.7 1.1 convert_element_type.101
  1.8 1.3 %multiply_multiply_fusion.3 = (f32[8,10752]{1,0:T(8,128)S(1)}, f32[8,10752]{1,0:T(8,128)S(1)}) fusion(f32[8,10752]{1,0:T(8,128)} %param.14, f32[8]{0:T(128)S(1)} %add_divide_fusion, s32[8,10752]{1,0:T(8,128)} %param.18), kind=kLoop, calls=%fused_computation.129 | loop fusion | flops 430080 | bytes 1376288 | tf_op jit(solution)/shard_map/mul | solution.py:256
  3.5 1.3 %collective-permute-start = (bf16[3,10752]{1,0:T(4,128)(2,1)S(1)}, bf16[3,10752]{1,0:T(4,128)(2,1)S(1)}, u32[]{:S(2)}, u32[]{:S(2)}) collective-permute-start(bf16[3,10752]{1,0:T(4,128)(2,1)S(1)} %pad_maximum_fusion.4), channel_id=1, source_target_pairs={{4,0},{8,4},{12,8},{16,12},{20,16},{24,20},{28,24},{5,1},{9,5},{13... | collective-permute-start | bytes 193544 | tf_op jit(solution)/shard_map/ppermute | solution.py:21
  4.8 1.2 fusion.119
  6.0 1.1 concatenate.86
  7.0 5.5 %collective-permute-start.1 = (bf16[6,10752]{1,0:T(8,128)(2,1)}, bf16[6,10752]{1,0:T(8,128)(2,1)S(1)}, u32[]{:S(2)}, u32[]{:S(2)}) collective-permute-start(bf16[6,10752]{1,0:T(8,128)(2,1)} %concatenate.86), channel_id=1, source_target_pairs={{0,4},{4,8},{8,12},{12,16},{16,20},{20,24},{24,28},{1,5},{5,9},{9,... | collective-permute-start | bytes 387080 | tf_op jit(solution)/shard_map/ppermute | solution.py:21
  14.4 1.3 %broadcast_multiply_fusion.3 = (f32[8,10752]{1,0:T(8,128)S(1)}, f32[8,10752]{1,0:T(8,128)}, f32[8,10752]{1,0:T(8,128)S(1)}, f32[8,10752]{1,0:T(8,128)S(1)}, f32[...) fusion(f32[8]{0:T(128)S(1)} %add_divide_fusion, f32[8,10752]{1,0:T(8,128)S(1)} %get-tuple-element.56, ...), kind=kLoop, calls=%fused_computation.137 | loop fusion | flops 1892352 | bytes 6537248 | tf_op jit(solution)/shard_map/mul | solution.py:266
  17.3 0.9 convert_bitcast_fusion.2
  21.0 11.5 %shard_map.147 = bf16[8,32,128]{2,1,0:T(8,128)(2,1)} custom-call(bf16[8,32,128]{2,1,0:T(8,128)(2,1)} %bitcast.243), custom_call_target="tpu_custom_call" | custom-call | tf_op jit(solution)/shard_map/pallas_call | solution.py:166
  33.6 5.3 %fusion.45 = bf16[2,128,2,64]{3,2,0,1:T(2,128)(2,1)S(1)} fusion(bf16[128,64,256]{2,1,0:T(8,128)(2,1)} %param.19, bf16[2,128,2,64]{3,2,0,1:T(2,128)(2,1)S(1)} %copy.41, f32[256]{0:T(256)S(1)} %copy-done.38), kind=kOutput, calls=%fused_computation.25 | convolution fusion | flops 33849344 | bytes 4326400 | tf_op jit(solution)/shard_map/cmfl,mil->cmfi/dot_general | solution.py:65
  39.7 11.9 %shard_map.148 = bf16[8,32,128]{2,1,0:T(8,128)(2,1)} custom-call(bf16[8,32,128]{2,1,0:T(8,128)(2,1)} %bitcast.245), custom_call_target="tpu_custom_call" | custom-call | tf_op jit(solution)/shard_map/pallas_call | solution.py:166
  51.6 0.9 copy.26
  53.7 1.0 reshape.126
  54.6 1.3 %broadcast_multiply_fusion.1 = f32[2,8,10752]{2,1,0:T(8,128)S(1)} fusion(f32[2,8,10752]{2,1,0:T(8,128)} %reshape.126, f32[2,8]{1,0:T(2,128)S(1)} %copy-done.34), kind=kLoop, calls=%fused_computation.125 | loop fusion | flops 172032 | bytes 1376320 | tf_op jit(solution)/shard_map/mul | solution.py:81
  57.1 1.3 %collective-permute-start.2 = (bf16[2,10752]{1,0:T(2,128)(2,1)S(1)}, bf16[2,10752]{1,0:T(2,128)(2,1)S(1)}, u32[]{:S(2)}, u32[]{:S(2)}) collective-permute-start(bf16[2,10752]{1,0:T(2,128)(2,1)S(1)} %pad_maximum_fusion.5), channel_id=1, source_target_pairs={{4,0},{8,4},{12,8},{16,12},{20,16},{24,20},{28,24},{5,1},{9,5},{13... | collective-permute-start | bytes 129032 | tf_op jit(solution)/shard_map/ppermute | solution.py:21
  58.5 4.7 %collective-permute-start.3 = (bf16[2,10752]{1,0:T(2,128)(2,1)S(1)}, bf16[2,10752]{1,0:T(2,128)(2,1)S(1)}, u32[]{:S(2)}, u32[]{:S(2)}) collective-permute-start(bf16[2,10752]{1,0:T(2,128)(2,1)S(1)} %pad_maximum_fusion.6), channel_id=1, source_target_pairs={{0,4},{4,8},{8,12},{12,16},{16,20},{20,24},{24,28},{1,5},{5,9},{9,... | collective-permute-start | bytes 129032 | tf_op jit(solution)/shard_map/ppermute | solution.py:21
  63.3 0.9 multiply_bitcast_fusion.1
  64.7 1.3 %fusion.141 = (f32[8,10752]{1,0:T(8,128)S(1)}, f32[8,10752]{1,0:T(8,128)}, f32[8,10752]{1,0:T(8,128)S(1)}, f32[8,10752]{1,0:T(8,128)}, f32[1,8,10752]{2,1,0:T(8,...) fusion(f32[8,10752]{1,0:T(8,128)S(1)} %get-tuple-element.35, f32[8,10752]{1,0:T(8,128)S(1)} %get-tuple-element.34, ...), kind=kLoop, calls=%fused_computation.201 | loop fusion | flops 1978368 | bytes 7225376 | tf_op jit(solution)/shard_map/mul | solution.py:290
  66.2 2.0 %fusion.137 = (f32[1,10752]{1,0:T(1,128)S(1)}, f32[1,10752]{1,0:T(1,128)}, f32[1,10752]{1,0:T(1,128)S(1)}) fusion(f32[1,10752]{1,0:T(1,128)S(1)} %copy-done.28, f32[1,10752]{1,0:T(1,128)S(1)} %copy-done.30, f32[2,10752]{1,0:T(2,128)S(1)} %convert_element_type.114, f32[8,10752]{1,0:T(8,128)S(1)} %get-tuple-element.55, f32[6,10752]{1,0:T(8,128)} %copy-done.19, ...), kind=kLoop, calls=%fused_computation.199 | loop fusion | flops 129024 | bytes 516096 | tf_op jit(solution)/shard_map/mul | solution.py:293
  71.4 9.7 %shard_map.149 = bf16[8,32,128]{2,1,0:T(8,128)(2,1)} custom-call(bf16[8,32,128]{2,1,0:T(8,128)(2,1)} %bitcast.248), custom_call_target="tpu_custom_call" | custom-call | tf_op jit(solution)/shard_map/pallas_call | solution.py:166
  82.1 5.3 %fusion.40 = bf16[2,128,2,64]{3,2,0,1:T(2,128)(2,1)S(1)} fusion(bf16[128,64,256]{2,1,0:T(8,128)(2,1)} %param.19, bf16[2,128,2,64]{3,2,0,1:T(2,128)(2,1)S(1)} %copy.49, f32[256]{0:T(256)S(1)} %copy-done.39), kind=kOutput, calls=%fused_computation.24 | convolution fusion | flops 33849344 | bytes 4326400 | tf_op jit(solution)/shard_map/cmfl,mil->cmfi/dot_general | solution.py:65
  88.2 10.9 %shard_map.150 = bf16[8,32,128]{2,1,0:T(8,128)(2,1)} custom-call(bf16[8,32,128]{2,1,0:T(8,128)(2,1)} %bitcast.250), custom_call_target="tpu_custom_call" | custom-call | tf_op jit(solution)/shard_map/pallas_call | solution.py:166
  99.1 0.9 copy.34
  101.2 1.0 reshape.135
  102.1 1.2 %broadcast_multiply_fusion = f32[2,8,10752]{2,1,0:T(8,128)S(1)} fusion(f32[2,8,10752]{2,1,0:T(8,128)} %reshape.135, f32[2,8]{1,0:T(2,128)S(1)} %copy-done.35), kind=kLoop, calls=%fused_computation.124 | loop fusion | flops 172032 | bytes 1376320 | tf_op jit(solution)/shard_map/mul | solution.py:81
  104.3 4.7 %collective-permute-start.5 = (bf16[1,10752]{1,0:T(2,128)(2,1)S(1)}, bf16[1,10752]{1,0:T(2,128)(2,1)S(1)}, u32[]{:S(2)}, u32[]{:S(2)}) collective-permute-start(bf16[1,10752]{1,0:T(2,128)(2,1)S(1)} %get-tuple-element.59), channel_id=1, source_target_pairs={{0,4},{4,8},{8,12},{12,16},{16,20},{20,24},{24,28},{1,5},{5,9},{9,... | collective-permute-start | bytes 64520 | tf_op jit(solution)/shard_map/ppermute | solution.py:21
  109.0 1.3 %collective-permute-start.4 = (bf16[1,10752]{1,0:T(2,128)(2,1)S(1)}, bf16[1,10752]{1,0:T(2,128)(2,1)S(1)}, u32[]{:S(2)}, u32[]{:S(2)}) collective-permute-start(bf16[1,10752]{1,0:T(2,128)(2,1)S(1)} %get-tuple-element.60), channel_id=1, source_target_pairs={{4,0},{8,4},{12,8},{16,12},{20,16},{24,20},{28,24},{5,1},{9,5},{13... | collective-permute-start | bytes 64520 | tf_op jit(solution)/shard_map/ppermute | solution.py:21
  110.3 0.9 pad_maximum_fusion.1
  111.4 3.6 %collective-permute-done.4 = bf16[1,10752]{1,0:T(2,128)(2,1)S(1)} collective-permute-done((bf16[1,10752]{1,0:T(2,128)(2,1)S(1)}, bf16[1,10752]{1,0:T(2,128)(2,1)S(1)}, u32[]{:S(2)}, u32[]{:S(2)}) %collective-permute-start.4) | collective-permute-done | bytes 21536 | tf_op jit(solution)/shard_map/ppermute | solution.py:21
  115.4 0.9 pad_maximum_fusion
  116.4 1.1 multiply_multiply_fusion.4
  117.5 0.9 fusion.101
  (179 shorter events, 18.9 us)
Async XLA Ops:
  0.6 2.5 %copy-start.3 = (f32[8,10752]{1,0:T(8,128)S(1)}, f32[8,10752]{1,0:T(8,128)}, u32[]{:S(2)}) copy-start(f32[8,10752]{1,0:T(8,128)} %param.16) | copy-start | bytes 1032196
  0.6 4.1 %copy-start.4 = (f32[8,10752]{1,0:T(8,128)S(1)}, f32[8,10752]{1,0:T(8,128)}, u32[]{:S(2)}) copy-start(f32[8,10752]{1,0:T(8,128)} %param.17) | copy-start | bytes 1032196
  1.8 10.8 %copy-start.1 = (f32[8,10752]{1,0:T(8,128)}, f32[8,10752]{1,0:T(8,128)S(1)}, u32[]{:S(2)}) copy-start(f32[8,10752]{1,0:T(8,128)S(1)} %convert_element_type.101) | copy-start | bytes 1032196
  3.5 10.9 %collective-permute-start = (bf16[3,10752]{1,0:T(4,128)(2,1)S(1)}, bf16[3,10752]{1,0:T(4,128)(2,1)S(1)}, u32[]{:S(2)}, u32[]{:S(2)}) collective-permute-start(bf16[3,10752]{1,0:T(4,128)(2,1)S(1)} %pad_maximum_fusion.4), channel_id=1, source_target_pairs={{4,0},{8,4},{12,8},{16,12},{20,16},{24,20},{28,24},{5,1},{9,5},{13... | collective-permute-start | bytes 193544 | tf_op jit(solution)/shard_map/ppermute | solution.py:21
  7.0 9.4 %collective-permute-start.1 = (bf16[6,10752]{1,0:T(8,128)(2,1)}, bf16[6,10752]{1,0:T(8,128)(2,1)S(1)}, u32[]{:S(2)}, u32[]{:S(2)}) collective-permute-start(bf16[6,10752]{1,0:T(8,128)(2,1)} %concatenate.86), channel_id=1, source_target_pairs={{0,4},{4,8},{8,12},{12,16},{16,20},{20,24},{24,28},{1,5},{5,9},{9,... | collective-permute-start | bytes 387080 | tf_op jit(solution)/shard_map/ppermute | solution.py:21
  12.8 1.6 %copy-start = (s32[8,10752]{1,0:T(8,128)S(1)}, s32[8,10752]{1,0:T(8,128)}, u32[]{:S(2)}) copy-start(s32[8,10752]{1,0:T(8,128)} %param.18) | copy-start | bytes 1032196
  12.8 1.6 %slice-start = ((f32[8,10752]{1,0:T(8,128)}), f32[8,1]{1,0:T(8,128)S(1)}, s32[]{:S(2)}) async-start(f32[8,10752]{1,0:T(8,128)} %copy-done.1), calls=%async_computation | async-start | bytes 8192 | tf_op jit(solution)/shard_map/jit(_roll_static)/slice | solution.py:239
  12.9 1.6 %slice-start.1 = ((f32[8,10752]{1,0:T(8,128)}), f32[8,1]{1,0:T(8,128)S(1)}, s32[]{:S(2)}) async-start(f32[8,10752]{1,0:T(8,128)} %param.16), calls=%async_computation.1 | async-start | bytes 8192 | tf_op jit(solution)/shard_map/jit(_roll_static)/slice | solution.py:241
  12.9 1.6 %copy-start.20 = (f32[2,8,10752]{2,1,0:T(8,128)S(1)}, f32[2,8,10752]{2,1,0:T(8,128)}, u32[]{:S(2)}) copy-start(f32[2,8,10752]{2,1,0:T(8,128)} %param.15) | copy-start | bytes 2064388
  14.3 6.0 %copy-start.36 = (f32[2,8]{1,0:T(2,128)}, f32[2,8]{1,0:T(2,128)S(1)}, u32[]{:S(2)}) copy-start(f32[2,8]{1,0:T(2,128)S(1)} %get-tuple-element.78) | copy-start | bytes 196
  14.4 2.0 %copy-start.2 = (f32[8,10752]{1,0:T(8,128)S(1)}, f32[8,10752]{1,0:T(8,128)}, u32[]{:S(2)}) copy-start(f32[8,10752]{1,0:T(8,128)} %copy-done.1) | copy-start | bytes 1032196
  16.5 1.7 %copy-start.19 = (f32[6,10752]{1,0:T(8,128)}, f32[6,10752]{1,0:T(8,128)S(1)}, u32[]{:S(2)}) copy-start(f32[6,10752]{1,0:T(8,128)S(1)} %convert_element_type.104) | copy-start | bytes 774148
  19.2 14.3 %copy-start.38 = (f32[256]{0:T(256)S(1)}, f32[256]{0:T(256)}, u32[]{:S(2)}) copy-start(f32[256]{0:T(256)} %param.20) | copy-start | bytes 3076
  33.5 19.2 %copy-start.33 = (bf16[2,2,13,128,1]{3,2,1,0,4:T(8,128)(2,1)S(1)}, bf16[2,2,13,128,1]{3,2,1,0,4:T(8,128)(2,1)}, u32[]{:S(2)}) copy-start(bf16[2,2,13,128,1]{3,2,1,0,4:T(8,128)(2,1)} %constant.69) | copy-start | bytes 39940
  56.3 7.0 %copy-start.18 = (f32[8,10752]{1,0:T(8,128)S(1)}, f32[8,10752]{1,0:T(8,128)}, u32[]{:S(2)}) copy-start(f32[8,10752]{1,0:T(8,128)} %get-tuple-element.33) | copy-start | bytes 1032196
  57.1 7.1 %collective-permute-start.2 = (bf16[2,10752]{1,0:T(2,128)(2,1)S(1)}, bf16[2,10752]{1,0:T(2,128)(2,1)S(1)}, u32[]{:S(2)}, u32[]{:S(2)}) collective-permute-start(bf16[2,10752]{1,0:T(2,128)(2,1)S(1)} %pad_maximum_fusion.5), channel_id=1, source_target_pairs={{4,0},{8,4},{12,8},{16,12},{20,16},{24,20},{28,24},{5,1},{9,5},{13... | collective-permute-start | bytes 129032 | tf_op jit(solution)/shard_map/ppermute | solution.py:21
  58.5 7.7 %collective-permute-start.3 = (bf16[2,10752]{1,0:T(2,128)(2,1)S(1)}, bf16[2,10752]{1,0:T(2,128)(2,1)S(1)}, u32[]{:S(2)}, u32[]{:S(2)}) collective-permute-start(bf16[2,10752]{1,0:T(2,128)(2,1)S(1)} %pad_maximum_fusion.6), channel_id=1, source_target_pairs={{0,4},{4,8},{8,12},{12,16},{16,20},{20,24},{24,28},{1,5},{5,9},{9,... | collective-permute-start | bytes 129032 | tf_op jit(solution)/shard_map/ppermute | solution.py:21
  63.3 1.4 %copy-start.21 = (f32[2,8,10752]{2,1,0:T(8,128)S(1)}, f32[2,8,10752]{2,1,0:T(8,128)}, u32[]{:S(2)}) copy-start(f32[2,8,10752]{2,1,0:T(8,128)} %param.13) | copy-start | bytes 2064388
  64.7 1.5 %copy-start.27 = (f32[1,10752]{1,0:T(1,128)S(1)}, f32[1,10752]{1,0:T(1,128)}, u32[]{:S(2)}) copy-start(f32[1,10752]{1,0:T(1,128)} %copy-done.26) | copy-start | bytes 129028
  64.7 1.5 %copy-start.28 = (f32[1,10752]{1,0:T(1,128)S(1)}, f32[1,10752]{1,0:T(1,128)}, u32[]{:S(2)}) copy-start(f32[1,10752]{1,0:T(1,128)} %get-tuple-element.27) | copy-start | bytes 129028
  64.7 1.5 %copy-start.30 = (f32[1,10752]{1,0:T(1,128)S(1)}, f32[1,10752]{1,0:T(1,128)}, u32[]{:S(2)}) copy-start(f32[1,10752]{1,0:T(1,128)} %get-tuple-element.28) | copy-start | bytes 129028
  69.6 12.5 %copy-start.39 = (f32[256]{0:T(256)S(1)}, f32[256]{0:T(256)}, u32[]{:S(2)}) copy-start(f32[256]{0:T(256)} %param.20) | copy-start | bytes 3076
  101.2 2.2 %copy-start.7 = (f32[8,10752]{1,0:T(8,128)S(1)}, f32[8,10752]{1,0:T(8,128)}, u32[]{:S(2)}) copy-start(f32[8,10752]{1,0:T(8,128)} %copy-done.6) | copy-start | bytes 1032196
  103.3 6.9 %copy-start.12 = (f32[1,8,10752]{2,1,0:T(8,128)S(1)}, f32[1,8,10752]{2,1,0:T(8,128)}, u32[]{:S(2)}) copy-start(f32[1,8,10752]{2,1,0:T(8,128)} %get-tuple-element.49) | copy-start | bytes 1032196
  103.3 6.9 %copy-start.15 = (f32[1,8,10752]{2,1,0:T(8,128)S(1)}, f32[1,8,10752]{2,1,0:T(8,128)}, u32[]{:S(2)}) copy-start(f32[1,8,10752]{2,1,0:T(8,128)} %get-tuple-element.4) | copy-start | bytes 1032196
  104.2 10.8 %copy-start.9 = (f32[8,10752]{1,0:T(8,128)S(1)}, f32[8,10752]{1,0:T(8,128)}, u32[]{:S(2)}) copy-start(f32[8,10752]{1,0:T(8,128)} %get-tuple-element.47) | copy-start | bytes 1032196
  104.2 10.8 %copy-start.11 = (f32[8,10752]{1,0:T(8,128)S(1)}, f32[8,10752]{1,0:T(8,128)}, u32[]{:S(2)}) copy-start(f32[8,10752]{1,0:T(8,128)} %get-tuple-element.48) | copy-start | bytes 1032196
  104.3 10.8 %copy-start.16 = (f32[8,10752]{1,0:T(8,128)S(1)}, f32[8,10752]{1,0:T(8,128)}, u32[]{:S(2)}) copy-start(f32[8,10752]{1,0:T(8,128)} %get-tuple-element.23) | copy-start | bytes 1032196
  104.3 10.8 %copy-start.17 = (f32[8,10752]{1,0:T(8,128)S(1)}, f32[8,10752]{1,0:T(8,128)}, u32[]{:S(2)}) copy-start(f32[8,10752]{1,0:T(8,128)} %get-tuple-element.45) | copy-start | bytes 1032196
  104.3 12.1 %collective-permute-start.5 = (bf16[1,10752]{1,0:T(2,128)(2,1)S(1)}, bf16[1,10752]{1,0:T(2,128)(2,1)S(1)}, u32[]{:S(2)}, u32[]{:S(2)}) collective-permute-start(bf16[1,10752]{1,0:T(2,128)(2,1)S(1)} %get-tuple-element.59), channel_id=1, source_target_pairs={{0,4},{4,8},{8,12},{12,16},{16,20},{20,24},{24,28},{1,5},{5,9},{9,... | collective-permute-start | bytes 64520 | tf_op jit(solution)/shard_map/ppermute | solution.py:21
  109.0 6.0 %collective-permute-start.4 = (bf16[1,10752]{1,0:T(2,128)(2,1)S(1)}, bf16[1,10752]{1,0:T(2,128)(2,1)S(1)}, u32[]{:S(2)}, u32[]{:S(2)}) collective-permute-start(bf16[1,10752]{1,0:T(2,128)(2,1)S(1)} %get-tuple-element.60), channel_id=1, source_target_pairs={{4,0},{8,4},{12,8},{16,12},{20,16},{24,20},{28,24},{5,1},{9,5},{13... | collective-permute-start | bytes 64520 | tf_op jit(solution)/shard_map/ppermute | solution.py:21
  115.1 1.3 %copy-start.29 = (f32[1,10752]{1,0:T(1,128)S(1)}, f32[1,10752]{1,0:T(1,128)}, u32[]{:S(2)}) copy-start(f32[1,10752]{1,0:T(1,128)} %get-tuple-element.27) | copy-start | bytes 129028
  (18 other events, 18.8 us)

commit v4 on v3

--- a/solution.py
+++ b/solution.py
@@ -9,6 +9,7 @@
 
 STEPS = 2
 LANES = 128
+GROUP = 32
 
 
 kappa_x = 0.3
@@ -57,12 +58,6 @@
     spectra = jnp.einsum("crkb,dcnb->drnk", turned, second, preferred_element_type=jnp.float32)
     spectra = spectra.reshape(2, 2, row_count, -1)[..., :order_count] * (1.0 / lon_count)
     return (spectra * analysis_weight[None, :, :, None]).astype(jnp.bfloat16)
-
-
-def legendre(spectra, basis, love):
-    coeffs = jnp.einsum("cmfi,mil->cmfl", spectra, basis, preferred_element_type=jnp.float32)
-    scaled = (coeffs * love[None, None, None, :]).astype(jnp.bfloat16)
-    return jnp.einsum("cmfl,mil->cmfi", scaled, basis, preferred_element_type=jnp.float32)
 
 
 def synthesise(coeffs, factors, tables, output_weight):
@@ -107,53 +102,109 @@
     return lambda: lax.fori_loop(1, count, finish, 0)
 
 
-def spread_kernel(lat_count, send_ref, out_ref, held, send_sem, recv_sem):
-    me_lat, me_deg = lax.axis_index("lat"), lax.axis_index("deg")
-
-    def device_of(step):
-        return (lax.rem(me_lat + step, lat_count), me_deg)
-
-    def copy_of(step):
-        peer = device_of(step)
-        return pltpu.make_async_remote_copy(
-            src_ref=send_ref.at[peer[0]],
-            dst_ref=held.at[me_lat],
-            send_sem=send_sem.at[step - 1],
-            recv_sem=recv_sem.at[step - 1],
-            device_id=peer,
-            device_id_type=pl.DeviceIdType.MESH,
-        )
-
-    greet(lat_count, device_of)
-    finish = swap(lat_count, copy_of)
-    held[me_lat] = send_ref[me_lat]
-    finish()
-    out_ref[...] = held[...]
-
-
-def gather_kernel(lat_count, deg_count, send_ref, out_ref, held, send_sem, recv_sem):
+def load_kernel(
+    sizes, send_ref, basis_ref, love_ref, out_ref, basis, landed, ready, held,
+    basis_sem, spread_out, spread_in, gather_out, gather_in,
+):
+    lat_count, deg_count, row_count, halves, cluster = sizes
+    tall = 4 * cluster
     count = lat_count * deg_count
+    total_rows = lat_count * row_count
     me_lat, me_deg = lax.axis_index("lat"), lax.axis_index("deg")
     me = me_lat * deg_count + me_deg
+
+    def band_of(step):
+        return (lax.rem(me_lat + step, lat_count), me_deg)
 
     def device_of(step):
         peer = lax.rem(me + step, count)
         return (lax.div(peer, deg_count), lax.rem(peer, deg_count))
 
-    def copy_of(step):
+    def spread_copy(step):
+        peer = band_of(step)
+        return pltpu.make_async_remote_copy(
+            src_ref=send_ref.at[peer[0]],
+            dst_ref=landed.at[me_lat],
+            send_sem=spread_out.at[step - 1],
+            recv_sem=spread_in.at[step - 1],
+            device_id=peer,
+            device_id_type=pl.DeviceIdType.MESH,
+        )
+
+    def gather_copy(step):
         peer = device_of(step)
         return pltpu.make_async_remote_copy(
-            src_ref=send_ref.at[peer[0]],
+            src_ref=ready.at[peer[0]],
             dst_ref=held.at[me],
-            send_sem=send_sem.at[step - 1],
-            recv_sem=recv_sem.at[step - 1],
+            send_sem=gather_out.at[step - 1],
+            recv_sem=gather_in.at[step - 1],
             device_id=peer,
             device_id_type=pl.DeviceIdType.MESH,
         )
 
+    fetch = pltpu.make_async_copy(basis_ref, basis, basis_sem)
+    fetch.start()
     greet(count, device_of)
-    finish = swap(count, copy_of)
-    held[me] = send_ref[me_lat]
+    finish = swap(lat_count, spread_copy)
+    landed[me_lat] = send_ref[me_lat]
+    finish()
+    fetch.wait()
+
+    copies = max(1, LANES // total_rows)
+    width = copies * total_rows
+    row_order = lax.broadcasted_iota(jnp.int32, (tall, width), 0) % cluster
+    lane_part = lax.broadcasted_iota(jnp.int32, (tall, width), 1) // total_rows
+    chunk = min(cluster, max(copies, 2048 // total_rows))
+    blocks = [landed[source].astype(jnp.float32) for source in range(lat_count)]
+    groups = blocks[0].shape[1] // tall
+    love = love_ref[...]
+    done = []
+    for half in range(halves):
+        for group in range(groups):
+            first = (half * groups + group) * cluster
+            lanes = slice(group * tall, (group + 1) * tall)
+            rows = slice(half * row_count, (half + 1) * row_count)
+            tile = jnp.concatenate([block[rows, lanes] for block in blocks], 0).T
+            tile = jnp.concatenate([tile] * copies, 1)
+            masks = [row_order == order + lane_part for order in range(0, cluster, copies)]
+            total = jnp.zeros((tall, love.shape[1]), jnp.float32)
+            for start in range(0, cluster, chunk):
+                spaced = jnp.concatenate(
+                    [
+                        jnp.where(masks[order // copies], tile, 0.0).astype(jnp.bfloat16)
+                        for order in range(start, start + chunk, copies)
+                    ],
+                    1,
+                )
+                part = basis[first + start : first + start + chunk]
+                part = part.reshape(chunk * total_rows, love.shape[1])
+                total = total + jnp.dot(spaced, part, preferred_element_type=jnp.float32)
+            scaled = (total * love).astype(jnp.bfloat16)
+            merged = jnp.zeros((tall, width), jnp.float32)
+            for start in range(0, cluster, chunk):
+                part = basis[first + start : first + start + chunk]
+                part = part.reshape(chunk * total_rows, love.shape[1])
+                wide = lax.dot_general(
+                    scaled, part, (((1,), (1,)), ((), ())), preferred_element_type=jnp.float32
+                )
+                for step in range(chunk // copies):
+                    mask = masks[start // copies + step]
+                    merged = merged + jnp.where(
+                        mask, wide[:, step * width : (step + 1) * width], 0.0
+                    )
+            summed = merged[:, :total_rows]
+            for copy in range(1, copies):
+                summed = summed + merged[:, copy * total_rows : (copy + 1) * total_rows]
+            done.append(summed.T)
+    for band in range(lat_count):
+        rows = slice(band * row_count, (band + 1) * row_count)
+        lines = [
+            jnp.concatenate([done[half * groups + g][rows] for g in range(groups)], 1)
+            for half in range(halves)
+        ]
+        ready[band] = jnp.concatenate(lines, 0).astype(jnp.bfloat16)
+    finish = swap(count, gather_copy)
+    held[me] = ready[me_lat]
     finish()
     for source in range(lat_count):
         total = held[source * deg_count].astype(jnp.float32)
@@ -162,40 +213,39 @@
         out_ref[source] = total.astype(out_ref.dtype)
 
 
-def exchange(kernel, count, peers, blocks, collective_id):
-    return pl.pallas_call(
-        kernel,
-        out_shape=jax.ShapeDtypeStruct(blocks.shape, blocks.dtype),
-        in_specs=[pl.BlockSpec(memory_space=pltpu.VMEM)],
-        out_specs=pl.BlockSpec(memory_space=pltpu.VMEM),
-        scratch_shapes=[
-            pltpu.VMEM((count,) + blocks.shape[1:], blocks.dtype),
-            pltpu.SemaphoreType.DMA((peers - 1,)),
-            pltpu.SemaphoreType.DMA((peers - 1,)),
-        ],
-        compiler_params=pltpu.CompilerParams(collective_id=collective_id, has_side_effects=True),
-    )(blocks)
-
-
-def spread_orders(spectra, lat_count):
+def load_spectra(spectra, basis, love, lat_count, deg_count):
     row_count, order_total = spectra.shape[2:]
     owned = order_total // lat_count
-    blocks = spectra.reshape(4 * row_count, lat_count, owned).transpose(1, 0, 2)
-    kernel = functools.partial(spread_kernel, lat_count)
-    got = exchange(kernel, lat_count, lat_count, blocks, 0)
-    got = got.reshape(lat_count, 2, 2, row_count, owned).transpose(1, 4, 2, 0, 3)
-    return got.reshape(2, owned, 2, lat_count * row_count)
-
-
-def gather_rows(partial_value, lat_count, deg_count):
-    owned, total_rows = partial_value.shape[1], partial_value.shape[3]
-    row_count = total_rows // lat_count
-    blocks = partial_value.reshape(2, owned, 2, lat_count, row_count).transpose(3, 0, 2, 4, 1)
-    blocks = blocks.reshape(lat_count, 4 * row_count, owned)
-    kernel = functools.partial(gather_kernel, lat_count, deg_count)
+    halves = max(1, 16 // row_count)
+    cluster = min(GROUP, owned // halves)
+    groups = owned // (halves * cluster)
+    split = spectra.reshape(2, 2, row_count, lat_count, halves, groups, cluster)
+    blocks = split.transpose(3, 4, 2, 5, 0, 1, 6)
+    blocks = blocks.reshape(lat_count, halves * row_count, groups * 4 * cluster)
     count = lat_count * deg_count
-    got = exchange(kernel, count, count, blocks, 1)
-    return got.transpose(1, 0, 2).reshape(2, 2, row_count, lat_count * owned)
+    vmem = pl.BlockSpec(memory_space=pltpu.VMEM)
+    got = pl.pallas_call(
+        functools.partial(load_kernel, (lat_count, deg_count, row_count, halves, cluster)),
+        out_shape=jax.ShapeDtypeStruct(blocks.shape, blocks.dtype),
+        in_specs=[vmem, pl.BlockSpec(memory_space=pl.ANY), vmem],
+        out_specs=vmem,
+        scratch_shapes=[
+            pltpu.VMEM(basis.shape, basis.dtype),
+            pltpu.VMEM(blocks.shape, blocks.dtype),
+            pltpu.VMEM(blocks.shape, blocks.dtype),
+            pltpu.VMEM((count,) + blocks.shape[1:], blocks.dtype),
+            pltpu.SemaphoreType.DMA,
+            pltpu.SemaphoreType.DMA((lat_count - 1,)),
+            pltpu.SemaphoreType.DMA((lat_count - 1,)),
+            pltpu.SemaphoreType.DMA((count - 1,)),
+            pltpu.SemaphoreType.DMA((count - 1,)),
+        ],
+        compiler_params=pltpu.CompilerParams(
+            collective_id=0, has_side_effects=True, vmem_limit_bytes=40 * 2**20
+        ),
+    )(blocks, basis, love[None, :])
+    got = got.reshape(lat_count, halves, row_count, groups, 2, 2, cluster)
+    return got.transpose(4, 5, 2, 0, 1, 3, 6).reshape(spectra.shape)
 
 
 def edges_from(rows, by):
@@ -267,9 +317,7 @@
         q_down = southward(q_term, q_edge)
         psi_bar = flux_p - jnp.roll(flux_p, 1, 1) + kappa_y * (q_term - q_down)
         spectra = analyse(jnp.stack([state_eta, psi_bar]), analysis_weight, tables, order_total)
-        owned_rows = spread_orders(spectra, lat_count)
-        partial_value = legendre(owned_rows, basis, love).astype(jnp.bfloat16)
-        banded = gather_rows(partial_value, lat_count, lax.axis_size("deg"))
+        banded = load_spectra(spectra, basis, love, lat_count, lax.axis_size("deg"))
         loads = synthesise(banded, full_factor, tables, output_weight)
         last = step_index == STEPS - 1
         psi_now = state_eta - loads[0]

time: 120 us -> 105 us (0.88)
  matrix products: 13.5 us -> 3.62 us
  Pallas kernels: 44 us -> 38.5 us
  starting transfers between devices: 18.7 us -> 20.2 us
    dot_general x2 -> x0, matrix products: 10.7 us -> none  [legendre(): jnp.einsum('cmfl,mil->cmfi', scaled, basis, preferred_element_type=jnp.fl...]
    pallas_call x4 -> x2, Pallas kernels: 44 us -> 38.5 us  [load_spectra(): pl.pallas_call(functools.partial(load_kernel, (lat_count, deg_count, row_...]
    unnamed x86 -> x78, local copies, waits for them, and re-layouts: 3.03 us -> 7.32 us
    transpose x4 -> x2, local copies, waits for them, and re-layouts: 3.03 us -> 0.82 us  [load_spectra(): blocks = split.transpose(3, 4, 2, 5, 0, 1, 6)]
    ppermute x6, starting transfers between devices: 18.7 us -> 20.2 us  [passed_along(): return lax.ppermute(value, axis, pairs)]
    reshape x8 -> x10, local copies, waits for them, and re-layouts: 3.3 us -> 2.02 us  [the longest x4 0.73 us: load_spectra(): got = got.reshape(lat_count, halves, row_count, groups, 2, 2, cluster)]
where the time goes in v4:
time: 105 us
  Pallas kernels  38.5 us (37%)
  starting transfers between devices  20.2 us (19%)
  other arithmetic  18.7 us (18%)
  local copies, waits for them, and re-layouts  17.8 us (17%)
  waiting for transfers between devices  4.08 us (4%)
  matrix products  3.62 us (3%)
  between operations  1.65 us (2%)
    pallas_call x2, Pallas kernels, load_spectra(): pl.pallas_call(functools.partial(load_kernel, (lat_count, deg_count, row_...  38.5 us
    ppermute x6, starting transfers between devices, passed_along(): return lax.ppermute(value, axis, pairs)  20.2 us
    unnamed x78, local copies, waits for them, and re-layouts  7.32 us
    ppermute x6, waiting for transfers between devices, passed_along(): return lax.ppermute(value, axis, pairs)  4.08 us
    reshape x2, local copies, waits for them, and re-layouts, synthesise(): return grid_out.reshape(2, row_count, -1) * output_weight[:, :, None]  3.08 us
    another operation x3, other arithmetic, on_device(): state_vel, back_vel = (jnp.stack(state_vel), jnp.stack(back_vel))  2.66 us
    mul x2, other arithmetic, synthesise(): return grid_out.reshape(2, row_count, -1) * output_weight[:, :, None]  2.52 us
    mul x2, other arithmetic, on_device(): flux_down = southward(flux_y, south_height * south_v)  2.48 us
  transfers between devices with their start and end apart: 6, of which 2 were waited for; matrix products, arithmetic and copies ran while one was open for 8% of the time, Pallas kernels for 0%

profile of v4, /device:TPU:0, one launch (start us, length us, event | category | flops | bytes accessed | tf_op | source)
XLA Modules:
  0.0 104.5 jit_solution(881203236700184641)
XLA Ops:
  0.7 1.1 %convert_element_type.77 = f32[8,10752]{1,0:T(8,128)S(1)} convert(s32[8,10752]{1,0:T(8,128)} %param.18) | non-fusion elementwise | flops 86016 | bytes 688128 | tf_op jit(solution)/shard_map/convert_element_type | solution.py:276
  1.8 1.3 %multiply_multiply_fusion.3 = (f32[8,10752]{1,0:T(8,128)S(1)}, f32[8,10752]{1,0:T(8,128)S(1)}) fusion(f32[8,10752]{1,0:T(8,128)} %param.14, f32[8]{0:T(128)S(1)} %add_divide_fusion, s32[8,10752]{1,0:T(8,128)} %param.18), kind=kLoop, calls=%fused_computation.111 | loop fusion | flops 430080 | bytes 1376288 | tf_op jit(solution)/shard_map/mul | solution.py:306
  3.5 1.3 %collective-permute-start = (bf16[3,10752]{1,0:T(4,128)(2,1)S(1)}, bf16[3,10752]{1,0:T(4,128)(2,1)S(1)}, u32[]{:S(2)}, u32[]{:S(2)}) collective-permute-start(bf16[3,10752]{1,0:T(4,128)(2,1)S(1)} %pad_maximum_fusion.4), channel_id=1, source_target_pairs={{4,0},{8,4},{12,8},{16,12},{20,16},{24,20},{28,24},{5,1},{9,5},{13... | collective-permute-start | bytes 193544 | tf_op jit(solution)/shard_map/ppermute | solution.py:22
  4.8 1.2 %fusion.67 = (bf16[1,10752]{1,0:T(2,128)(2,1)S(1)}, bf16[1,10752]{1,0:T(2,128)(2,1)S(1)}) fusion(f32[2,8,10752]{2,1,0:T(8,128)} %param.15, f32[2,8,10752]{2,1,0:T(8,128)} %param.13), kind=kLoop, calls=%fused_computation.145 | loop fusion | bytes 86016 | tf_op jit(solution)/shard_map/squeeze | solution.py:282
  6.4 5.5 %collective-permute-start.1 = (bf16[6,10752]{1,0:T(8,128)(2,1)S(1)}, bf16[6,10752]{1,0:T(8,128)(2,1)S(1)}, u32[]{:S(2)}, u32[]{:S(2)}) collective-permute-start(bf16[6,10752]{1,0:T(8,128)(2,1)S(1)} %concatenate.86), channel_id=1, source_target_pairs={{0,4},{4,8},{8,12},{12,16},{16,20},{20,24},{24,28},{1,5},{5,9},{9,... | collective-permute-start | bytes 387080 | tf_op jit(solution)/shard_map/ppermute | solution.py:22
  12.6 0.5 copy-done.8
  13.5 1.3 %broadcast_multiply_fusion.3 = (f32[8,10752]{1,0:T(8,128)S(1)}, f32[8,10752]{1,0:T(8,128)}, f32[8,10752]{1,0:T(8,128)S(1)}, f32[8,10752]{1,0:T(8,128)S(1)}, f32[...) fusion(f32[8]{0:T(128)S(1)} %add_divide_fusion, f32[8,10752]{1,0:T(8,128)S(1)} %get-tuple-element.56, ...), kind=kLoop, calls=%fused_computation.119 | loop fusion | flops 1892352 | bytes 6537248 | tf_op jit(solution)/shard_map/mul | solution.py:316
  14.9 0.6 collective-permute-done.1
  15.8 0.9 convert_bitcast_fusion.2
  19.6 2.2 %copy-done = bf16[128,64,256]{2,1,0:T(8,128)(2,1)S(1)} copy-done((bf16[128,64,256]{2,1,0:T(8,128)(2,1)S(1)}, bf16[128,64,256]{2,1,0:T(8,128)(2,1)}, u32[]{:S(2)}) %copy-start) | copy-done | bytes 4194328
  21.8 20.4 %shard_map.147 = bf16[8,16,256]{2,1,0:T(8,128)(2,1)S(1)} custom-call(bf16[8,16,256]{2,1,0:T(8,128)(2,1)S(1)} %reshape.107.send_ref, bf16[128,64,256]{2,1,0:T(8,128)(2,1)S(1)} %copy-done, f32[1,256]{1,0:T(1,128)S(1)} %bitcast.138), custom_call_target="tpu_custom_call" | custom-call | tf_op jit(solution)/shard_map/pallas_call | solution.py:227
  43.8 1.2 %convolution_bitcast_fusion.5 = f32[16,84,128]{2,1,0:T(8,128)} fusion(bf16[2,84,84,1]{2,1,0,3:T(8,128)(2,1)S(1)} %copy-done.28, bf16[1,16,84,128]{3,2,0,1:T(8,128)(2,1)S(1)} %get-tuple-element.41, bf16[1,16,84,128]{3,2,0,1:T(8,128)(2,1)S(1)} %get-tuple-element.40), kind=kOutput, calls=%fused_computation.5 | convolution fusion | flops 58146816 | bytes 1404480 | tf_op jit(solution)/shard_map/cka,crkb->rab/dot_general | solution.py:75
  45.0 2.1 %reshape.111 = f32[2,8,10752]{2,1,0:T(8,128)} reshape(f32[16,84,128]{2,1,0:T(8,128)} %convolution_bitcast_fusion.5) | data formatting | bytes 1376256 | tf_op jit(solution)/shard_map/reshape | solution.py:76
  47.1 1.3 %broadcast_multiply_fusion.1 = f32[2,8,10752]{2,1,0:T(8,128)S(1)} fusion(f32[2,8,10752]{2,1,0:T(8,128)} %reshape.111, f32[2,8]{1,0:T(2,128)S(1)} %get-tuple-element.77), kind=kLoop, calls=%fused_computation.107 | loop fusion | flops 172032 | bytes 1376320 | tf_op jit(solution)/shard_map/mul | solution.py:76
  49.6 1.3 %collective-permute-start.2 = (bf16[2,10752]{1,0:T(2,128)(2,1)S(1)}, bf16[2,10752]{1,0:T(2,128)(2,1)S(1)}, u32[]{:S(2)}, u32[]{:S(2)}) collective-permute-start(bf16[2,10752]{1,0:T(2,128)(2,1)S(1)} %pad_maximum_fusion.5), channel_id=1, source_target_pairs={{4,0},{8,4},{12,8},{16,12},{20,16},{24,20},{28,24},{5,1},{9,5},{13... | collective-permute-start | bytes 129032 | tf_op jit(solution)/shard_map/ppermute | solution.py:22
  51.0 5.8 %collective-permute-start.3 = (bf16[2,10752]{1,0:T(2,128)(2,1)S(1)}, bf16[2,10752]{1,0:T(2,128)(2,1)S(1)}, u32[]{:S(2)}, u32[]{:S(2)}) collective-permute-start(bf16[2,10752]{1,0:T(2,128)(2,1)S(1)} %pad_maximum_fusion.6), channel_id=1, source_target_pairs={{0,4},{4,8},{8,12},{12,16},{16,20},{20,24},{24,28},{1,5},{5,9},{9,... | collective-permute-start | bytes 129032 | tf_op jit(solution)/shard_map/ppermute | solution.py:22
  56.8 0.8 multiply_bitcast_fusion.1
  58.2 1.3 %fusion.89 = (f32[8,10752]{1,0:T(8,128)S(1)}, f32[8,10752]{1,0:T(8,128)}, f32[8,10752]{1,0:T(8,128)S(1)}, f32[8,10752]{1,0:T(8,128)}, f32[1,8,10752]{2,1,0:T(8,1...) fusion(f32[8,10752]{1,0:T(8,128)S(1)} %get-tuple-element.35, f32[8,10752]{1,0:T(8,128)S(1)} %get-tuple-element.34, ...), kind=kLoop, calls=%fused_computation.179 | loop fusion | flops 1978368 | bytes 7225376 | tf_op jit(solution)/shard_map/mul | solution.py:338
  59.7 1.3 %fusion.85 = (f32[1,10752]{1,0:T(1,128)S(1)}, f32[1,10752]{1,0:T(1,128)S(1)}, f32[1,10752]{1,0:T(1,128)S(1)}) fusion(f32[1,10752]{1,0:T(1,128)S(1)} %get-tuple-element.27, f32[1,10752]{1,0:T(1,128)S(1)} %get-tuple-element.28, f32[2,10752]{1,0:T(2,128)S(1)} %convert_element_type.86, f32[8,10752]{1,0:T(8,128)S(1)} %get-tuple-element.55, ...), kind=kLoop, calls=%fused_computation.177 | loop fusion | flops 129024 | bytes 516096 | tf_op jit(solution)/shard_map/mul | solution.py:341
  61.2 0.9 convert_bitcast_fusion
  64.8 2.2 %copy-done.1 = bf16[128,64,256]{2,1,0:T(8,128)(2,1)S(1)} copy-done((bf16[128,64,256]{2,1,0:T(8,128)(2,1)S(1)}, bf16[128,64,256]{2,1,0:T(8,128)(2,1)}, u32[]{:S(2)}) %copy-start.1) | copy-done | bytes 4194328
  67.0 18.1 %shard_map.148 = bf16[8,16,256]{2,1,0:T(8,128)(2,1)S(1)} custom-call(bf16[8,16,256]{2,1,0:T(8,128)(2,1)S(1)} %reshape.114.send_ref, bf16[128,64,256]{2,1,0:T(8,128)(2,1)S(1)} %copy-done.1, f32[1,256]{1,0:T(1,128)S(1)} %bitcast.139), custom_call_target="tpu_custom_call" | custom-call | tf_op jit(solution)/shard_map/pallas_call | solution.py:227
  86.9 1.0 reshape.118
  87.8 1.3 %broadcast_multiply_fusion = f32[2,8,10752]{2,1,0:T(8,128)S(1)} fusion(f32[2,8,10752]{2,1,0:T(8,128)} %reshape.118, f32[2,8]{1,0:T(2,128)S(1)} %copy-done.34), kind=kLoop, calls=%fused_computation.106 | loop fusion | flops 172032 | bytes 1376320 | tf_op jit(solution)/shard_map/mul | solution.py:76
  89.1 0.9 fusion.12
  90.1 5.1 %collective-permute-start.5 = (bf16[1,10752]{1,0:T(2,128)(2,1)S(1)}, bf16[1,10752]{1,0:T(2,128)(2,1)S(1)}, u32[]{:S(2)}, u32[]{:S(2)}) collective-permute-start(bf16[1,10752]{1,0:T(2,128)(2,1)S(1)} %get-tuple-element.59), channel_id=1, source_target_pairs={{0,4},{4,8},{8,12},{12,16},{16,20},{20,24},{24,28},{1,5},{5,9},{9,... | collective-permute-start | bytes 64520 | tf_op jit(solution)/shard_map/ppermute | solution.py:22
  95.2 1.3 %collective-permute-start.4 = (bf16[1,10752]{1,0:T(2,128)(2,1)S(1)}, bf16[1,10752]{1,0:T(2,128)(2,1)S(1)}, u32[]{:S(2)}, u32[]{:S(2)}) collective-permute-start(bf16[1,10752]{1,0:T(2,128)(2,1)S(1)} %get-tuple-element.60), channel_id=1, source_target_pairs={{4,0},{8,4},{12,8},{16,12},{20,16},{24,20},{28,24},{5,1},{9,5},{13... | collective-permute-start | bytes 64520 | tf_op jit(solution)/shard_map/ppermute | solution.py:22
  96.5 0.9 pad_maximum_fusion.1
  97.6 3.5 %collective-permute-done.4 = bf16[1,10752]{1,0:T(2,128)(2,1)S(1)} collective-permute-done((bf16[1,10752]{1,0:T(2,128)(2,1)S(1)}, bf16[1,10752]{1,0:T(2,128)(2,1)S(1)}, u32[]{:S(2)}, u32[]{:S(2)}) %collective-permute-start.4) | collective-permute-done | bytes 21536 | tf_op jit(solution)/shard_map/ppermute | solution.py:22
  101.5 0.9 pad_maximum_fusion
  102.5 1.1 %multiply_multiply_fusion.4 = f32[1,10752]{1,0:T(1,128)S(1)} fusion(f32[1,10752]{1,0:T(1,128)S(1)} %get-tuple-element.27, f32[1,10752]{1,0:T(1,128)S(1)} %get-tuple-element.28, bf16[1,10752]{1,0:T(2,128)(2,1)S(1)} %collective-permute-done.5, f32[1,10752]{1,0:T(1,128)S(1)} %get-tuple-element.19, f32[8,10752]{1,0:T(8,128)S(1)} %get-tuple-element.52, ...), kind=kLoop, calls=%fused_computation.154 | loop fusion | flops 86016 | bytes 279552 | tf_op jit(solution)/shard_map/mul | solution.py:341
  103.6 0.9 fusion.51
  (165 shorter events, 13.7 us)
Async XLA Ops:
  0.6 2.5 %copy-start.6 = (f32[8,10752]{1,0:T(8,128)S(1)}, f32[8,10752]{1,0:T(8,128)}, u32[]{:S(2)}) copy-start(f32[8,10752]{1,0:T(8,128)} %param.16) | copy-start | bytes 1032196
  0.6 4.1 %copy-start.7 = (f32[8,10752]{1,0:T(8,128)S(1)}, f32[8,10752]{1,0:T(8,128)}, u32[]{:S(2)}) copy-start(f32[8,10752]{1,0:T(8,128)} %param.17) | copy-start | bytes 1032196
  1.8 10.2 %copy-start.4 = (f32[8,10752]{1,0:T(8,128)}, f32[8,10752]{1,0:T(8,128)S(1)}, u32[]{:S(2)}) copy-start(f32[8,10752]{1,0:T(8,128)S(1)} %convert_element_type.77) | copy-start | bytes 1032196
  3.5 9.8 %collective-permute-start = (bf16[3,10752]{1,0:T(4,128)(2,1)S(1)}, bf16[3,10752]{1,0:T(4,128)(2,1)S(1)}, u32[]{:S(2)}, u32[]{:S(2)}) collective-permute-start(bf16[3,10752]{1,0:T(4,128)(2,1)S(1)} %pad_maximum_fusion.4), channel_id=1, source_target_pairs={{4,0},{8,4},{12,8},{16,12},{20,16},{24,20},{28,24},{5,1},{9,5},{13... | collective-permute-start | bytes 193544 | tf_op jit(solution)/shard_map/ppermute | solution.py:22
  6.4 9.1 %collective-permute-start.1 = (bf16[6,10752]{1,0:T(8,128)(2,1)S(1)}, bf16[6,10752]{1,0:T(8,128)(2,1)S(1)}, u32[]{:S(2)}, u32[]{:S(2)}) collective-permute-start(bf16[6,10752]{1,0:T(8,128)(2,1)S(1)} %concatenate.86), channel_id=1, source_target_pairs={{0,4},{4,8},{8,12},{12,16},{16,20},{20,24},{24,28},{1,5},{5,9},{9,... | collective-permute-start | bytes 387080 | tf_op jit(solution)/shard_map/ppermute | solution.py:22
  12.3 1.3 %copy-start.26 = (f32[2,8,10752]{2,1,0:T(8,128)S(1)}, f32[2,8,10752]{2,1,0:T(8,128)}, u32[]{:S(2)}) copy-start(f32[2,8,10752]{2,1,0:T(8,128)} %param.15) | copy-start | bytes 2064388
  13.2 5.5 %copy-start.35 = (f32[2,8]{1,0:T(2,128)}, f32[2,8]{1,0:T(2,128)S(1)}, u32[]{:S(2)}) copy-start(f32[2,8]{1,0:T(2,128)S(1)} %get-tuple-element.78) | copy-start | bytes 196
  13.2 33.9 %copy-start.33 = (f32[2,8]{1,0:T(2,128)}, f32[2,8]{1,0:T(2,128)S(1)}, u32[]{:S(2)}) copy-start(f32[2,8]{1,0:T(2,128)S(1)} %get-tuple-element.77) | copy-start | bytes 196
  13.5 2.0 %copy-start.5 = (f32[8,10752]{1,0:T(8,128)S(1)}, f32[8,10752]{1,0:T(8,128)}, u32[]{:S(2)}) copy-start(f32[8,10752]{1,0:T(8,128)} %copy-done.4) | copy-start | bytes 1032196
  18.2 1.4 %copy-start.2 = (f32[256]{0:T(256)S(1)}, f32[256]{0:T(256)}, u32[]{:S(2)}) copy-start(f32[256]{0:T(256)} %param.20) | copy-start | bytes 3076
  19.6 2.2 %copy-start = (bf16[128,64,256]{2,1,0:T(8,128)(2,1)S(1)}, bf16[128,64,256]{2,1,0:T(8,128)(2,1)}, u32[]{:S(2)}) copy-start(bf16[128,64,256]{2,1,0:T(8,128)(2,1)} %basis_ref.3) | copy-start | bytes 12582916
  44.9 3.4 %copy-start.9 = (f32[8,10752]{1,0:T(8,128)S(1)}, f32[8,10752]{1,0:T(8,128)}, u32[]{:S(2)}) copy-start(f32[8,10752]{1,0:T(8,128)} %param.12) | copy-start | bytes 1032196
  45.0 3.4 %copy-start.18 = (f32[8,10752]{1,0:T(8,128)S(1)}, f32[8,10752]{1,0:T(8,128)}, u32[]{:S(2)}) copy-start(f32[8,10752]{1,0:T(8,128)} %param.14) | copy-start | bytes 1032196
  47.1 1.3 %copy-start.20 = (f32[8,10752]{1,0:T(8,128)S(1)}, f32[8,10752]{1,0:T(8,128)}, u32[]{:S(2)}) copy-start(f32[8,10752]{1,0:T(8,128)} %get-tuple-element.25) | copy-start | bytes 1032196
  48.7 8.0 %copy-start.24 = (f32[8,10752]{1,0:T(8,128)S(1)}, f32[8,10752]{1,0:T(8,128)}, u32[]{:S(2)}) copy-start(f32[8,10752]{1,0:T(8,128)} %get-tuple-element.33) | copy-start | bytes 1032196
  49.6 8.1 %collective-permute-start.2 = (bf16[2,10752]{1,0:T(2,128)(2,1)S(1)}, bf16[2,10752]{1,0:T(2,128)(2,1)S(1)}, u32[]{:S(2)}, u32[]{:S(2)}) collective-permute-start(bf16[2,10752]{1,0:T(2,128)(2,1)S(1)} %pad_maximum_fusion.5), channel_id=1, source_target_pairs={{4,0},{8,4},{12,8},{16,12},{20,16},{24,20},{28,24},{5,1},{9,5},{13... | collective-permute-start | bytes 129032 | tf_op jit(solution)/shard_map/ppermute | solution.py:22
  51.0 8.7 %collective-permute-start.3 = (bf16[2,10752]{1,0:T(2,128)(2,1)S(1)}, bf16[2,10752]{1,0:T(2,128)(2,1)S(1)}, u32[]{:S(2)}, u32[]{:S(2)}) collective-permute-start(bf16[2,10752]{1,0:T(2,128)(2,1)S(1)} %pad_maximum_fusion.6), channel_id=1, source_target_pairs={{0,4},{4,8},{8,12},{12,16},{16,20},{20,24},{24,28},{1,5},{5,9},{9,... | collective-permute-start | bytes 129032 | tf_op jit(solution)/shard_map/ppermute | solution.py:22
  56.8 1.4 %copy-start.27 = (f32[2,8,10752]{2,1,0:T(8,128)S(1)}, f32[2,8,10752]{2,1,0:T(8,128)}, u32[]{:S(2)}) copy-start(f32[2,8,10752]{2,1,0:T(8,128)} %param.13) | copy-start | bytes 2064388
  58.2 2.8 %copy-start.10 = (f32[8,10752]{1,0:T(8,128)S(1)}, f32[8,10752]{1,0:T(8,128)}, u32[]{:S(2)}) copy-start(f32[8,10752]{1,0:T(8,128)} %param.12) | copy-start | bytes 1032196
  62.7 1.2 %copy-start.36 = (f32[2,8]{1,0:T(2,128)S(1)}, f32[2,8]{1,0:T(2,128)}, u32[]{:S(2)}) copy-start(f32[2,8]{1,0:T(2,128)} %copy-done.35) | copy-start | bytes 196
  64.8 2.2 %copy-start.1 = (bf16[128,64,256]{2,1,0:T(8,128)(2,1)S(1)}, bf16[128,64,256]{2,1,0:T(8,128)(2,1)}, u32[]{:S(2)}) copy-start(bf16[128,64,256]{2,1,0:T(8,128)(2,1)} %basis_ref.3) | copy-start | bytes 12582916
  86.6 1.3 %copy-start.34 = (f32[2,8]{1,0:T(2,128)S(1)}, f32[2,8]{1,0:T(2,128)}, u32[]{:S(2)}) copy-start(f32[2,8]{1,0:T(2,128)} %copy-done.33) | copy-start | bytes 196
  86.9 2.3 %copy-start.12 = (f32[8,10752]{1,0:T(8,128)S(1)}, f32[8,10752]{1,0:T(8,128)}, u32[]{:S(2)}) copy-start(f32[8,10752]{1,0:T(8,128)} %copy-done.11) | copy-start | bytes 1032196
  87.8 1.3 %copy-start.19 = (f32[8,10752]{1,0:T(8,128)S(1)}, f32[8,10752]{1,0:T(8,128)}, u32[]{:S(2)}) copy-start(f32[8,10752]{1,0:T(8,128)} %get-tuple-element.15) | copy-start | bytes 1032196
  89.1 7.4 %copy-start.17 = (f32[1,8,10752]{2,1,0:T(8,128)S(1)}, f32[1,8,10752]{2,1,0:T(8,128)}, u32[]{:S(2)}) copy-start(f32[1,8,10752]{2,1,0:T(8,128)} %get-tuple-element.49) | copy-start | bytes 1032196
  89.1 7.4 %copy-start.21 = (f32[1,8,10752]{2,1,0:T(8,128)S(1)}, f32[1,8,10752]{2,1,0:T(8,128)}, u32[]{:S(2)}) copy-start(f32[1,8,10752]{2,1,0:T(8,128)} %get-tuple-element.4) | copy-start | bytes 1032196
  90.1 11.1 %copy-start.14 = (f32[8,10752]{1,0:T(8,128)S(1)}, f32[8,10752]{1,0:T(8,128)}, u32[]{:S(2)}) copy-start(f32[8,10752]{1,0:T(8,128)} %get-tuple-element.47) | copy-start | bytes 1032196
  90.1 11.1 %copy-start.16 = (f32[8,10752]{1,0:T(8,128)S(1)}, f32[8,10752]{1,0:T(8,128)}, u32[]{:S(2)}) copy-start(f32[8,10752]{1,0:T(8,128)} %get-tuple-element.48) | copy-start | bytes 1032196
  90.1 11.1 %copy-start.22 = (f32[8,10752]{1,0:T(8,128)S(1)}, f32[8,10752]{1,0:T(8,128)}, u32[]{:S(2)}) copy-start(f32[8,10752]{1,0:T(8,128)} %get-tuple-element.23) | copy-start | bytes 1032196
  90.1 11.1 %copy-start.23 = (f32[8,10752]{1,0:T(8,128)S(1)}, f32[8,10752]{1,0:T(8,128)}, u32[]{:S(2)}) copy-start(f32[8,10752]{1,0:T(8,128)} %get-tuple-element.45) | copy-start | bytes 1032196
  90.1 12.4 %collective-permute-start.5 = (bf16[1,10752]{1,0:T(2,128)(2,1)S(1)}, bf16[1,10752]{1,0:T(2,128)(2,1)S(1)}, u32[]{:S(2)}, u32[]{:S(2)}) collective-permute-start(bf16[1,10752]{1,0:T(2,128)(2,1)S(1)} %get-tuple-element.59), channel_id=1, source_target_pairs={{0,4},{4,8},{8,12},{12,16},{16,20},{20,24},{24,28},{1,5},{5,9},{9,... | collective-permute-start | bytes 64520 | tf_op jit(solution)/shard_map/ppermute | solution.py:22
  95.2 5.9 %collective-permute-start.4 = (bf16[1,10752]{1,0:T(2,128)(2,1)S(1)}, bf16[1,10752]{1,0:T(2,128)(2,1)S(1)}, u32[]{:S(2)}, u32[]{:S(2)}) collective-permute-start(bf16[1,10752]{1,0:T(2,128)(2,1)S(1)} %get-tuple-element.60), channel_id=1, source_target_pairs={{4,0},{8,4},{12,8},{16,12},{20,16},{24,20},{28,24},{5,1},{9,5},{13... | collective-permute-start | bytes 64520 | tf_op jit(solution)/shard_map/ppermute | solution.py:22
  (15 other events, 14.4 us)

commit v5 on v4

--- a/solution.py
+++ b/solution.py
@@ -241,7 +241,7 @@
             pltpu.SemaphoreType.DMA((count - 1,)),
         ],
         compiler_params=pltpu.CompilerParams(
-            collective_id=0, has_side_effects=True, vmem_limit_bytes=40 * 2**20
+            collective_id=0, has_side_effects=True, vmem_limit_bytes=56 * 2**20
         ),
     )(blocks, basis, love[None, :])
     got = got.reshape(lat_count, halves, row_count, groups, 2, 2, cluster)

time: 105 us -> 106 us (level)
  Pallas kernels: 38.5 us -> 40.4 us
  local copies, waits for them, and re-layouts: 17.8 us -> 16 us
  other arithmetic: 18.7 us -> 19.8 us
    unnamed x78 -> x80, local copies, waits for them, and re-layouts: 7.32 us -> 3.01 us
    pallas_call x2, Pallas kernels: 38.5 us -> 40.4 us  [load_spectra(): pl.pallas_call(functools.partial(load_kernel, (lat_count, deg_count, row_...]
    reshape x4, local copies, waits for them, and re-layouts: 0.73 us -> 2.5 us  [load_spectra(): got = got.reshape(lat_count, halves, row_count, groups, 2, 2, cluster)]
    reshape x2, local copies, waits for them, and re-layouts: 0.36 us -> 1.68 us  [load_spectra(): blocks = blocks.reshape(lat_count, halves * row_count, groups * 4 * cluster)]
    reshape x2, local copies, waits for them, and re-layouts: 3.08 us -> 1.9 us  [synthesise(): return grid_out.reshape(2, row_count, -1) * output_weight[:, :, None]]
  transfers between devices with their start and end apart: 6 -> 6, of which waited for: 2 -> 2; matrix products, arithmetic and copies ran while one was open for 8% -> 9% of each run, Pallas kernels for 0% -> 0%
where the time goes in v5:
time: 106 us; the launch traced here: 105 us
  Pallas kernels  40.4 us (38%)
  starting transfers between devices  20.2 us (19%)
  other arithmetic  19.8 us (19%)
  local copies, waits for them, and re-layouts  16 us (15%)
  waiting for transfers between devices  4.07 us (4%)
  matrix products  2.78 us (3%)
  between operations  1.6 us (2%)
    pallas_call x2, Pallas kernels, load_spectra(): pl.pallas_call(functools.partial(load_kernel, (lat_count, deg_count, row_...  40.4 us
    ppermute x6, starting transfers between devices, passed_along(): return lax.ppermute(value, axis, pairs)  20.2 us
    ppermute x6, waiting for transfers between devices, passed_along(): return lax.ppermute(value, axis, pairs)  4.07 us
    mul x2, other arithmetic, on_device(): flux_down = southward(flux_y, south_height * south_v)  3.1 us
    unnamed x80, local copies, waits for them, and re-layouts  3.01 us
    another operation x3, other arithmetic, on_device(): state_vel, back_vel = (jnp.stack(state_vel), jnp.stack(back_vel))  2.65 us
    reshape x4, local copies, waits for them, and re-layouts, load_spectra(): got = got.reshape(lat_count, halves, row_count, groups, 2, 2, cluster)  2.5 us
    mul x2, other arithmetic, synthesise(): return grid_out.reshape(2, row_count, -1) * output_weight[:, :, None]  2.49 us
  transfers between devices with their start and end apart: 6, of which 2 were waited for; matrix products, arithmetic and copies ran while one was open for 9% of the time, Pallas kernels for 0%

profile of v5, /device:TPU:0, one launch (start us, length us, event | category | flops | bytes accessed | tf_op | source)
XLA Modules:
  0.0 104.8 jit_solution(3555866948514367051)
XLA Ops:
  0.7 1.1 %convert_element_type.77 = f32[8,10752]{1,0:T(8,128)S(1)} convert(s32[8,10752]{1,0:T(8,128)} %param.18) | non-fusion elementwise | flops 86016 | bytes 688128 | tf_op jit(solution)/shard_map/convert_element_type | solution.py:276
  1.8 1.3 %multiply_multiply_fusion.3 = (f32[8,10752]{1,0:T(8,128)S(1)}, f32[8,10752]{1,0:T(8,128)S(1)}) fusion(f32[8,10752]{1,0:T(8,128)} %param.14, f32[8]{0:T(128)S(1)} %add_divide_fusion, s32[8,10752]{1,0:T(8,128)} %param.18), kind=kLoop, calls=%fused_computation.111 | loop fusion | flops 430080 | bytes 1376288 | tf_op jit(solution)/shard_map/mul | solution.py:306
  3.5 1.3 %collective-permute-start = (bf16[3,10752]{1,0:T(4,128)(2,1)S(1)}, bf16[3,10752]{1,0:T(4,128)(2,1)S(1)}, u32[]{:S(2)}, u32[]{:S(2)}) collective-permute-start(bf16[3,10752]{1,0:T(4,128)(2,1)S(1)} %pad_maximum_fusion.4), channel_id=1, source_target_pairs={{4,0},{8,4},{12,8},{16,12},{20,16},{24,20},{28,24},{5,1},{9,5},{13... | collective-permute-start | bytes 193544 | tf_op jit(solution)/shard_map/ppermute | solution.py:22
  4.8 1.2 %fusion.67 = (bf16[1,10752]{1,0:T(2,128)(2,1)S(1)}, bf16[1,10752]{1,0:T(2,128)(2,1)S(1)}) fusion(f32[2,8,10752]{2,1,0:T(8,128)} %param.15, f32[2,8,10752]{2,1,0:T(8,128)} %param.13), kind=kLoop, calls=%fused_computation.145 | loop fusion | bytes 86016 | tf_op jit(solution)/shard_map/squeeze | solution.py:282
  6.0 1.1 %concatenate.86 = bf16[6,10752]{1,0:T(8,128)(2,1)} concatenate(bf16[1,10752]{1,0:T(2,128)(2,1)S(1)} %get-tuple-element.69, bf16[1,10752]{1,0:T(2,128)(2,1)S(1)} %get-tuple-element.80, bf16[1,10752]{1,0:T(2,128)(2,1)S(1)} %get-tuple-element.65, bf16[1,10752]{1,0:T(2,128)(2,1)S(1)} %slice.550, bf16[1,10752]{1,0:T(2,128)(2,1)S(1)} %get-tuple-element.82, ...), dimensions={0} | concatenate | bytes 258048 | tf_op jit(solution)/shard_map/concatenate | solution.py:252
  7.0 5.5 %collective-permute-start.1 = (bf16[6,10752]{1,0:T(8,128)(2,1)}, bf16[6,10752]{1,0:T(8,128)(2,1)S(1)}, u32[]{:S(2)}, u32[]{:S(2)}) collective-permute-start(bf16[6,10752]{1,0:T(8,128)(2,1)} %concatenate.86), channel_id=1, source_target_pairs={{0,4},{4,8},{8,12},{12,16},{16,20},{20,24},{24,28},{1,5},{5,9},{9,... | collective-permute-start | bytes 387080 | tf_op jit(solution)/shard_map/ppermute | solution.py:22
  14.5 1.3 %broadcast_multiply_fusion.3 = (f32[8,10752]{1,0:T(8,128)S(1)}, f32[8,10752]{1,0:T(8,128)}, f32[8,10752]{1,0:T(8,128)S(1)}, f32[8,10752]{1,0:T(8,128)S(1)}, f32[...) fusion(f32[8]{0:T(128)S(1)} %add_divide_fusion, f32[8,10752]{1,0:T(8,128)S(1)} %get-tuple-element.56, ...), kind=kLoop, calls=%fused_computation.119 | loop fusion | flops 1892352 | bytes 6537248 | tf_op jit(solution)/shard_map/mul | solution.py:316
  16.5 0.8 fusion.69
  17.3 0.9 convert_bitcast_fusion.2
  21.0 0.8 reshape.107.send_ref
  21.8 21.4 %shard_map.147 = bf16[8,16,256]{2,1,0:T(8,128)(2,1)} custom-call(bf16[8,16,256]{2,1,0:T(8,128)(2,1)} %reshape.107.send_ref, bf16[128,64,256]{2,1,0:T(8,128)(2,1)} %basis_ref.3, f32[1,256]{1,0:T(1,128)} %bitcast.152), custom_call_target="tpu_custom_call" | custom-call | tf_op jit(solution)/shard_map/pallas_call | solution.py:227
  43.2 1.0 %reshape.108 = bf16[8,2,8,2,2,2,32]{6,5,4,3,2,1,0:T(2,128)(2,1)S(1)} reshape(bf16[8,16,256]{2,1,0:T(8,128)(2,1)} %shard_map.147) | data formatting | bytes 131072 | tf_op jit(solution)/shard_map/reshape | solution.py:247
  45.9 1.0 reshape.111
  46.9 1.3 %broadcast_multiply_fusion.1 = f32[2,8,10752]{2,1,0:T(8,128)S(1)} fusion(f32[2,8,10752]{2,1,0:T(8,128)} %reshape.111, f32[2,8]{1,0:T(2,128)S(1)} %copy-done.34), kind=kLoop, calls=%fused_computation.107 | loop fusion | flops 172032 | bytes 1376320 | tf_op jit(solution)/shard_map/mul | solution.py:76
  49.3 1.3 %collective-permute-start.2 = (bf16[2,10752]{1,0:T(2,128)(2,1)S(1)}, bf16[2,10752]{1,0:T(2,128)(2,1)S(1)}, u32[]{:S(2)}, u32[]{:S(2)}) collective-permute-start(bf16[2,10752]{1,0:T(2,128)(2,1)S(1)} %pad_maximum_fusion.5), channel_id=1, source_target_pairs={{4,0},{8,4},{12,8},{16,12},{20,16},{24,20},{28,24},{5,1},{9,5},{13... | collective-permute-start | bytes 129032 | tf_op jit(solution)/shard_map/ppermute | solution.py:22
  50.7 5.8 %collective-permute-start.3 = (bf16[2,10752]{1,0:T(2,128)(2,1)S(1)}, bf16[2,10752]{1,0:T(2,128)(2,1)S(1)}, u32[]{:S(2)}, u32[]{:S(2)}) collective-permute-start(bf16[2,10752]{1,0:T(2,128)(2,1)S(1)} %pad_maximum_fusion.6), channel_id=1, source_target_pairs={{0,4},{4,8},{8,12},{12,16},{16,20},{20,24},{24,28},{1,5},{5,9},{9,... | collective-permute-start | bytes 129032 | tf_op jit(solution)/shard_map/ppermute | solution.py:22
  56.5 0.9 multiply_bitcast_fusion.1
  58.0 1.3 %fusion.89 = (f32[8,10752]{1,0:T(8,128)S(1)}, f32[8,10752]{1,0:T(8,128)}, f32[8,10752]{1,0:T(8,128)S(1)}, f32[8,10752]{1,0:T(8,128)}, f32[1,8,10752]{2,1,0:T(8,1...) fusion(f32[8,10752]{1,0:T(8,128)S(1)} %get-tuple-element.35, f32[8,10752]{1,0:T(8,128)S(1)} %get-tuple-element.34, ...), kind=kLoop, calls=%fused_computation.179 | loop fusion | flops 1978368 | bytes 7225376 | tf_op jit(solution)/shard_map/mul | solution.py:338
  59.5 2.0 %fusion.85 = (f32[1,10752]{1,0:T(1,128)S(1)}, f32[1,10752]{1,0:T(1,128)}, f32[1,10752]{1,0:T(1,128)S(1)}) fusion(f32[1,10752]{1,0:T(1,128)S(1)} %copy-done.28, f32[1,10752]{1,0:T(1,128)S(1)} %copy-done.30, f32[2,10752]{1,0:T(2,128)S(1)} %convert_element_type.86, f32[8,10752]{1,0:T(8,128)S(1)} %get-tuple-element.55, f32[6,10752]{1,0:T(8,128)} %copy-done.19, ...), kind=kLoop, calls=%fused_computation.177 | loop fusion | flops 129024 | bytes 516096 | tf_op jit(solution)/shard_map/mul | solution.py:341
  64.6 0.8 reshape.114.send_ref
  65.5 19.0 %shard_map.148 = bf16[8,16,256]{2,1,0:T(8,128)(2,1)} custom-call(bf16[8,16,256]{2,1,0:T(8,128)(2,1)} %reshape.114.send_ref, bf16[128,64,256]{2,1,0:T(8,128)(2,1)} %basis_ref.3, f32[1,256]{1,0:T(1,128)} %bitcast.153), custom_call_target="tpu_custom_call" | custom-call | tf_op jit(solution)/shard_map/pallas_call | solution.py:227
  84.5 1.0 reshape.115
  87.2 1.0 reshape.118
  88.1 1.2 %broadcast_multiply_fusion = f32[2,8,10752]{2,1,0:T(8,128)S(1)} fusion(f32[2,8,10752]{2,1,0:T(8,128)} %reshape.118, f32[2,8]{1,0:T(2,128)S(1)} %copy-done.35), kind=kLoop, calls=%fused_computation.106 | loop fusion | flops 172032 | bytes 1376320 | tf_op jit(solution)/shard_map/mul | solution.py:76
  89.4 0.8 fusion.12
  90.3 5.1 %collective-permute-start.5 = (bf16[1,10752]{1,0:T(2,128)(2,1)S(1)}, bf16[1,10752]{1,0:T(2,128)(2,1)S(1)}, u32[]{:S(2)}, u32[]{:S(2)}) collective-permute-start(bf16[1,10752]{1,0:T(2,128)(2,1)S(1)} %get-tuple-element.59), channel_id=1, source_target_pairs={{0,4},{4,8},{8,12},{12,16},{16,20},{20,24},{24,28},{1,5},{5,9},{9,... | collective-permute-start | bytes 64520 | tf_op jit(solution)/shard_map/ppermute | solution.py:22
  95.4 1.3 %collective-permute-start.4 = (bf16[1,10752]{1,0:T(2,128)(2,1)S(1)}, bf16[1,10752]{1,0:T(2,128)(2,1)S(1)}, u32[]{:S(2)}, u32[]{:S(2)}) collective-permute-start(bf16[1,10752]{1,0:T(2,128)(2,1)S(1)} %get-tuple-element.60), channel_id=1, source_target_pairs={{4,0},{8,4},{12,8},{16,12},{20,16},{24,20},{28,24},{5,1},{9,5},{13... | collective-permute-start | bytes 64520 | tf_op jit(solution)/shard_map/ppermute | solution.py:22
  96.7 0.9 pad_maximum_fusion.1
  97.8 3.5 %collective-permute-done.4 = bf16[1,10752]{1,0:T(2,128)(2,1)S(1)} collective-permute-done((bf16[1,10752]{1,0:T(2,128)(2,1)S(1)}, bf16[1,10752]{1,0:T(2,128)(2,1)S(1)}, u32[]{:S(2)}, u32[]{:S(2)}) %collective-permute-start.4) | collective-permute-done | bytes 21536 | tf_op jit(solution)/shard_map/ppermute | solution.py:22
  101.7 0.9 pad_maximum_fusion
  102.7 1.1 %multiply_multiply_fusion.4 = f32[1,10752]{1,0:T(1,128)S(1)} fusion(f32[1,10752]{1,0:T(1,128)S(1)} %copy-done.29, f32[1,10752]{1,0:T(1,128)S(1)} %copy-done.31, bf16[1,10752]{1,0:T(2,128)(2,1)S(1)} %collective-permute-done.5, f32[1,10752]{1,0:T(1,128)S(1)} %copy-done.32, f32[8,10752]{1,0:T(8,128)S(1)} %get-tuple-element.52, f32[6,10752]{1,0:T(8,128)} %copy-done.19), kind=kLoop, calls=%fused_computation.154 | loop fusion | flops 86016 | bytes 279552 | tf_op jit(solution)/shard_map/mul | solution.py:341
  103.9 0.9 fusion.51
  (167 shorter events, 14.6 us)
Async XLA Ops:
  0.6 2.5 %copy-start.3 = (f32[8,10752]{1,0:T(8,128)S(1)}, f32[8,10752]{1,0:T(8,128)}, u32[]{:S(2)}) copy-start(f32[8,10752]{1,0:T(8,128)} %param.16) | copy-start | bytes 1032196
  0.6 4.1 %copy-start.4 = (f32[8,10752]{1,0:T(8,128)S(1)}, f32[8,10752]{1,0:T(8,128)}, u32[]{:S(2)}) copy-start(f32[8,10752]{1,0:T(8,128)} %param.17) | copy-start | bytes 1032196
  1.8 10.8 %copy-start.1 = (f32[8,10752]{1,0:T(8,128)}, f32[8,10752]{1,0:T(8,128)S(1)}, u32[]{:S(2)}) copy-start(f32[8,10752]{1,0:T(8,128)S(1)} %convert_element_type.77) | copy-start | bytes 1032196
  3.5 10.9 %collective-permute-start = (bf16[3,10752]{1,0:T(4,128)(2,1)S(1)}, bf16[3,10752]{1,0:T(4,128)(2,1)S(1)}, u32[]{:S(2)}, u32[]{:S(2)}) collective-permute-start(bf16[3,10752]{1,0:T(4,128)(2,1)S(1)} %pad_maximum_fusion.4), channel_id=1, source_target_pairs={{4,0},{8,4},{12,8},{16,12},{20,16},{24,20},{28,24},{5,1},{9,5},{13... | collective-permute-start | bytes 193544 | tf_op jit(solution)/shard_map/ppermute | solution.py:22
  7.0 9.4 %collective-permute-start.1 = (bf16[6,10752]{1,0:T(8,128)(2,1)}, bf16[6,10752]{1,0:T(8,128)(2,1)S(1)}, u32[]{:S(2)}, u32[]{:S(2)}) collective-permute-start(bf16[6,10752]{1,0:T(8,128)(2,1)} %concatenate.86), channel_id=1, source_target_pairs={{0,4},{4,8},{8,12},{12,16},{16,20},{20,24},{24,28},{1,5},{5,9},{9,... | collective-permute-start | bytes 387080 | tf_op jit(solution)/shard_map/ppermute | solution.py:22
  12.8 1.6 %copy-start = (s32[8,10752]{1,0:T(8,128)S(1)}, s32[8,10752]{1,0:T(8,128)}, u32[]{:S(2)}) copy-start(s32[8,10752]{1,0:T(8,128)} %param.18) | copy-start | bytes 1032196
  12.8 1.6 %slice-start = ((f32[8,10752]{1,0:T(8,128)}), f32[8,1]{1,0:T(8,128)S(1)}, s32[]{:S(2)}) async-start(f32[8,10752]{1,0:T(8,128)} %copy-done.1), calls=%async_computation | async-start | bytes 8192 | tf_op jit(solution)/shard_map/jit(_roll_static)/slice | solution.py:289
  12.9 1.6 %slice-start.1 = ((f32[8,10752]{1,0:T(8,128)}), f32[8,1]{1,0:T(8,128)S(1)}, s32[]{:S(2)}) async-start(f32[8,10752]{1,0:T(8,128)} %param.16), calls=%async_computation.1 | async-start | bytes 8192 | tf_op jit(solution)/shard_map/jit(_roll_static)/slice | solution.py:291
  12.9 1.6 %copy-start.20 = (f32[2,8,10752]{2,1,0:T(8,128)S(1)}, f32[2,8,10752]{2,1,0:T(8,128)}, u32[]{:S(2)}) copy-start(f32[2,8,10752]{2,1,0:T(8,128)} %param.15) | copy-start | bytes 2064388
  14.4 5.9 %copy-start.36 = (f32[2,8]{1,0:T(2,128)}, f32[2,8]{1,0:T(2,128)S(1)}, u32[]{:S(2)}) copy-start(f32[2,8]{1,0:T(2,128)S(1)} %get-tuple-element.78) | copy-start | bytes 196
  14.5 2.0 %copy-start.2 = (f32[8,10752]{1,0:T(8,128)S(1)}, f32[8,10752]{1,0:T(8,128)}, u32[]{:S(2)}) copy-start(f32[8,10752]{1,0:T(8,128)} %copy-done.1) | copy-start | bytes 1032196
  16.5 1.7 %copy-start.19 = (f32[6,10752]{1,0:T(8,128)}, f32[6,10752]{1,0:T(8,128)S(1)}, u32[]{:S(2)}) copy-start(f32[6,10752]{1,0:T(8,128)S(1)} %convert_element_type.80) | copy-start | bytes 774148
  43.2 1.8 %copy-start.33 = (bf16[2,2,13,128,1]{3,2,1,0,4:T(8,128)(2,1)S(1)}, bf16[2,2,13,128,1]{3,2,1,0,4:T(8,128)(2,1)}, u32[]{:S(2)}) copy-start(bf16[2,2,13,128,1]{3,2,1,0,4:T(8,128)(2,1)} %constant.69) | copy-start | bytes 39940
  48.5 8.0 %copy-start.18 = (f32[8,10752]{1,0:T(8,128)S(1)}, f32[8,10752]{1,0:T(8,128)}, u32[]{:S(2)}) copy-start(f32[8,10752]{1,0:T(8,128)} %get-tuple-element.33) | copy-start | bytes 1032196
  49.3 8.1 %collective-permute-start.2 = (bf16[2,10752]{1,0:T(2,128)(2,1)S(1)}, bf16[2,10752]{1,0:T(2,128)(2,1)S(1)}, u32[]{:S(2)}, u32[]{:S(2)}) collective-permute-start(bf16[2,10752]{1,0:T(2,128)(2,1)S(1)} %pad_maximum_fusion.5), channel_id=1, source_target_pairs={{4,0},{8,4},{12,8},{16,12},{20,16},{24,20},{28,24},{5,1},{9,5},{13... | collective-permute-start | bytes 129032 | tf_op jit(solution)/shard_map/ppermute | solution.py:22
  50.7 8.7 %collective-permute-start.3 = (bf16[2,10752]{1,0:T(2,128)(2,1)S(1)}, bf16[2,10752]{1,0:T(2,128)(2,1)S(1)}, u32[]{:S(2)}, u32[]{:S(2)}) collective-permute-start(bf16[2,10752]{1,0:T(2,128)(2,1)S(1)} %pad_maximum_fusion.6), channel_id=1, source_target_pairs={{0,4},{4,8},{8,12},{12,16},{16,20},{20,24},{24,28},{1,5},{5,9},{9,... | collective-permute-start | bytes 129032 | tf_op jit(solution)/shard_map/ppermute | solution.py:22
  56.5 1.4 %copy-start.21 = (f32[2,8,10752]{2,1,0:T(8,128)S(1)}, f32[2,8,10752]{2,1,0:T(8,128)}, u32[]{:S(2)}) copy-start(f32[2,8,10752]{2,1,0:T(8,128)} %param.13) | copy-start | bytes 2064388
  58.0 1.5 %copy-start.27 = (f32[1,10752]{1,0:T(1,128)S(1)}, f32[1,10752]{1,0:T(1,128)}, u32[]{:S(2)}) copy-start(f32[1,10752]{1,0:T(1,128)} %copy-done.26) | copy-start | bytes 129028
  58.0 1.5 %copy-start.28 = (f32[1,10752]{1,0:T(1,128)S(1)}, f32[1,10752]{1,0:T(1,128)}, u32[]{:S(2)}) copy-start(f32[1,10752]{1,0:T(1,128)} %get-tuple-element.27) | copy-start | bytes 129028
  58.0 1.5 %copy-start.30 = (f32[1,10752]{1,0:T(1,128)S(1)}, f32[1,10752]{1,0:T(1,128)}, u32[]{:S(2)}) copy-start(f32[1,10752]{1,0:T(1,128)} %get-tuple-element.28) | copy-start | bytes 129028
  87.2 2.2 %copy-start.7 = (f32[8,10752]{1,0:T(8,128)S(1)}, f32[8,10752]{1,0:T(8,128)}, u32[]{:S(2)}) copy-start(f32[8,10752]{1,0:T(8,128)} %copy-done.6) | copy-start | bytes 1032196
  89.4 7.3 %copy-start.12 = (f32[1,8,10752]{2,1,0:T(8,128)S(1)}, f32[1,8,10752]{2,1,0:T(8,128)}, u32[]{:S(2)}) copy-start(f32[1,8,10752]{2,1,0:T(8,128)} %get-tuple-element.49) | copy-start | bytes 1032196
  89.4 7.3 %copy-start.15 = (f32[1,8,10752]{2,1,0:T(8,128)S(1)}, f32[1,8,10752]{2,1,0:T(8,128)}, u32[]{:S(2)}) copy-start(f32[1,8,10752]{2,1,0:T(8,128)} %get-tuple-element.4) | copy-start | bytes 1032196
  90.3 11.1 %copy-start.9 = (f32[8,10752]{1,0:T(8,128)S(1)}, f32[8,10752]{1,0:T(8,128)}, u32[]{:S(2)}) copy-start(f32[8,10752]{1,0:T(8,128)} %get-tuple-element.47) | copy-start | bytes 1032196
  90.3 11.1 %copy-start.11 = (f32[8,10752]{1,0:T(8,128)S(1)}, f32[8,10752]{1,0:T(8,128)}, u32[]{:S(2)}) copy-start(f32[8,10752]{1,0:T(8,128)} %get-tuple-element.48) | copy-start | bytes 1032196
  90.3 11.1 %copy-start.16 = (f32[8,10752]{1,0:T(8,128)S(1)}, f32[8,10752]{1,0:T(8,128)}, u32[]{:S(2)}) copy-start(f32[8,10752]{1,0:T(8,128)} %get-tuple-element.23) | copy-start | bytes 1032196
  90.3 11.1 %copy-start.17 = (f32[8,10752]{1,0:T(8,128)S(1)}, f32[8,10752]{1,0:T(8,128)}, u32[]{:S(2)}) copy-start(f32[8,10752]{1,0:T(8,128)} %get-tuple-element.45) | copy-start | bytes 1032196
  90.3 12.4 %collective-permute-start.5 = (bf16[1,10752]{1,0:T(2,128)(2,1)S(1)}, bf16[1,10752]{1,0:T(2,128)(2,1)S(1)}, u32[]{:S(2)}, u32[]{:S(2)}) collective-permute-start(bf16[1,10752]{1,0:T(2,128)(2,1)S(1)} %get-tuple-element.59), channel_id=1, source_target_pairs={{0,4},{4,8},{8,12},{12,16},{16,20},{20,24},{24,28},{1,5},{5,9},{9,... | collective-permute-start | bytes 64520 | tf_op jit(solution)/shard_map/ppermute | solution.py:22
  95.4 5.9 %collective-permute-start.4 = (bf16[1,10752]{1,0:T(2,128)(2,1)S(1)}, bf16[1,10752]{1,0:T(2,128)(2,1)S(1)}, u32[]{:S(2)}, u32[]{:S(2)}) collective-permute-start(bf16[1,10752]{1,0:T(2,128)(2,1)S(1)} %get-tuple-element.60), channel_id=1, source_target_pairs={{4,0},{8,4},{12,8},{16,12},{20,16},{24,20},{28,24},{5,1},{9,5},{13... | collective-permute-start | bytes 64520 | tf_op jit(solution)/shard_map/ppermute | solution.py:22
  101.4 1.3 %copy-start.29 = (f32[1,10752]{1,0:T(1,128)S(1)}, f32[1,10752]{1,0:T(1,128)}, u32[]{:S(2)}) copy-start(f32[1,10752]{1,0:T(1,128)} %get-tuple-element.27) | copy-start | bytes 129028
  101.4 1.3 %copy-start.31 = (f32[1,10752]{1,0:T(1,128)S(1)}, f32[1,10752]{1,0:T(1,128)}, u32[]{:S(2)}) copy-start(f32[1,10752]{1,0:T(1,128)} %get-tuple-element.28) | copy-start | bytes 129028
  101.4 1.3 %copy-start.32 = (f32[1,10752]{1,0:T(1,128)S(1)}, f32[1,10752]{1,0:T(1,128)}, u32[]{:S(2)}) copy-start(f32[1,10752]{1,0:T(1,128)} %get-tuple-element.19) | copy-start | bytes 129028
  (16 other events, 16.1 us)

commit v6 on v4

--- a/solution.py
+++ b/solution.py
@@ -85,7 +85,7 @@
         )
         return carry
 
-    lax.fori_loop(1, count, one, 0)
+    lax.fori_loop(1, count, one, 0, unroll=count <= 32)
     pl.semaphore_wait(barrier, count - 1)
 
 
@@ -98,7 +98,7 @@
         copy_of(step).wait()
         return carry
 
-    lax.fori_loop(1, count, begin, 0)
+    lax.fori_loop(1, count, begin, 0, unroll=count <= 32)
     return lambda: lax.fori_loop(1, count, finish, 0)
 
 

time: 105 us -> 105 us (level)
  no operation moved by 1% of the time
where the time goes in v6:
time: 105 us; the launch traced here: 104 us
  Pallas kernels  38.3 us (36%)
  starting transfers between devices  20 us (19%)
  other arithmetic  18.7 us (18%)
  local copies, waits for them, and re-layouts  17.8 us (17%)
  waiting for transfers between devices  4.08 us (4%)
  matrix products  3.62 us (3%)
  between operations  1.65 us (2%)
    pallas_call x2, Pallas kernels, load_spectra(): pl.pallas_call(functools.partial(load_kernel, (lat_count, deg_count, row_...  38.3 us
    ppermute x6, starting transfers between devices, passed_along(): return lax.ppermute(value, axis, pairs)  20 us
    unnamed x78, local copies, waits for them, and re-layouts  7.32 us
    ppermute x6, waiting for transfers between devices, passed_along(): return lax.ppermute(value, axis, pairs)  4.08 us
    reshape x2, local copies, waits for them, and re-layouts, synthesise(): return grid_out.reshape(2, row_count, -1) * output_weight[:, :, None]  3.08 us
    another operation x3, other arithmetic, on_device(): state_vel, back_vel = (jnp.stack(state_vel), jnp.stack(back_vel))  2.66 us
    mul x2, other arithmetic, synthesise(): return grid_out.reshape(2, row_count, -1) * output_weight[:, :, None]  2.52 us
    mul x2, other arithmetic, on_device(): flux_down = southward(flux_y, south_height * south_v)  2.48 us
  transfers between devices with their start and end apart: 6, of which 2 were waited for; matrix products, arithmetic and copies ran while one was open for 8% of the time, Pallas kernels for 0%

profile of v6, /device:TPU:0, one launch (start us, length us, event | category | flops | bytes accessed | tf_op | source)
XLA Modules:
  0.0 104.2 jit_solution(11657347917435180451)
XLA Ops:
  0.7 1.1 %convert_element_type.77 = f32[8,10752]{1,0:T(8,128)S(1)} convert(s32[8,10752]{1,0:T(8,128)} %param.18) | non-fusion elementwise | flops 86016 | bytes 688128 | tf_op jit(solution)/shard_map/convert_element_type | solution.py:276
  1.8 1.3 %multiply_multiply_fusion.3 = (f32[8,10752]{1,0:T(8,128)S(1)}, f32[8,10752]{1,0:T(8,128)S(1)}) fusion(f32[8,10752]{1,0:T(8,128)} %param.14, f32[8]{0:T(128)S(1)} %add_divide_fusion, s32[8,10752]{1,0:T(8,128)} %param.18), kind=kLoop, calls=%fused_computation.111 | loop fusion | flops 430080 | bytes 1376288 | tf_op jit(solution)/shard_map/mul | solution.py:306
  3.5 1.3 %collective-permute-start = (bf16[3,10752]{1,0:T(4,128)(2,1)S(1)}, bf16[3,10752]{1,0:T(4,128)(2,1)S(1)}, u32[]{:S(2)}, u32[]{:S(2)}) collective-permute-start(bf16[3,10752]{1,0:T(4,128)(2,1)S(1)} %pad_maximum_fusion.4), channel_id=1, source_target_pairs={{4,0},{8,4},{12,8},{16,12},{20,16},{24,20},{28,24},{5,1},{9,5},{13... | collective-permute-start | bytes 193544 | tf_op jit(solution)/shard_map/ppermute | solution.py:22
  4.8 1.2 %fusion.67 = (bf16[1,10752]{1,0:T(2,128)(2,1)S(1)}, bf16[1,10752]{1,0:T(2,128)(2,1)S(1)}) fusion(f32[2,8,10752]{2,1,0:T(8,128)} %param.15, f32[2,8,10752]{2,1,0:T(8,128)} %param.13), kind=kLoop, calls=%fused_computation.145 | loop fusion | bytes 86016 | tf_op jit(solution)/shard_map/squeeze | solution.py:282
  6.4 5.5 %collective-permute-start.1 = (bf16[6,10752]{1,0:T(8,128)(2,1)S(1)}, bf16[6,10752]{1,0:T(8,128)(2,1)S(1)}, u32[]{:S(2)}, u32[]{:S(2)}) collective-permute-start(bf16[6,10752]{1,0:T(8,128)(2,1)S(1)} %concatenate.86), channel_id=1, source_target_pairs={{0,4},{4,8},{8,12},{12,16},{16,20},{20,24},{24,28},{1,5},{5,9},{9,... | collective-permute-start | bytes 387080 | tf_op jit(solution)/shard_map/ppermute | solution.py:22
  12.6 0.5 copy-done.8
  13.5 1.3 %broadcast_multiply_fusion.3 = (f32[8,10752]{1,0:T(8,128)S(1)}, f32[8,10752]{1,0:T(8,128)}, f32[8,10752]{1,0:T(8,128)S(1)}, f32[8,10752]{1,0:T(8,128)S(1)}, f32[...) fusion(f32[8]{0:T(128)S(1)} %add_divide_fusion, f32[8,10752]{1,0:T(8,128)S(1)} %get-tuple-element.56, ...), kind=kLoop, calls=%fused_computation.119 | loop fusion | flops 1892352 | bytes 6537248 | tf_op jit(solution)/shard_map/mul | solution.py:316
  14.9 0.6 collective-permute-done.1
  15.8 0.9 convert_bitcast_fusion.2
  19.6 2.2 %copy-done = bf16[128,64,256]{2,1,0:T(8,128)(2,1)S(1)} copy-done((bf16[128,64,256]{2,1,0:T(8,128)(2,1)S(1)}, bf16[128,64,256]{2,1,0:T(8,128)(2,1)}, u32[]{:S(2)}) %copy-start) | copy-done | bytes 4194328
  21.8 20.4 %shard_map.147 = bf16[8,16,256]{2,1,0:T(8,128)(2,1)S(1)} custom-call(bf16[8,16,256]{2,1,0:T(8,128)(2,1)S(1)} %reshape.107.send_ref, bf16[128,64,256]{2,1,0:T(8,128)(2,1)S(1)} %copy-done, f32[1,256]{1,0:T(1,128)S(1)} %bitcast.138), custom_call_target="tpu_custom_call" | custom-call | tf_op jit(solution)/shard_map/pallas_call | solution.py:227
  43.7 1.2 %convolution_bitcast_fusion.5 = f32[16,84,128]{2,1,0:T(8,128)} fusion(bf16[2,84,84,1]{2,1,0,3:T(8,128)(2,1)S(1)} %copy-done.28, bf16[1,16,84,128]{3,2,0,1:T(8,128)(2,1)S(1)} %get-tuple-element.41, bf16[1,16,84,128]{3,2,0,1:T(8,128)(2,1)S(1)} %get-tuple-element.40), kind=kOutput, calls=%fused_computation.5 | convolution fusion | flops 58146816 | bytes 1404480 | tf_op jit(solution)/shard_map/cka,crkb->rab/dot_general | solution.py:75
  44.9 2.1 %reshape.111 = f32[2,8,10752]{2,1,0:T(8,128)} reshape(f32[16,84,128]{2,1,0:T(8,128)} %convolution_bitcast_fusion.5) | data formatting | bytes 1376256 | tf_op jit(solution)/shard_map/reshape | solution.py:76
  47.0 1.3 %broadcast_multiply_fusion.1 = f32[2,8,10752]{2,1,0:T(8,128)S(1)} fusion(f32[2,8,10752]{2,1,0:T(8,128)} %reshape.111, f32[2,8]{1,0:T(2,128)S(1)} %get-tuple-element.77), kind=kLoop, calls=%fused_computation.107 | loop fusion | flops 172032 | bytes 1376320 | tf_op jit(solution)/shard_map/mul | solution.py:76
  49.5 1.3 %collective-permute-start.2 = (bf16[2,10752]{1,0:T(2,128)(2,1)S(1)}, bf16[2,10752]{1,0:T(2,128)(2,1)S(1)}, u32[]{:S(2)}, u32[]{:S(2)}) collective-permute-start(bf16[2,10752]{1,0:T(2,128)(2,1)S(1)} %pad_maximum_fusion.5), channel_id=1, source_target_pairs={{4,0},{8,4},{12,8},{16,12},{20,16},{24,20},{28,24},{5,1},{9,5},{13... | collective-permute-start | bytes 129032 | tf_op jit(solution)/shard_map/ppermute | solution.py:22
  50.9 5.7 %collective-permute-start.3 = (bf16[2,10752]{1,0:T(2,128)(2,1)S(1)}, bf16[2,10752]{1,0:T(2,128)(2,1)S(1)}, u32[]{:S(2)}, u32[]{:S(2)}) collective-permute-start(bf16[2,10752]{1,0:T(2,128)(2,1)S(1)} %pad_maximum_fusion.6), channel_id=1, source_target_pairs={{0,4},{4,8},{8,12},{12,16},{16,20},{20,24},{24,28},{1,5},{5,9},{9,... | collective-permute-start | bytes 129032 | tf_op jit(solution)/shard_map/ppermute | solution.py:22
  56.6 0.8 multiply_bitcast_fusion.1
  58.1 1.3 %fusion.89 = (f32[8,10752]{1,0:T(8,128)S(1)}, f32[8,10752]{1,0:T(8,128)}, f32[8,10752]{1,0:T(8,128)S(1)}, f32[8,10752]{1,0:T(8,128)}, f32[1,8,10752]{2,1,0:T(8,1...) fusion(f32[8,10752]{1,0:T(8,128)S(1)} %get-tuple-element.35, f32[8,10752]{1,0:T(8,128)S(1)} %get-tuple-element.34, ...), kind=kLoop, calls=%fused_computation.179 | loop fusion | flops 1978368 | bytes 7225376 | tf_op jit(solution)/shard_map/mul | solution.py:338
  59.5 1.3 %fusion.85 = (f32[1,10752]{1,0:T(1,128)S(1)}, f32[1,10752]{1,0:T(1,128)S(1)}, f32[1,10752]{1,0:T(1,128)S(1)}) fusion(f32[1,10752]{1,0:T(1,128)S(1)} %get-tuple-element.27, f32[1,10752]{1,0:T(1,128)S(1)} %get-tuple-element.28, f32[2,10752]{1,0:T(2,128)S(1)} %convert_element_type.86, f32[8,10752]{1,0:T(8,128)S(1)} %get-tuple-element.55, ...), kind=kLoop, calls=%fused_computation.177 | loop fusion | flops 129024 | bytes 516096 | tf_op jit(solution)/shard_map/mul | solution.py:341
  61.1 0.9 convert_bitcast_fusion
  64.6 2.2 %copy-done.1 = bf16[128,64,256]{2,1,0:T(8,128)(2,1)S(1)} copy-done((bf16[128,64,256]{2,1,0:T(8,128)(2,1)S(1)}, bf16[128,64,256]{2,1,0:T(8,128)(2,1)}, u32[]{:S(2)}) %copy-start.1) | copy-done | bytes 4194328
  66.8 17.9 %shard_map.148 = bf16[8,16,256]{2,1,0:T(8,128)(2,1)S(1)} custom-call(bf16[8,16,256]{2,1,0:T(8,128)(2,1)S(1)} %reshape.114.send_ref, bf16[128,64,256]{2,1,0:T(8,128)(2,1)S(1)} %copy-done.1, f32[1,256]{1,0:T(1,128)S(1)} %bitcast.139), custom_call_target="tpu_custom_call" | custom-call | tf_op jit(solution)/shard_map/pallas_call | solution.py:227
  86.6 1.0 reshape.118
  87.6 1.3 %broadcast_multiply_fusion = f32[2,8,10752]{2,1,0:T(8,128)S(1)} fusion(f32[2,8,10752]{2,1,0:T(8,128)} %reshape.118, f32[2,8]{1,0:T(2,128)S(1)} %copy-done.34), kind=kLoop, calls=%fused_computation.106 | loop fusion | flops 172032 | bytes 1376320 | tf_op jit(solution)/shard_map/mul | solution.py:76
  88.9 0.9 fusion.12
  89.8 5.0 %collective-permute-start.5 = (bf16[1,10752]{1,0:T(2,128)(2,1)S(1)}, bf16[1,10752]{1,0:T(2,128)(2,1)S(1)}, u32[]{:S(2)}, u32[]{:S(2)}) collective-permute-start(bf16[1,10752]{1,0:T(2,128)(2,1)S(1)} %get-tuple-element.59), channel_id=1, source_target_pairs={{0,4},{4,8},{8,12},{12,16},{16,20},{20,24},{24,28},{1,5},{5,9},{9,... | collective-permute-start | bytes 64520 | tf_op jit(solution)/shard_map/ppermute | solution.py:22
  94.8 1.3 %collective-permute-start.4 = (bf16[1,10752]{1,0:T(2,128)(2,1)S(1)}, bf16[1,10752]{1,0:T(2,128)(2,1)S(1)}, u32[]{:S(2)}, u32[]{:S(2)}) collective-permute-start(bf16[1,10752]{1,0:T(2,128)(2,1)S(1)} %get-tuple-element.60), channel_id=1, source_target_pairs={{4,0},{8,4},{12,8},{16,12},{20,16},{24,20},{28,24},{5,1},{9,5},{13... | collective-permute-start | bytes 64520 | tf_op jit(solution)/shard_map/ppermute | solution.py:22
  96.2 0.9 pad_maximum_fusion.1
  97.3 3.5 %collective-permute-done.4 = bf16[1,10752]{1,0:T(2,128)(2,1)S(1)} collective-permute-done((bf16[1,10752]{1,0:T(2,128)(2,1)S(1)}, bf16[1,10752]{1,0:T(2,128)(2,1)S(1)}, u32[]{:S(2)}, u32[]{:S(2)}) %collective-permute-start.4) | collective-permute-done | bytes 21536 | tf_op jit(solution)/shard_map/ppermute | solution.py:22
  101.2 0.9 pad_maximum_fusion
  102.1 1.1 %multiply_multiply_fusion.4 = f32[1,10752]{1,0:T(1,128)S(1)} fusion(f32[1,10752]{1,0:T(1,128)S(1)} %get-tuple-element.27, f32[1,10752]{1,0:T(1,128)S(1)} %get-tuple-element.28, bf16[1,10752]{1,0:T(2,128)(2,1)S(1)} %collective-permute-done.5, f32[1,10752]{1,0:T(1,128)S(1)} %get-tuple-element.19, f32[8,10752]{1,0:T(8,128)S(1)} %get-tuple-element.52, ...), kind=kLoop, calls=%fused_computation.154 | loop fusion | flops 86016 | bytes 279552 | tf_op jit(solution)/shard_map/mul | solution.py:341
  103.3 0.9 fusion.51
  (165 shorter events, 13.7 us)
Async XLA Ops:
  0.6 2.5 %copy-start.6 = (f32[8,10752]{1,0:T(8,128)S(1)}, f32[8,10752]{1,0:T(8,128)}, u32[]{:S(2)}) copy-start(f32[8,10752]{1,0:T(8,128)} %param.16) | copy-start | bytes 1032196
  0.6 4.1 %copy-start.7 = (f32[8,10752]{1,0:T(8,128)S(1)}, f32[8,10752]{1,0:T(8,128)}, u32[]{:S(2)}) copy-start(f32[8,10752]{1,0:T(8,128)} %param.17) | copy-start | bytes 1032196
  1.8 10.2 %copy-start.4 = (f32[8,10752]{1,0:T(8,128)}, f32[8,10752]{1,0:T(8,128)S(1)}, u32[]{:S(2)}) copy-start(f32[8,10752]{1,0:T(8,128)S(1)} %convert_element_type.77) | copy-start | bytes 1032196
  3.5 9.8 %collective-permute-start = (bf16[3,10752]{1,0:T(4,128)(2,1)S(1)}, bf16[3,10752]{1,0:T(4,128)(2,1)S(1)}, u32[]{:S(2)}, u32[]{:S(2)}) collective-permute-start(bf16[3,10752]{1,0:T(4,128)(2,1)S(1)} %pad_maximum_fusion.4), channel_id=1, source_target_pairs={{4,0},{8,4},{12,8},{16,12},{20,16},{24,20},{28,24},{5,1},{9,5},{13... | collective-permute-start | bytes 193544 | tf_op jit(solution)/shard_map/ppermute | solution.py:22
  6.4 9.1 %collective-permute-start.1 = (bf16[6,10752]{1,0:T(8,128)(2,1)S(1)}, bf16[6,10752]{1,0:T(8,128)(2,1)S(1)}, u32[]{:S(2)}, u32[]{:S(2)}) collective-permute-start(bf16[6,10752]{1,0:T(8,128)(2,1)S(1)} %concatenate.86), channel_id=1, source_target_pairs={{0,4},{4,8},{8,12},{12,16},{16,20},{20,24},{24,28},{1,5},{5,9},{9,... | collective-permute-start | bytes 387080 | tf_op jit(solution)/shard_map/ppermute | solution.py:22
  12.3 1.3 %copy-start.26 = (f32[2,8,10752]{2,1,0:T(8,128)S(1)}, f32[2,8,10752]{2,1,0:T(8,128)}, u32[]{:S(2)}) copy-start(f32[2,8,10752]{2,1,0:T(8,128)} %param.15) | copy-start | bytes 2064388
  13.2 5.5 %copy-start.35 = (f32[2,8]{1,0:T(2,128)}, f32[2,8]{1,0:T(2,128)S(1)}, u32[]{:S(2)}) copy-start(f32[2,8]{1,0:T(2,128)S(1)} %get-tuple-element.78) | copy-start | bytes 196
  13.2 33.8 %copy-start.33 = (f32[2,8]{1,0:T(2,128)}, f32[2,8]{1,0:T(2,128)S(1)}, u32[]{:S(2)}) copy-start(f32[2,8]{1,0:T(2,128)S(1)} %get-tuple-element.77) | copy-start | bytes 196
  13.5 2.0 %copy-start.5 = (f32[8,10752]{1,0:T(8,128)S(1)}, f32[8,10752]{1,0:T(8,128)}, u32[]{:S(2)}) copy-start(f32[8,10752]{1,0:T(8,128)} %copy-done.4) | copy-start | bytes 1032196
  18.2 1.4 %copy-start.2 = (f32[256]{0:T(256)S(1)}, f32[256]{0:T(256)}, u32[]{:S(2)}) copy-start(f32[256]{0:T(256)} %param.20) | copy-start | bytes 3076
  19.6 2.2 %copy-start = (bf16[128,64,256]{2,1,0:T(8,128)(2,1)S(1)}, bf16[128,64,256]{2,1,0:T(8,128)(2,1)}, u32[]{:S(2)}) copy-start(bf16[128,64,256]{2,1,0:T(8,128)(2,1)} %basis_ref.3) | copy-start | bytes 12582916
  44.9 3.4 %copy-start.9 = (f32[8,10752]{1,0:T(8,128)S(1)}, f32[8,10752]{1,0:T(8,128)}, u32[]{:S(2)}) copy-start(f32[8,10752]{1,0:T(8,128)} %param.12) | copy-start | bytes 1032196
  44.9 3.4 %copy-start.18 = (f32[8,10752]{1,0:T(8,128)S(1)}, f32[8,10752]{1,0:T(8,128)}, u32[]{:S(2)}) copy-start(f32[8,10752]{1,0:T(8,128)} %param.14) | copy-start | bytes 1032196
  47.0 1.3 %copy-start.20 = (f32[8,10752]{1,0:T(8,128)S(1)}, f32[8,10752]{1,0:T(8,128)}, u32[]{:S(2)}) copy-start(f32[8,10752]{1,0:T(8,128)} %get-tuple-element.25) | copy-start | bytes 1032196
  48.7 7.9 %copy-start.24 = (f32[8,10752]{1,0:T(8,128)S(1)}, f32[8,10752]{1,0:T(8,128)}, u32[]{:S(2)}) copy-start(f32[8,10752]{1,0:T(8,128)} %get-tuple-element.33) | copy-start | bytes 1032196
  49.5 8.0 %collective-permute-start.2 = (bf16[2,10752]{1,0:T(2,128)(2,1)S(1)}, bf16[2,10752]{1,0:T(2,128)(2,1)S(1)}, u32[]{:S(2)}, u32[]{:S(2)}) collective-permute-start(bf16[2,10752]{1,0:T(2,128)(2,1)S(1)} %pad_maximum_fusion.5), channel_id=1, source_target_pairs={{4,0},{8,4},{12,8},{16,12},{20,16},{24,20},{28,24},{5,1},{9,5},{13... | collective-permute-start | bytes 129032 | tf_op jit(solution)/shard_map/ppermute | solution.py:22
  50.9 8.6 %collective-permute-start.3 = (bf16[2,10752]{1,0:T(2,128)(2,1)S(1)}, bf16[2,10752]{1,0:T(2,128)(2,1)S(1)}, u32[]{:S(2)}, u32[]{:S(2)}) collective-permute-start(bf16[2,10752]{1,0:T(2,128)(2,1)S(1)} %pad_maximum_fusion.6), channel_id=1, source_target_pairs={{0,4},{4,8},{8,12},{12,16},{16,20},{20,24},{24,28},{1,5},{5,9},{9,... | collective-permute-start | bytes 129032 | tf_op jit(solution)/shard_map/ppermute | solution.py:22
  56.6 1.4 %copy-start.27 = (f32[2,8,10752]{2,1,0:T(8,128)S(1)}, f32[2,8,10752]{2,1,0:T(8,128)}, u32[]{:S(2)}) copy-start(f32[2,8,10752]{2,1,0:T(8,128)} %param.13) | copy-start | bytes 2064388
  58.0 2.8 %copy-start.10 = (f32[8,10752]{1,0:T(8,128)S(1)}, f32[8,10752]{1,0:T(8,128)}, u32[]{:S(2)}) copy-start(f32[8,10752]{1,0:T(8,128)} %param.12) | copy-start | bytes 1032196
  62.5 1.2 %copy-start.36 = (f32[2,8]{1,0:T(2,128)S(1)}, f32[2,8]{1,0:T(2,128)}, u32[]{:S(2)}) copy-start(f32[2,8]{1,0:T(2,128)} %copy-done.35) | copy-start | bytes 196
  64.6 2.2 %copy-start.1 = (bf16[128,64,256]{2,1,0:T(8,128)(2,1)S(1)}, bf16[128,64,256]{2,1,0:T(8,128)(2,1)}, u32[]{:S(2)}) copy-start(bf16[128,64,256]{2,1,0:T(8,128)(2,1)} %basis_ref.3) | copy-start | bytes 12582916
  86.3 1.3 %copy-start.34 = (f32[2,8]{1,0:T(2,128)S(1)}, f32[2,8]{1,0:T(2,128)}, u32[]{:S(2)}) copy-start(f32[2,8]{1,0:T(2,128)} %copy-done.33) | copy-start | bytes 196
  86.6 2.3 %copy-start.12 = (f32[8,10752]{1,0:T(8,128)S(1)}, f32[8,10752]{1,0:T(8,128)}, u32[]{:S(2)}) copy-start(f32[8,10752]{1,0:T(8,128)} %copy-done.11) | copy-start | bytes 1032196
  87.6 1.3 %copy-start.19 = (f32[8,10752]{1,0:T(8,128)S(1)}, f32[8,10752]{1,0:T(8,128)}, u32[]{:S(2)}) copy-start(f32[8,10752]{1,0:T(8,128)} %get-tuple-element.15) | copy-start | bytes 1032196
  88.8 7.3 %copy-start.17 = (f32[1,8,10752]{2,1,0:T(8,128)S(1)}, f32[1,8,10752]{2,1,0:T(8,128)}, u32[]{:S(2)}) copy-start(f32[1,8,10752]{2,1,0:T(8,128)} %get-tuple-element.49) | copy-start | bytes 1032196
  88.9 7.3 %copy-start.21 = (f32[1,8,10752]{2,1,0:T(8,128)S(1)}, f32[1,8,10752]{2,1,0:T(8,128)}, u32[]{:S(2)}) copy-start(f32[1,8,10752]{2,1,0:T(8,128)} %get-tuple-element.4) | copy-start | bytes 1032196
  89.8 11.0 %copy-start.14 = (f32[8,10752]{1,0:T(8,128)S(1)}, f32[8,10752]{1,0:T(8,128)}, u32[]{:S(2)}) copy-start(f32[8,10752]{1,0:T(8,128)} %get-tuple-element.47) | copy-start | bytes 1032196
  89.8 11.0 %copy-start.16 = (f32[8,10752]{1,0:T(8,128)S(1)}, f32[8,10752]{1,0:T(8,128)}, u32[]{:S(2)}) copy-start(f32[8,10752]{1,0:T(8,128)} %get-tuple-element.48) | copy-start | bytes 1032196
  89.8 11.0 %copy-start.22 = (f32[8,10752]{1,0:T(8,128)S(1)}, f32[8,10752]{1,0:T(8,128)}, u32[]{:S(2)}) copy-start(f32[8,10752]{1,0:T(8,128)} %get-tuple-element.23) | copy-start | bytes 1032196
  89.8 11.0 %copy-start.23 = (f32[8,10752]{1,0:T(8,128)S(1)}, f32[8,10752]{1,0:T(8,128)}, u32[]{:S(2)}) copy-start(f32[8,10752]{1,0:T(8,128)} %get-tuple-element.45) | copy-start | bytes 1032196
  89.8 12.3 %collective-permute-start.5 = (bf16[1,10752]{1,0:T(2,128)(2,1)S(1)}, bf16[1,10752]{1,0:T(2,128)(2,1)S(1)}, u32[]{:S(2)}, u32[]{:S(2)}) collective-permute-start(bf16[1,10752]{1,0:T(2,128)(2,1)S(1)} %get-tuple-element.59), channel_id=1, source_target_pairs={{0,4},{4,8},{8,12},{12,16},{16,20},{20,24},{24,28},{1,5},{5,9},{9,... | collective-permute-start | bytes 64520 | tf_op jit(solution)/shard_map/ppermute | solution.py:22
  94.8 5.9 %collective-permute-start.4 = (bf16[1,10752]{1,0:T(2,128)(2,1)S(1)}, bf16[1,10752]{1,0:T(2,128)(2,1)S(1)}, u32[]{:S(2)}, u32[]{:S(2)}) collective-permute-start(bf16[1,10752]{1,0:T(2,128)(2,1)S(1)} %get-tuple-element.60), channel_id=1, source_target_pairs={{4,0},{8,4},{12,8},{16,12},{20,16},{24,20},{28,24},{5,1},{9,5},{13... | collective-permute-start | bytes 64520 | tf_op jit(solution)/shard_map/ppermute | solution.py:22
  (15 other events, 14.4 us)
